TPU v7x, 32 devices: a whole 2x2x4 slice. The times are simulated.
32 devices in a mesh: dp: 8 (over z, x), chan: 4 (over y, core).
Axes of the slice: x: 2, y: 2, z: 4, core: 2. Of those that a mesh axis runs over, the one named last changes fastest.
Arguments:
- x_maps: bfloat16 [64, 16, 16, 256], P('dp', None, None, 'chan'), may hold values from -6 to 6
- timesteps: int32 [64], P('dp'), may hold values from 0 to 999
- counts: int32 [8], P('dp'), may hold values from 2 to 8, as said below
- emb_table: bfloat16 [1000, 512], replicated, may hold values from -5 to 5
- w_first: bfloat16 [3, 3, 256, 256], P(None, None, None, 'chan'), may hold values from -0.125 to 0.125
- w_second: bfloat16 [3, 3, 256, 256], P(None, None, None, 'chan'), may hold values from -0.125 to 0.125
- w_embed: bfloat16 [512, 256], P(None, 'chan'), may hold values from -0.25 to 0.25
- w_qkv: bfloat16 [256, 3, 256], P(None, None, 'chan'), may hold values from -0.375 to 0.375
- w_out: bfloat16 [256, 256], P(None, 'chan'), may hold values from -1.5 to 1.5
- gain_one: bfloat16 [256], P('chan'), may hold values from 0.099609375 to 1.8984375
- shift_one: bfloat16 [256], P('chan'), may hold values from -3 to 3
- gain_two: bfloat16 [256], P('chan'), may hold values from 0.099609375 to 1.8984375
- shift_two: bfloat16 [256], P('chan'), may hold values from -3 to 3
- gain_three: bfloat16 [256], P('chan'), may hold values from 0.099609375 to 1.8984375
- shift_three: bfloat16 [256], P('chan'), may hold values from -3 to 3
- cotangent: bfloat16 [64, 16, 16, 256], P('dp', None, None, 'chan'), may hold values from -6 to 6
Outputs:
- y_maps: bfloat16 [64, 16, 16, 256], P('dp', None, None, 'chan')
- d_maps: bfloat16 [64, 16, 16, 256], P('dp', None, None, 'chan')
- d_table: float32 [1000, 512], replicated
- d_first: float32 [3, 3, 256, 256], P(None, None, None, 'chan')
- d_second: float32 [3, 3, 256, 256], P(None, None, None, 'chan')
- d_embed: float32 [512, 256], P(None, 'chan')
- d_qkv: float32 [256, 3, 256], P(None, None, 'chan')
- d_out: float32 [256, 256], P(None, 'chan')
- d_gain_one: float32 [256], P('chan')
- d_shift_one: float32 [256], P('chan')
- d_gain_two: float32 [256], P('chan')
- d_shift_two: float32 [256], P('chan')
- d_gain_three: float32 [256], P('chan')
- d_shift_three: float32 [256], P('chan')
Inputs may be any that keep to these rules, and one draw needn't show every extreme that they name: `counts`: slots of an index of dp at or beyond its count are unused; one index of dp has a full count of 8, another the least count.
All inputs are finite; a program needn't handle non-finite values.
Results may differ from a plain program's by a relative error of at most 0.04.
Values may be sent and summed in bfloat16 or wider, within the bound.
A program may use at most 128 MiB of HBM per device.

v0:
```python
import jax
import jax.numpy as jnp
from jax import lax
from jax.sharding import PartitionSpec as P

GROUPS = 32
MB = 2


HIGH = lax.Precision.HIGHEST
EPS = 1e-06


def silu_grad(values):
    sig = jax.nn.sigmoid(values)
    return sig * (1.0 + values * (1.0 - sig))


def group_stats(values, gain, shift, size):
    count = values.shape[0]
    width = values.shape[-1]
    grouped = values.reshape(count, -1, width // size, size)
    center = jnp.mean(grouped, axis=(1, 3), keepdims=True)
    spread = jnp.mean(jnp.square(grouped - center), axis=(1, 3), keepdims=True)
    rstd = lax.rsqrt(spread + EPS)
    normed = ((grouped - center) * rstd).reshape(values.shape)
    return (normed * gain.astype(jnp.float32) + shift.astype(jnp.float32), normed, rstd)


def group_back(dout, normed, rstd, gain, size):
    count = dout.shape[0]
    width = dout.shape[-1]
    scaled = (dout * gain.astype(jnp.float32)).reshape(count, -1, width // size, size)
    flat_norm = normed.reshape(scaled.shape)
    dvals = rstd * (
        scaled
        - jnp.mean(scaled, axis=(1, 3), keepdims=True)
        - flat_norm * jnp.mean(scaled * flat_norm, axis=(1, 3), keepdims=True)
    )
    return (
        dvals.reshape(dout.shape),
        jnp.sum(dout * normed, axis=(0, 1, 2)),
        jnp.sum(dout, axis=(0, 1, 2)),
    )


def conv_forward(inputs, weight):
    side = inputs.shape[1]
    padded = jnp.pad(inputs, ((0, 0), (1, 1), (1, 1), (0, 0)))
    total = jnp.zeros(inputs.shape[:3] + (weight.shape[3],), jnp.float32)
    for row in range(3):
        for col in range(3):
            total = total + jnp.einsum(
                "nhwc,cd->nhwd",
                padded[:, row : row + side, col : col + side, :],
                weight[row, col],
                preferred_element_type=jnp.float32,
            )
    return total


def conv_backward(inputs, weight, grad_out):
    side = inputs.shape[1]
    padded = jnp.pad(inputs, ((0, 0), (1, 1), (1, 1), (0, 0)))
    dpad = jnp.zeros(padded.shape, jnp.float32)
    taps = []
    for row in range(3):
        for col in range(3):
            taps.append(
                jnp.einsum(
                    "nhwc,nhwd->cd",
                    padded[:, row : row + side, col : col + side, :],
                    grad_out,
                    preferred_element_type=jnp.float32,
                )
            )
            dpad = dpad.at[:, row : row + side, col : col + side, :].add(
                jnp.einsum(
                    "nhwd,cd->nhwc", grad_out, weight[row, col], preferred_element_type=jnp.float32
                )
            )
    dweight = jnp.stack(taps).reshape(weight.shape)
    return (dweight, dpad[:, 1:-1, 1:-1, :])


def run_block(x_block, dy_block, t_block, live, weights, table, funcs):
    widen, narrow, score_total, prob_total = funcs
    (
        w_first,
        w_second,
        w_embed,
        w_qkv,
        w_out,
        gain_one,
        shift_one,
        gain_two,
        shift_two,
        gain_three,
        shift_three,
    ) = weights
    count = x_block.shape[0]
    side = x_block.shape[1]
    chans_out = x_block.shape[3]
    width = w_first.shape[2]
    size = width // GROUPS
    scale = width ** (-0.5)
    x_float = x_block.astype(jnp.float32)
    onehot = (t_block[:, None] == jnp.arange(table.shape[0], dtype=jnp.int32)[None, :]).astype(
        jnp.bfloat16
    )
    temb = jnp.dot(onehot, table, preferred_element_type=jnp.float32)
    tsil = jax.nn.silu(temb).astype(jnp.bfloat16)
    norm_one, normed_one, rstd_one = group_stats(x_float, gain_one, shift_one, size)
    act_one = widen(jax.nn.silu(norm_one).astype(jnp.bfloat16))
    hidden_one = conv_forward(act_one, w_first)
    embed = jnp.dot(tsil, w_embed, preferred_element_type=jnp.float32)
    hsum = hidden_one + embed[:, None, None, :]
    norm_two, normed_two, rstd_two = group_stats(hsum, gain_two, shift_two, size)
    act_two = widen(jax.nn.silu(norm_two).astype(jnp.bfloat16))
    hidden_two = conv_forward(act_two, w_second)
    resid = x_float + hidden_two
    norm_three, normed_three, rstd_three = group_stats(resid, gain_three, shift_three, size)
    act_three = widen(norm_three.astype(jnp.bfloat16)).reshape(count, side * side, width)
    proj = jnp.einsum("npc,cjd->jnpd", act_three, w_qkv, preferred_element_type=jnp.float32).astype(
        jnp.bfloat16
    )
    queries, keyvecs, values = (proj[0], proj[1], proj[2])
    scores = (
        score_total(
            jnp.einsum("nqd,nkd->nqk", queries, keyvecs, preferred_element_type=jnp.float32)
        )
        * scale
    )
    probs = jax.nn.softmax(scores, axis=-1)
    probs_low = probs.astype(jnp.bfloat16)
    mixed = jnp.einsum(
        "nqk,nkd->nqd", probs_low, values, preferred_element_type=jnp.float32
    ).astype(jnp.bfloat16)
    mixed_all = widen(mixed.reshape(count, side, side, chans_out)).reshape(
        count, side * side, width
    )
    outcome = jnp.einsum(
        "npc,cd->npd", mixed_all, w_out, preferred_element_type=jnp.float32
    ).reshape(x_block.shape)
    mask = live[:, None, None, None]
    out_maps = ((resid + outcome) * mask).astype(jnp.bfloat16)
    dy_low = (dy_block.astype(jnp.float32) * mask).astype(jnp.bfloat16)
    d_resid = dy_low.astype(jnp.float32)
    dy_rows = dy_low.reshape(count, side * side, chans_out)
    g_out = jnp.einsum("npc,npd->cd", mixed_all, dy_rows, preferred_element_type=jnp.float32)
    d_mixed = narrow(
        jnp.einsum("npd,cd->npc", dy_rows, w_out, preferred_element_type=jnp.float32).reshape(
            count, side, side, width
        )
    )
    d_mixed = d_mixed.reshape(count, side * side, chans_out).astype(jnp.bfloat16)
    d_probs = prob_total(
        jnp.einsum("nqd,nkd->nqk", d_mixed, values, preferred_element_type=jnp.float32)
    )
    d_values = jnp.einsum(
        "nqk,nqd->nkd", probs_low, d_mixed, preferred_element_type=jnp.float32
    ).astype(jnp.bfloat16)
    d_scores = (
        probs * (d_probs - jnp.sum(probs * d_probs, axis=-1, keepdims=True)) * scale
    ).astype(jnp.bfloat16)
    d_queries = jnp.einsum(
        "nqk,nkd->nqd", d_scores, keyvecs, preferred_element_type=jnp.float32
    ).astype(jnp.bfloat16)
    d_keys = jnp.einsum(
        "nqk,nqd->nkd", d_scores, queries, preferred_element_type=jnp.float32
    ).astype(jnp.bfloat16)
    d_proj = jnp.stack([d_queries, d_keys, d_values])
    g_qkv = jnp.einsum("npc,jnpd->cjd", act_three, d_proj, preferred_element_type=jnp.float32)
    d_act_three = narrow(
        jnp.einsum("jnpd,cjd->npc", d_proj, w_qkv, preferred_element_type=jnp.float32).reshape(
            count, side, side, width
        )
    )
    d_norm_three, g_gain_three, g_shift_three = group_back(
        d_act_three, normed_three, rstd_three, gain_three, size
    )
    d_resid = d_resid + d_norm_three
    g_second, d_act_two = conv_backward(act_two, w_second, d_resid.astype(jnp.bfloat16))
    d_act_two = narrow(d_act_two)
    d_hsum, g_gain_two, g_shift_two = group_back(
        d_act_two * silu_grad(norm_two), normed_two, rstd_two, gain_two, size
    )
    d_embed = jnp.sum(d_hsum, axis=(1, 2)).astype(jnp.bfloat16)
    g_embed = jnp.dot(tsil.T, d_embed, preferred_element_type=jnp.float32)
    d_temb = jnp.dot(d_embed, w_embed.T, preferred_element_type=jnp.float32) * silu_grad(temb)
    g_table = jnp.dot(onehot.astype(jnp.float32).T, d_temb, precision=HIGH)
    g_first, d_act_one = conv_backward(act_one, w_first, d_hsum.astype(jnp.bfloat16))
    d_act_one = narrow(d_act_one)
    d_norm_one, g_gain_one, g_shift_one = group_back(
        d_act_one * silu_grad(norm_one), normed_one, rstd_one, gain_one, size
    )
    d_input = (d_resid + d_norm_one).astype(jnp.bfloat16)
    grads = (
        g_first,
        g_second,
        g_embed,
        g_qkv,
        g_out,
        g_gain_one,
        g_shift_one,
        g_gain_two,
        g_shift_two,
        g_gain_three,
        g_shift_three,
    )
    return (out_maps, d_input, grads, g_table)


def sweep(local_x, local_dy, local_t, slot_ids, live_count, weights, table, funcs):
    live_all = (slot_ids < live_count).astype(jnp.float32)
    trips = local_x.shape[0] // MB
    grads_zero = tuple((jnp.zeros(w.shape, jnp.float32) for w in weights))
    start_carry = (
        jnp.zeros_like(local_x),
        jnp.zeros_like(local_x),
        grads_zero,
        jnp.zeros(table.shape, jnp.float32),
    )

    def advance(index, carry):
        out_buf, grad_buf, grad_sums, table_sum = carry
        start = index * MB
        x_block = lax.dynamic_slice_in_dim(local_x, start, MB, 0)
        dy_block = lax.dynamic_slice_in_dim(local_dy, start, MB, 0)
        t_block = lax.dynamic_slice_in_dim(local_t, start, MB, 0)
        live = lax.dynamic_slice_in_dim(live_all, start, MB, 0)
        out_maps, d_input, grads, g_table = run_block(
            x_block, dy_block, t_block, live, weights, table, funcs
        )
        out_buf = lax.dynamic_update_slice_in_dim(out_buf, out_maps, start, 0)
        grad_buf = lax.dynamic_update_slice_in_dim(grad_buf, d_input, start, 0)
        return (out_buf, grad_buf, jax.tree.map(jnp.add, grad_sums, grads), table_sum + g_table)

    return lax.fori_loop(0, trips, advance, start_carry)


def per_device(
    x_maps,
    timesteps,
    counts,
    emb_table,
    w_first,
    w_second,
    w_embed,
    w_qkv,
    w_out,
    gain_one,
    shift_one,
    gain_two,
    shift_two,
    gain_three,
    shift_three,
    cotangent,
):
    weights = (
        w_first,
        w_second,
        w_embed,
        w_qkv,
        w_out,
        gain_one,
        shift_one,
        gain_two,
        shift_two,
        gain_three,
        shift_three,
    )
    slots = x_maps.shape[0]
    live_count = counts[0]

    def widen(values):
        return lax.all_gather(values, "chan", axis=3, tiled=True)

    def narrow(values):
        return lax.psum_scatter(
            values.astype(jnp.bfloat16), "chan", scatter_dimension=3, tiled=True
        ).astype(jnp.float32)

    def score_total(values):
        return lax.psum(values.astype(jnp.bfloat16), "chan").astype(jnp.float32)

    def prob_total(values):
        return lax.psum(values.astype(jnp.bfloat16), "chan").astype(jnp.float32)

    slot_ids = jnp.arange(slots, dtype=jnp.int32)
    out_maps, d_input, grads, table_part = sweep(
        x_maps,
        cotangent,
        timesteps,
        slot_ids,
        live_count,
        weights,
        emb_table,
        (widen, narrow, score_total, prob_total),
    )
    grads = lax.psum(grads, "dp")
    table_grad = lax.psum(table_part, ("dp", "chan"))
    return (out_maps, d_input, table_grad) + tuple(grads)


def solution(mesh):
    in_specs = (
        P("dp", None, None, "chan"),
        P("dp"),
        P("dp"),
        P(),
        P(None, None, None, "chan"),
        P(None, None, None, "chan"),
        P(None, "chan"),
        P(None, None, "chan"),
        P(None, "chan"),
        P("chan"),
        P("chan"),
        P("chan"),
        P("chan"),
        P("chan"),
        P("chan"),
        P("dp", None, None, "chan"),
    )
    out_specs = (
        P("dp", None, None, "chan"),
        P("dp", None, None, "chan"),
        P(),
        P(None, None, None, "chan"),
        P(None, None, None, "chan"),
        P(None, "chan"),
        P(None, None, "chan"),
        P(None, "chan"),
        P("chan"),
        P("chan"),
        P("chan"),
        P("chan"),
        P("chan"),
        P("chan"),
    )
    return jax.shard_map(
        per_device, mesh=mesh, in_specs=in_specs, out_specs=out_specs, check_vma=False
    )
```

profile of v0, /device:TPU:0, one launch (start us, length us, event | category | flops | bytes accessed | tf_op | source)
XLA Modules:
  0.0 1582.3 jit_solution(7113563758789595579)
XLA Ops:
  11.0 1322.8 %while.61 = (s32[]{:T(128)}, bf16[8,16,16,64]{3,2,1,0:T(8,128)(2,1)}, bf16[8,16,16,64]{3,2,1,0:T(8,128)(2,1)}, f32[3,3,256,64]{2,3,1,0:T(8,128)}, f32[3,3,256,64...) while((s32[]{:T(128)}, ...), condition=%wide.region_42.43_spmd.clone, body=%wide.region_0.42_spmd.clone.sunk | while | flops 1238222720 | bytes 161420832 | solution.py:239
  16.4 4.3 reshape.1903
  23.8 17.3 %all_gather.52 = bf16[2,16,16,256]{2,1,0,3:T(8,128)(2,1)S(1)} all-gather(bf16[2,16,16,64]{2,1,0,3:T(8,128)(2,1)S(1)} %copy.380), channel_id=1, replica_groups=mesh['dp'=8,'chan'=4] {'chan'}, dimensions={3}, use_global_device_ids=true | all-gather | bytes 327680 | tf_op jit(solution)/shard_map/while/body/eval_jaxpr/all_gather | solution.py:277
  47.6 16.3 %all_gather.53 = bf16[2,16,16,256]{2,1,0,3:T(8,128)(2,1)} all-gather(bf16[2,16,16,64]{2,1,0,3:T(8,128)(2,1)S(1)} %copy.382), channel_id=1, replica_groups=mesh['dp'=8,'chan'=4] {'chan'}, dimensions={3}, use_global_device_ids=true | all-gather | bytes 327680 | tf_op jit(solution)/shard_map/while/body/eval_jaxpr/all_gather | solution.py:277
  73.4 16.6 %all_gather.54 = bf16[2,16,16,256]{2,1,0,3:T(8,128)(2,1)} all-gather(bf16[2,16,16,64]{2,1,0,3:T(8,128)(2,1)S(1)} %copy.384), channel_id=1, replica_groups=mesh['dp'=8,'chan'=4] {'chan'}, dimensions={3}, use_global_device_ids=true | all-gather | bytes 327680 | tf_op jit(solution)/shard_map/while/body/eval_jaxpr/all_gather | solution.py:277
  99.6 32.1 %all-reduce.17.cloned.1.call-done = (bf16[2,256,256]{2,1,0:T(8,128)(2,1)}, bf16[2,256,256]{2,1,0:T(8,128)(2,1)}) async-done(((bf16[2,256,256]{2,1,0:T(8,128)(2,1)}, bf16[2,256,256]{2,1,0:T(8,128)(2,1)}), (bf16[2,256,256]{2,1,0:T(8,128)(2,1)}, bf16[2,256,256]{2,1,0:T(8,128)(2,1)})) %all-reduce.17.cloned.1.call-update) | async-done | bytes 524304 | tf_op jit(solution)/shard_map/while/body/eval_jaxpr/psum | solution.py:285
  141.7 4.2 fusion.563
  146.9 15.0 all_gather.55
  168.7 5.2 reshape.1905
  176.6 18.8 %reduce-scatter.23.cloned.1.call-done = bf16[64,512]{1,0:T(8,128)(2,1)} async-done(((bf16[256,512]{1,0:T(8,128)(2,1)}), bf16[64,512]{1,0:T(8,128)(2,1)}) %reduce-scatter.23.cloned.1.call-update) | async-done | bytes 65552 | tf_op jit(solution)/shard_map/while
  235.3 4.6 copy.393
  239.8 5.2 reshape.1907
  252.2 13.0 reduce-scatter.25.cloned.1.call-done
  274.5 4.3 scatter-add.148
  306.6 4.6 copy.395
  311.2 5.2 reshape.1909
  323.4 13.3 reduce-scatter.27.cloned.1.call-done
  347.9 4.3 reshape.1903
  355.3 15.4 all_gather.52
  377.1 16.3 %all_gather.53 = bf16[2,16,16,256]{2,1,0,3:T(8,128)(2,1)} all-gather(bf16[2,16,16,64]{2,1,0,3:T(8,128)(2,1)S(1)} %copy.382), channel_id=1, replica_groups=mesh['dp'=8,'chan'=4] {'chan'}, dimensions={3}, use_global_device_ids=true | all-gather | bytes 327680 | tf_op jit(solution)/shard_map/while/body/eval_jaxpr/all_gather | solution.py:277
  402.9 16.6 %all_gather.54 = bf16[2,16,16,256]{2,1,0,3:T(8,128)(2,1)} all-gather(bf16[2,16,16,64]{2,1,0,3:T(8,128)(2,1)S(1)} %copy.384), channel_id=1, replica_groups=mesh['dp'=8,'chan'=4] {'chan'}, dimensions={3}, use_global_device_ids=true | all-gather | bytes 327680 | tf_op jit(solution)/shard_map/while/body/eval_jaxpr/all_gather | solution.py:277
  429.2 31.7 %all-reduce.17.cloned.1.call-done = (bf16[2,256,256]{2,1,0:T(8,128)(2,1)}, bf16[2,256,256]{2,1,0:T(8,128)(2,1)}) async-done(((bf16[2,256,256]{2,1,0:T(8,128)(2,1)}, bf16[2,256,256]{2,1,0:T(8,128)(2,1)}), (bf16[2,256,256]{2,1,0:T(8,128)(2,1)}, bf16[2,256,256]{2,1,0:T(8,128)(2,1)})) %all-reduce.17.cloned.1.call-update) | async-done | bytes 524304 | tf_op jit(solution)/shard_map/while/body/eval_jaxpr/psum | solution.py:285
  470.9 4.2 fusion.563
  476.1 15.0 all_gather.55
  497.9 5.2 reshape.1905
  506.0 18.6 %reduce-scatter.23.cloned.1.call-done = bf16[64,512]{1,0:T(8,128)(2,1)} async-done(((bf16[256,512]{1,0:T(8,128)(2,1)}), bf16[64,512]{1,0:T(8,128)(2,1)}) %reduce-scatter.23.cloned.1.call-update) | async-done | bytes 65552 | tf_op jit(solution)/shard_map/while
  564.4 4.6 copy.393
  569.0 5.2 reshape.1907
  581.4 13.0 reduce-scatter.25.cloned.1.call-done
  636.4 4.6 copy.395
  641.0 5.2 reshape.1909
  653.2 13.2 reduce-scatter.27.cloned.1.call-done
  677.7 4.3 reshape.1903
  685.1 15.4 all_gather.52
  707.0 16.3 %all_gather.53 = bf16[2,16,16,256]{2,1,0,3:T(8,128)(2,1)} all-gather(bf16[2,16,16,64]{2,1,0,3:T(8,128)(2,1)S(1)} %copy.382), channel_id=1, replica_groups=mesh['dp'=8,'chan'=4] {'chan'}, dimensions={3}, use_global_device_ids=true | all-gather | bytes 327680 | tf_op jit(solution)/shard_map/while/body/eval_jaxpr/all_gather | solution.py:277
  732.8 16.8 %all_gather.54 = bf16[2,16,16,256]{2,1,0,3:T(8,128)(2,1)} all-gather(bf16[2,16,16,64]{2,1,0,3:T(8,128)(2,1)S(1)} %copy.384), channel_id=1, replica_groups=mesh['dp'=8,'chan'=4] {'chan'}, dimensions={3}, use_global_device_ids=true | all-gather | bytes 327680 | tf_op jit(solution)/shard_map/while/body/eval_jaxpr/all_gather | solution.py:277
  759.2 31.7 %all-reduce.17.cloned.1.call-done = (bf16[2,256,256]{2,1,0:T(8,128)(2,1)}, bf16[2,256,256]{2,1,0:T(8,128)(2,1)}) async-done(((bf16[2,256,256]{2,1,0:T(8,128)(2,1)}, bf16[2,256,256]{2,1,0:T(8,128)(2,1)}), (bf16[2,256,256]{2,1,0:T(8,128)(2,1)}, bf16[2,256,256]{2,1,0:T(8,128)(2,1)})) %all-reduce.17.cloned.1.call-update) | async-done | bytes 524304 | tf_op jit(solution)/shard_map/while/body/eval_jaxpr/psum | solution.py:285
  806.1 15.0 all_gather.55
  827.9 5.2 reshape.1905
  835.8 18.9 %reduce-scatter.23.cloned.1.call-done = bf16[64,512]{1,0:T(8,128)(2,1)} async-done(((bf16[256,512]{1,0:T(8,128)(2,1)}), bf16[64,512]{1,0:T(8,128)(2,1)}) %reduce-scatter.23.cloned.1.call-update) | async-done | bytes 65552 | tf_op jit(solution)/shard_map/while
  894.4 4.6 copy.393
  899.0 5.2 reshape.1907
  911.4 13.0 reduce-scatter.25.cloned.1.call-done
  966.5 4.6 copy.395
  971.1 5.2 reshape.1909
  983.3 13.2 reduce-scatter.27.cloned.1.call-done
  1008.0 4.3 reshape.1903
  1015.4 15.4 all_gather.52
  1037.2 16.3 %all_gather.53 = bf16[2,16,16,256]{2,1,0,3:T(8,128)(2,1)} all-gather(bf16[2,16,16,64]{2,1,0,3:T(8,128)(2,1)S(1)} %copy.382), channel_id=1, replica_groups=mesh['dp'=8,'chan'=4] {'chan'}, dimensions={3}, use_global_device_ids=true | all-gather | bytes 327680 | tf_op jit(solution)/shard_map/while/body/eval_jaxpr/all_gather | solution.py:277
  1063.0 16.6 %all_gather.54 = bf16[2,16,16,256]{2,1,0,3:T(8,128)(2,1)} all-gather(bf16[2,16,16,64]{2,1,0,3:T(8,128)(2,1)S(1)} %copy.384), channel_id=1, replica_groups=mesh['dp'=8,'chan'=4] {'chan'}, dimensions={3}, use_global_device_ids=true | all-gather | bytes 327680 | tf_op jit(solution)/shard_map/while/body/eval_jaxpr/all_gather | solution.py:277
  1089.3 31.7 %all-reduce.17.cloned.1.call-done = (bf16[2,256,256]{2,1,0:T(8,128)(2,1)}, bf16[2,256,256]{2,1,0:T(8,128)(2,1)}) async-done(((bf16[2,256,256]{2,1,0:T(8,128)(2,1)}, bf16[2,256,256]{2,1,0:T(8,128)(2,1)}), (bf16[2,256,256]{2,1,0:T(8,128)(2,1)}, bf16[2,256,256]{2,1,0:T(8,128)(2,1)})) %all-reduce.17.cloned.1.call-update) | async-done | bytes 524304 | tf_op jit(solution)/shard_map/while/body/eval_jaxpr/psum | solution.py:285
  1136.2 15.0 all_gather.55
  1158.0 5.2 reshape.1905
  1165.9 18.8 %reduce-scatter.23.cloned.1.call-done = bf16[64,512]{1,0:T(8,128)(2,1)} async-done(((bf16[256,512]{1,0:T(8,128)(2,1)}), bf16[64,512]{1,0:T(8,128)(2,1)}) %reduce-scatter.23.cloned.1.call-update) | async-done | bytes 65552 | tf_op jit(solution)/shard_map/while
  1224.5 4.6 copy.393
  1229.1 5.2 reshape.1907
  1241.4 13.0 reduce-scatter.25.cloned.1.call-done
  1264.6 4.3 scatter-add.148
  1296.7 4.6 copy.395
  1301.3 5.2 reshape.1909
  1313.5 13.3 reduce-scatter.27.cloned.1.call-done
  1335.1 22.0 %all-reduce.5 = (f32[64]{0:T(128)}, f32[64]{0:T(128)}, f32[64]{0:T(128)}, f32[64]{0:T(128)}, f32[64]{0:T(128)}, /*index=5*/f32[64]{0:T(128)}) all-reduce(f32[64]{0:T(128)S(1)} %copy-done.84, f32[64]{0:T(128)S(1)} %copy-done.81, f32[64]{0:T(128)S(1)} %copy-done.78, f32[64]{0:T(128)S(1)} %copy-done.75, ...), channel_id=1, replica_groups=mesh['dp'=8,'chan'=4] {'dp'}, use_global_device_ids=true, to_apply=%region_49.50 | all-reduce | flops 384 | bytes 3072 | tf_op jit(solution)/shard_map/psum | solution.py:301
  1357.1 116.0 %all-reduce.13.cloned.1.call-done = f32[1000,512]{1,0:T(8,128)} async-done(((f32[1000,512]{1,0:T(8,128)}), f32[1000,512]{1,0:T(8,128)}) %all-reduce.13.cloned.1.call-update) | async-done | bytes 2048016 | tf_op jit(solution)/shard_map/psum | solution.py:302
  1473.1 94.8 %all-reduce.15.cloned.1.call-done = (f32[3,3,256,64]{2,3,1,0:T(8,128)}, f32[3,3,256,64]{2,3,1,0:T(8,128)}, f32[512,64]{0,1:T(8,128)}, f32[256,3,64]{0,2,1:T(8,128)}, f32[256,64]{0,1:T(8,128)}) async-done(((f32[3,3,256,64]{2,3,1,0:T(8,128)}, f32[3,3,256,64]{2,3,1,0:T(8,128)}, f32[512,64]{0,1:T(8,128)}, f32[256,3,64]{0,2,1:T(8,128)}, f32[256,64]{0,1:T(8,128)}), (f32[3,3,256,64]{2,3,1,0:T(8,128)}, ...) | async-done | bytes 1572880 | tf_op jit(solution)/shard_map/psum | solution.py:301
  (1595 shorter events, 628.6 us)
Async XLA Ops:
  11.0 82.9 %reduce-scatter.21.cloned.1.call-start = ((), (), s32[]{:S(2)}) async-start(), calls=%async_computation.6 | async-start | bytes 327680 | tf_op jit(solution)/shard_map/while
  20.7 111.1 %all-reduce.17.cloned.1.call-start = ((), (), s32[]{:S(2)}) async-start(), calls=%async_computation.7 | async-start | bytes 1048576 | tf_op jit(solution)/shard_map/while/body/eval_jaxpr/psum | solution.py:285
  20.8 50.9 %copy-start.45 = (f32[64]{0:T(128)}, f32[64]{0:T(128)S(1)}, u32[]{:S(2)}) copy-start(f32[64]{0:T(128)S(1)} %convert_element_type.797) | copy-start | bytes 772 | tf_op jit(solution)/shard_map/while
  20.8 25.8 %copy-start.54 = (f32[64]{0:T(128)}, f32[64]{0:T(128)S(1)}, u32[]{:S(2)}) copy-start(f32[64]{0:T(128)S(1)} %convert_element_type.795) | copy-start | bytes 772 | tf_op jit(solution)/shard_map/while
  20.9 21.9 %copy-start.52 = (f32[64]{0:T(128)}, f32[64]{0:T(128)S(1)}, u32[]{:S(2)}) copy-start(f32[64]{0:T(128)S(1)} %convert_element_type.793) | copy-start | bytes 772 | tf_op jit(solution)/shard_map/while
  20.9 25.8 %copy-start.61 = (f32[64]{0:T(128)}, f32[64]{0:T(128)S(1)}, u32[]{:S(2)}) copy-start(f32[64]{0:T(128)S(1)} %convert_element_type.794) | copy-start | bytes 772 | tf_op jit(solution)/shard_map/while
  21.0 23.6 %copy-start.65 = (s32[2]{0:T(128)}, s32[2]{0:T(128)S(1)}, u32[]{:S(2)}) copy-start(s32[2]{0:T(128)S(1)} %dynamic_slice.82) | copy-start | bytes 28 | tf_op jit(solution)/shard_map/while
  21.0 21.8 %copy-start.59 = (f32[64]{0:T(128)}, f32[64]{0:T(128)S(1)}, u32[]{:S(2)}) copy-start(f32[64]{0:T(128)S(1)} %convert_element_type.792) | copy-start | bytes 772 | tf_op jit(solution)/shard_map/while
  45.9 20.7 %copy-start.1 = (f32[2,16,16,64]{3,2,1,0:T(8,128)}, f32[2,16,16,64]{3,2,1,0:T(8,128)S(1)}, u32[]{:S(2)}) copy-start(f32[2,16,16,64]{3,2,1,0:T(8,128)S(1)} %get-tuple-element.1698) | copy-start | bytes 393220 | tf_op jit(solution)/shard_map/while
  97.5 97.9 %reduce-scatter.23.cloned.1.call-start = ((), (), s32[]{:S(2)}) async-start(), calls=%async_computation.8 | async-start | bytes 327680 | tf_op jit(solution)/shard_map/while
  99.6 36.5 %copy-start.14 = (bf16[3,2,256,64]{2,3,0,1:T(8,128)(2,1)S(1)}, bf16[3,2,256,64]{2,3,0,1:T(8,128)(2,1)}, u32[]{:S(2)}) copy-start(bf16[3,2,256,64]{2,3,0,1:T(8,128)(2,1)} %copy-done.13) | copy-start | bytes 589828 | tf_op jit(solution)/shard_map/while
  141.7 22.9 %copy-start.96 = (bf16[1,2,256,64]{2,3,1,0:T(8,128)(2,1)}, bf16[1,2,256,64]{2,3,1,0:T(8,128)(2,1)S(1)}, u32[]{:S(2)}) copy-start(bf16[1,2,256,64]{2,3,1,0:T(8,128)(2,1)S(1)} %fusion.564) | copy-start | bytes 196612 | tf_op jit(solution)/shard_map/while
  173.9 23.4 %copy-start.46 = (f32[64]{0:T(128)S(1)}, f32[64]{0:T(128)}, u32[]{:S(2)}) copy-start(f32[64]{0:T(128)} %copy-done.45) | copy-start | bytes 772 | tf_op jit(solution)/shard_map/while
  173.9 91.3 %reduce-scatter.25.cloned.1.call-start = ((), (), s32[]{:S(2)}) async-start(), calls=%async_computation.9 | async-start | bytes 327680 | tf_op jit(solution)/shard_map/while
  175.4 21.3 %copy-start.33 = (f32[256,64]{0,1:T(8,128)}, f32[256,64]{0,1:T(8,128)S(1)}, u32[]{:S(2)}) copy-start(f32[256,64]{0,1:T(8,128)S(1)} %fusion.599) | copy-start | bytes 196612 | tf_op jit(solution)/shard_map/while
  175.7 23.9 %copy-start.49 = (f32[256,3,64]{0,2,1:T(8,128)}, f32[256,3,64]{0,2,1:T(8,128)S(1)}, u32[]{:S(2)}) copy-start(f32[256,3,64]{0,2,1:T(8,128)S(1)} %fusion.598) | copy-start | bytes 589828 | tf_op jit(solution)/shard_map/while
  245.0 91.6 %reduce-scatter.27.cloned.1.call-start = ((), (), s32[]{:S(2)}) async-start(), calls=%async_computation.10 | async-start | bytes 327680 | tf_op jit(solution)/shard_map/while
  342.4 81.1 %reduce-scatter.21.cloned.1.call-start = ((), (), s32[]{:S(2)}) async-start(), calls=%async_computation.6 | async-start | bytes 327680 | tf_op jit(solution)/shard_map/while
  352.2 108.8 %all-reduce.17.cloned.1.call-start = ((), (), s32[]{:S(2)}) async-start(), calls=%async_computation.7 | async-start | bytes 1048576 | tf_op jit(solution)/shard_map/while/body/eval_jaxpr/psum | solution.py:285
  352.3 49.0 %copy-start.45 = (f32[64]{0:T(128)}, f32[64]{0:T(128)S(1)}, u32[]{:S(2)}) copy-start(f32[64]{0:T(128)S(1)} %convert_element_type.797) | copy-start | bytes 772 | tf_op jit(solution)/shard_map/while
  352.3 23.9 %copy-start.54 = (f32[64]{0:T(128)}, f32[64]{0:T(128)S(1)}, u32[]{:S(2)}) copy-start(f32[64]{0:T(128)S(1)} %convert_element_type.795) | copy-start | bytes 772 | tf_op jit(solution)/shard_map/while
  352.4 23.9 %copy-start.61 = (f32[64]{0:T(128)}, f32[64]{0:T(128)S(1)}, u32[]{:S(2)}) copy-start(f32[64]{0:T(128)S(1)} %convert_element_type.794) | copy-start | bytes 772 | tf_op jit(solution)/shard_map/while
  352.5 21.7 %copy-start.65 = (s32[2]{0:T(128)}, s32[2]{0:T(128)S(1)}, u32[]{:S(2)}) copy-start(s32[2]{0:T(128)S(1)} %dynamic_slice.82) | copy-start | bytes 28 | tf_op jit(solution)/shard_map/while
  375.5 20.7 %copy-start.1 = (f32[2,16,16,64]{3,2,1,0:T(8,128)}, f32[2,16,16,64]{3,2,1,0:T(8,128)S(1)}, u32[]{:S(2)}) copy-start(f32[2,16,16,64]{3,2,1,0:T(8,128)S(1)} %get-tuple-element.1698) | copy-start | bytes 393220 | tf_op jit(solution)/shard_map/while
  427.1 97.5 %reduce-scatter.23.cloned.1.call-start = ((), (), s32[]{:S(2)}) async-start(), calls=%async_computation.8 | async-start | bytes 327680 | tf_op jit(solution)/shard_map/while
  429.2 36.1 %copy-start.14 = (bf16[3,2,256,64]{2,3,0,1:T(8,128)(2,1)S(1)}, bf16[3,2,256,64]{2,3,0,1:T(8,128)(2,1)}, u32[]{:S(2)}) copy-start(bf16[3,2,256,64]{2,3,0,1:T(8,128)(2,1)} %copy-done.13) | copy-start | bytes 589828 | tf_op jit(solution)/shard_map/while
  470.9 22.9 %copy-start.96 = (bf16[1,2,256,64]{2,3,1,0:T(8,128)(2,1)}, bf16[1,2,256,64]{2,3,1,0:T(8,128)(2,1)S(1)}, u32[]{:S(2)}) copy-start(bf16[1,2,256,64]{2,3,1,0:T(8,128)(2,1)S(1)} %fusion.564) | copy-start | bytes 196612 | tf_op jit(solution)/shard_map/while
  503.1 23.4 %copy-start.46 = (f32[64]{0:T(128)S(1)}, f32[64]{0:T(128)}, u32[]{:S(2)}) copy-start(f32[64]{0:T(128)} %copy-done.45) | copy-start | bytes 772 | tf_op jit(solution)/shard_map/while
  503.1 91.3 %reduce-scatter.25.cloned.1.call-start = ((), (), s32[]{:S(2)}) async-start(), calls=%async_computation.9 | async-start | bytes 327680 | tf_op jit(solution)/shard_map/while
  504.8 21.1 %copy-start.33 = (f32[256,64]{0,1:T(8,128)}, f32[256,64]{0,1:T(8,128)S(1)}, u32[]{:S(2)}) copy-start(f32[256,64]{0,1:T(8,128)S(1)} %fusion.599) | copy-start | bytes 196612 | tf_op jit(solution)/shard_map/while
  505.1 23.7 %copy-start.49 = (f32[256,3,64]{0,2,1:T(8,128)}, f32[256,3,64]{0,2,1:T(8,128)S(1)}, u32[]{:S(2)}) copy-start(f32[256,3,64]{0,2,1:T(8,128)S(1)} %fusion.598) | copy-start | bytes 589828 | tf_op jit(solution)/shard_map/while
  574.2 92.2 %reduce-scatter.27.cloned.1.call-start = ((), (), s32[]{:S(2)}) async-start(), calls=%async_computation.10 | async-start | bytes 327680 | tf_op jit(solution)/shard_map/while
  672.2 81.3 %reduce-scatter.21.cloned.1.call-start = ((), (), s32[]{:S(2)}) async-start(), calls=%async_computation.6 | async-start | bytes 327680 | tf_op jit(solution)/shard_map/while
  682.0 109.0 %all-reduce.17.cloned.1.call-start = ((), (), s32[]{:S(2)}) async-start(), calls=%async_computation.7 | async-start | bytes 1048576 | tf_op jit(solution)/shard_map/while/body/eval_jaxpr/psum | solution.py:285
  682.1 49.0 %copy-start.45 = (f32[64]{0:T(128)}, f32[64]{0:T(128)S(1)}, u32[]{:S(2)}) copy-start(f32[64]{0:T(128)S(1)} %convert_element_type.797) | copy-start | bytes 772 | tf_op jit(solution)/shard_map/while
  682.1 23.9 %copy-start.54 = (f32[64]{0:T(128)}, f32[64]{0:T(128)S(1)}, u32[]{:S(2)}) copy-start(f32[64]{0:T(128)S(1)} %convert_element_type.795) | copy-start | bytes 772 | tf_op jit(solution)/shard_map/while
  682.2 23.9 %copy-start.61 = (f32[64]{0:T(128)}, f32[64]{0:T(128)S(1)}, u32[]{:S(2)}) copy-start(f32[64]{0:T(128)S(1)} %convert_element_type.794) | copy-start | bytes 772 | tf_op jit(solution)/shard_map/while
  682.3 21.7 %copy-start.65 = (s32[2]{0:T(128)}, s32[2]{0:T(128)S(1)}, u32[]{:S(2)}) copy-start(s32[2]{0:T(128)S(1)} %dynamic_slice.82) | copy-start | bytes 28 | tf_op jit(solution)/shard_map/while
  705.3 20.7 %copy-start.1 = (f32[2,16,16,64]{3,2,1,0:T(8,128)}, f32[2,16,16,64]{3,2,1,0:T(8,128)S(1)}, u32[]{:S(2)}) copy-start(f32[2,16,16,64]{3,2,1,0:T(8,128)S(1)} %get-tuple-element.1698) | copy-start | bytes 393220 | tf_op jit(solution)/shard_map/while
  757.2 97.5 %reduce-scatter.23.cloned.1.call-start = ((), (), s32[]{:S(2)}) async-start(), calls=%async_computation.8 | async-start | bytes 327680 | tf_op jit(solution)/shard_map/while
  759.2 36.1 %copy-start.14 = (bf16[3,2,256,64]{2,3,0,1:T(8,128)(2,1)S(1)}, bf16[3,2,256,64]{2,3,0,1:T(8,128)(2,1)}, u32[]{:S(2)}) copy-start(bf16[3,2,256,64]{2,3,0,1:T(8,128)(2,1)} %copy-done.13) | copy-start | bytes 589828 | tf_op jit(solution)/shard_map/while
  800.9 22.9 %copy-start.96 = (bf16[1,2,256,64]{2,3,1,0:T(8,128)(2,1)}, bf16[1,2,256,64]{2,3,1,0:T(8,128)(2,1)S(1)}, u32[]{:S(2)}) copy-start(bf16[1,2,256,64]{2,3,1,0:T(8,128)(2,1)S(1)} %fusion.564) | copy-start | bytes 196612 | tf_op jit(solution)/shard_map/while
  833.1 23.4 %copy-start.46 = (f32[64]{0:T(128)S(1)}, f32[64]{0:T(128)}, u32[]{:S(2)}) copy-start(f32[64]{0:T(128)} %copy-done.45) | copy-start | bytes 772 | tf_op jit(solution)/shard_map/while
  833.1 91.3 %reduce-scatter.25.cloned.1.call-start = ((), (), s32[]{:S(2)}) async-start(), calls=%async_computation.9 | async-start | bytes 327680 | tf_op jit(solution)/shard_map/while
  834.6 21.3 %copy-start.33 = (f32[256,64]{0,1:T(8,128)}, f32[256,64]{0,1:T(8,128)S(1)}, u32[]{:S(2)}) copy-start(f32[256,64]{0,1:T(8,128)S(1)} %fusion.599) | copy-start | bytes 196612 | tf_op jit(solution)/shard_map/while
  834.9 23.9 %copy-start.49 = (f32[256,3,64]{0,2,1:T(8,128)}, f32[256,3,64]{0,2,1:T(8,128)S(1)}, u32[]{:S(2)}) copy-start(f32[256,3,64]{0,2,1:T(8,128)S(1)} %fusion.598) | copy-start | bytes 589828 | tf_op jit(solution)/shard_map/while
  904.2 92.3 %reduce-scatter.27.cloned.1.call-start = ((), (), s32[]{:S(2)}) async-start(), calls=%async_computation.10 | async-start | bytes 327680 | tf_op jit(solution)/shard_map/while
  1002.5 81.1 %reduce-scatter.21.cloned.1.call-start = ((), (), s32[]{:S(2)}) async-start(), calls=%async_computation.6 | async-start | bytes 327680 | tf_op jit(solution)/shard_map/while
  1012.3 108.7 %all-reduce.17.cloned.1.call-start = ((), (), s32[]{:S(2)}) async-start(), calls=%async_computation.7 | async-start | bytes 1048576 | tf_op jit(solution)/shard_map/while/body/eval_jaxpr/psum | solution.py:285
  1012.4 49.0 %copy-start.45 = (f32[64]{0:T(128)}, f32[64]{0:T(128)S(1)}, u32[]{:S(2)}) copy-start(f32[64]{0:T(128)S(1)} %convert_element_type.797) | copy-start | bytes 772 | tf_op jit(solution)/shard_map/while
  1012.4 23.9 %copy-start.54 = (f32[64]{0:T(128)}, f32[64]{0:T(128)S(1)}, u32[]{:S(2)}) copy-start(f32[64]{0:T(128)S(1)} %convert_element_type.795) | copy-start | bytes 772 | tf_op jit(solution)/shard_map/while
  1012.5 23.9 %copy-start.61 = (f32[64]{0:T(128)}, f32[64]{0:T(128)S(1)}, u32[]{:S(2)}) copy-start(f32[64]{0:T(128)S(1)} %convert_element_type.794) | copy-start | bytes 772 | tf_op jit(solution)/shard_map/while
  1012.6 21.7 %copy-start.65 = (s32[2]{0:T(128)}, s32[2]{0:T(128)S(1)}, u32[]{:S(2)}) copy-start(s32[2]{0:T(128)S(1)} %dynamic_slice.82) | copy-start | bytes 28 | tf_op jit(solution)/shard_map/while
  1035.6 20.7 %copy-start.1 = (f32[2,16,16,64]{3,2,1,0:T(8,128)}, f32[2,16,16,64]{3,2,1,0:T(8,128)S(1)}, u32[]{:S(2)}) copy-start(f32[2,16,16,64]{3,2,1,0:T(8,128)S(1)} %get-tuple-element.1698) | copy-start | bytes 393220 | tf_op jit(solution)/shard_map/while
  1087.2 97.5 %reduce-scatter.23.cloned.1.call-start = ((), (), s32[]{:S(2)}) async-start(), calls=%async_computation.8 | async-start | bytes 327680 | tf_op jit(solution)/shard_map/while
  1089.3 36.1 %copy-start.14 = (bf16[3,2,256,64]{2,3,0,1:T(8,128)(2,1)S(1)}, bf16[3,2,256,64]{2,3,0,1:T(8,128)(2,1)}, u32[]{:S(2)}) copy-start(bf16[3,2,256,64]{2,3,0,1:T(8,128)(2,1)} %copy-done.13) | copy-start | bytes 589828 | tf_op jit(solution)/shard_map/while
  1131.0 22.9 %copy-start.96 = (bf16[1,2,256,64]{2,3,1,0:T(8,128)(2,1)}, bf16[1,2,256,64]{2,3,1,0:T(8,128)(2,1)S(1)}, u32[]{:S(2)}) copy-start(bf16[1,2,256,64]{2,3,1,0:T(8,128)(2,1)S(1)} %fusion.564) | copy-start | bytes 196612 | tf_op jit(solution)/shard_map/while
  1163.1 23.4 %copy-start.46 = (f32[64]{0:T(128)S(1)}, f32[64]{0:T(128)}, u32[]{:S(2)}) copy-start(f32[64]{0:T(128)} %copy-done.45) | copy-start | bytes 772 | tf_op jit(solution)/shard_map/while
  1163.2 91.3 %reduce-scatter.25.cloned.1.call-start = ((), (), s32[]{:S(2)}) async-start(), calls=%async_computation.9 | async-start | bytes 327680 | tf_op jit(solution)/shard_map/while
  1164.7 21.3 %copy-start.33 = (f32[256,64]{0,1:T(8,128)}, f32[256,64]{0,1:T(8,128)S(1)}, u32[]{:S(2)}) copy-start(f32[256,64]{0,1:T(8,128)S(1)} %fusion.599) | copy-start | bytes 196612 | tf_op jit(solution)/shard_map/while
  1165.0 23.9 %copy-start.49 = (f32[256,3,64]{0,2,1:T(8,128)}, f32[256,3,64]{0,2,1:T(8,128)S(1)}, u32[]{:S(2)}) copy-start(f32[256,3,64]{0,2,1:T(8,128)S(1)} %fusion.598) | copy-start | bytes 589828 | tf_op jit(solution)/shard_map/while
  1234.3 92.5 %reduce-scatter.27.cloned.1.call-start = ((), (), s32[]{:S(2)}) async-start(), calls=%async_computation.10 | async-start | bytes 327680 | tf_op jit(solution)/shard_map/while
  1333.8 139.3 %all-reduce.13.cloned.1.call-start = ((), (), s32[]{:S(2)}) async-start(), calls=%async_computation.4 | async-start | bytes 4096000 | tf_op jit(solution)/shard_map/psum | solution.py:302
  1334.4 233.5 %all-reduce.15.cloned.1.call-start = ((), (), s32[]{:S(2)}) async-start(), calls=%async_computation.5 | async-start | bytes 3145728 | tf_op jit(solution)/shard_map/psum | solution.py:301
  (325 other events, 2536.1 us)
Sparse Core Ops, SparseCore 0:
  20.8 22.7 reduce-scatter.20
  97.7 34.0 all-reduce.16
  174.0 21.3 reduce-scatter.22
  245.2 20.0 reduce-scatter.24
  316.5 20.0 reduce-scatter.26
  352.3 20.0 reduce-scatter.20
  427.3 33.6 all-reduce.16
  503.2 21.3 reduce-scatter.22
  574.3 20.0 reduce-scatter.24
  646.3 19.9 reduce-scatter.26
  682.1 20.0 reduce-scatter.20
  757.3 33.6 all-reduce.16
  833.2 21.3 reduce-scatter.22
  904.3 20.0 reduce-scatter.24
  976.4 20.0 reduce-scatter.26
  1012.4 20.0 reduce-scatter.20
  1087.3 33.6 all-reduce.16
  1163.3 21.3 reduce-scatter.22
  1234.4 19.9 reduce-scatter.24
  1306.6 20.0 reduce-scatter.26
Sparse Core Ops, SparseCore 1:
  1340.2 132.8 all-reduce.12
  1478.1 89.7 all-reduce.14
where the time goes:
time: 1600 us; the launch traced here: 1580 us
  waiting for transfers between devices  519 us (32%)
  local copies, waits for them, and re-layouts  432 us (27%)
  matrix products  286 us (18%)
  blocking collectives  277 us (17%)
  other arithmetic  39.2 us (2%)
  between operations  16.6 us (1%)
    all_gather x16, blocking collectives, widen(): return lax.all_gather(values, 'chan', axis=3, tiled=True)  255 us
    while x776, local copies, waits for them, and re-layouts  189 us
    while x36, waiting for transfers between devices  180 us
    scatter-add x56, local copies, waits for them, and re-layouts, conv_backward(): dpad.at[:, row:row + side, col:col + side, :]  147 us
    dot_general x72, matrix products, conv_backward(): jnp.einsum('nhwd,cd->nhwc', grad_out, weight[row, col], preferred_element...  133 us
    psum x4, waiting for transfers between devices, score_total(): return lax.psum(values.astype(jnp.bfloat16), 'chan').astype(jnp.float32)  127 us
    psum x1, waiting for transfers between devices, per_device(): table_grad = lax.psum(table_part, ('dp', 'chan'))  116 us
    psum x1, waiting for transfers between devices, per_device(): grads = lax.psum(grads, 'dp')  94.8 us
  transfers between devices with their start and end apart: 22, of which 18 were waited for; matrix products, arithmetic and copies ran while one was open for 9% of the time, Pallas kernels for 0%

commit v1 on v0

v1 whole, which is shorter than its diff:
```python
import functools
from types import SimpleNamespace

import jax
import jax.numpy as jnp
from jax import lax
from jax.experimental import pallas as pl
from jax.experimental.pallas import tpu as pltpu
from jax.sharding import PartitionSpec as P

F32 = jnp.float32
BF = jnp.bfloat16
MESH = pl.DeviceIdType.MESH
EPS = 1e-06
GROUPS = 32
CHAN = 4
ROWS = 256
C = 256
SL = C // CHAN
GAP = 16
STEP = ROWS + GAP
TALL = 2 * ROWS + GAP
CH = 32
COUNT = ROWS * (C // GROUPS)


def dot(a, b):
    return jnp.dot(a, b, preferred_element_type=F32)


def dot_nt(a, b):
    return lax.dot_general(a, b, (((1,), (1,)), ((), ())), preferred_element_type=F32)


def sigmoid(u):
    return 0.5 * jnp.tanh(0.5 * u) + 0.5


def fold(v):
    return v.reshape(v.shape[0] // 8, 8, v.shape[1]).sum(axis=0)


def group_total(rows, bd):
    at = lax.broadcasted_iota(jnp.int32, (8, C), 0)
    stack = jnp.zeros((8, C), F32)
    for i, row in enumerate(rows):
        stack = jnp.where(at == i, row, stack)
    high = stack.astype(BF).astype(F32)
    rest = stack - high
    mid = rest.astype(BF).astype(F32)
    parts = jnp.concatenate([high, mid, rest - mid, jnp.zeros((8, C), F32)], axis=0)
    total = dot(parts.astype(BF), bd)
    total = total[0:8] + total[8:16] + total[16:24]
    return [total[i : i + 1] for i in range(len(rows))]


def chunk_at(i):
    return pl.multiple_of(i * CH, CH)


def passes(body, carry=None):
    carry = (0, 0) if carry is None else carry

    def step(i, held):
        return tuple(body(m, chunk_at(i), held[m]) for m in range(2))

    return lax.fori_loop(0, ROWS // CH, step, carry)


def zero_pair():
    return (jnp.zeros((8, C), F32), jnp.zeros((8, C), F32))


def col(v):
    return jnp.sum(v, axis=0, keepdims=True)


def write_shift(dst, m, at, value, forward):
    place = lax.broadcasted_iota(jnp.int32, (CH, C), 0) % 16
    before = jnp.where(place == 0, 0.0, pltpu.roll(value, 1, 0))
    after = jnp.where(place == 15, 0.0, pltpu.roll(value, CH - 1, 0))
    first, last = (before, after) if forward else (after, before)
    rows = pl.ds(pl.multiple_of(at + (GAP + m * STEP), 16), CH)
    dst[rows, 0:C] = first.astype(BF)
    dst[rows, C : 2 * C] = value.astype(BF)
    dst[rows, 2 * C : 3 * C] = last.astype(BF)


def norm_forward(load, n_ref, gain, shift, bd, emit):
    def sums(m, at, held):
        return held + fold(load(m, at))

    total = passes(sums, zero_pair())
    mean = group_total([col(t) for t in total], bd)
    mean = [v * (1.0 / COUNT) for v in mean]

    def squares(m, at, held):
        d = load(m, at) - mean[m]
        return held + fold(d * d)

    total = passes(squares, zero_pair())
    var = group_total([col(t) for t in total], bd)
    rstd = [lax.rsqrt(v * (1.0 / COUNT) + EPS) for v in var]

    def last(m, at, held):
        n = (load(m, at) - mean[m]) * rstd[m]
        n_ref[pl.ds(pl.multiple_of(at + m * ROWS, CH), CH), :] = n
        emit(m, at, n * gain + shift)
        return held

    passes(last)
    return rstd


def norm_back(d_ref, n_ref, gain, shift, rstd, bd, active, e_ref, e_at, emit):
    def rows(m, at):
        return pl.ds(pl.multiple_of(at + m * STEP, 16), CH)

    def first(m, at, held):
        d = d_ref[rows(m, at), :]
        n = n_ref[pl.ds(pl.multiple_of(at + m * ROWS, CH), CH), :]
        if active:
            u = n * gain + shift
            s = sigmoid(u)
            d = d * (s * (1.0 + u * (1.0 - s)))
            d_ref[rows(m, at), :] = d
        return (held[0] + fold(d), held[1] + fold(d * n))

    total = passes(first, (zero_pair(), zero_pair()))
    ones = [col(t[0]) for t in total]
    twos = [col(t[1]) for t in total]
    e_ref[e_at : e_at + 1, :] = twos[0] + twos[1]
    e_ref[e_at + 1 : e_at + 2, :] = ones[0] + ones[1]
    means = group_total([gain * v for v in ones + twos], bd)
    means = [v * (1.0 / COUNT) for v in means]

    def second(m, at, held):
        d = d_ref[rows(m, at), :]
        n = n_ref[pl.ds(pl.multiple_of(at + m * ROWS, CH), CH), :]
        return emit(m, at, rstd[m] * (d * gain - means[m] - n * means[2 + m]), held)

    return second


def unpack(low, high):
    lane = lax.broadcasted_iota(jnp.int32, low.shape, 1)
    first = jnp.where(lane < SL, low, pltpu.roll(high, SL, 1))
    second = jnp.where(lane < SL, pltpu.roll(low, SL, 1), high)
    return first, second


def conv_forward(a_ref, w_ref, h_ref, ready):
    for row in range(3):
        ready(row)
        total = None
        for c in range(3):
            part = dot_nt(a_ref[16 * row : 16 * row + TALL, C * c : C * c + C], w_ref[3 * row + c])
            total = part if total is None else total + part
        h_ref[...] = total if row == 0 else h_ref[...] + total


def conv_back(d_ref, w_ref, h_ref):
    for row in range(3):
        at = 16 * (2 - row)
        w = w_ref[3 * row : 3 * row + 3].reshape(3 * C, C)
        part = dot(d_ref[at : at + TALL, :], w)
        h_ref[...] = part if row == 0 else h_ref[...] + part


def conv_weight(a_ref, turned, dw_ref, row):
    for c in range(3):
        total = None
        for m in range(2):
            at = 16 * row + STEP * m
            part = dot(turned[m], a_ref[at : at + ROWS, C * c : C * c + C])
            total = part if total is None else total + part
        dw_ref[3 * row + c] = total.astype(BF)


class Links:
    def __init__(self, send, recv, own):
        self.send, self.recv, self.own = send, recv, own
        self.used, self.local = 0, 0
        self.sent = []

    def remote(self, src, dst, device):
        at = self.used
        self.used += 1
        copy = pltpu.make_async_remote_copy(
            src_ref=src, dst_ref=dst, send_sem=self.send.at[at], recv_sem=self.recv.at[at],
            device_id=device, device_id_type=MESH)
        copy.start()
        self.sent.append(copy)
        return copy

    def here(self, src, dst):
        copy = pltpu.make_async_copy(src, dst, self.own.at[self.local])
        self.local += 1
        copy.start()
        return copy

    def close(self):
        for copy in self.sent:
            copy.wait_send()


def block_sizes(n_dp):
    team = min(8, n_dp)
    return team, n_dp // team


class Reduction:
    def __init__(self, at, links, grad, out, work):
        self.at, self.links, self.grad, self.out, self.work = at, links, grad, out, work
        self.taps = grad.shape[0]

    def rows_of(self, y, core):
        return pl.ds(pl.multiple_of(SL * (2 * y + core), SL), SL)

    def core(self):
        at, w = self.at, self.work
        self.waits = [
            self.links.remote(self.grad.at[:, self.rows_of(y, 1 - at.core), :], w.rc.at[y], at.sibling)
            for y in range(2)]

    def cross(self):
        at, w = self.at, self.work
        for copy in self.waits:
            copy.wait_recv()
        far = 1 - at.y
        for t in range(self.taps):
            w.sy[t] = (self.grad[t, self.rows_of(far, at.core), :].astype(F32) + w.rc[far, t].astype(F32)).astype(BF)
        self.waits = [self.links.remote(w.sy, w.ry, at.across)]

    def piece(self, ref, p):
        at = self.at
        span = ref.shape[1] // (at.team // 2)
        half, quarter = p // (at.team // 2), p % (at.team // 2)
        return ref.at[half, pl.ds(pl.multiple_of(span * quarter, span), span), :]

    def scatter(self):
        at, w = self.at, self.work
        for copy in self.waits:
            copy.wait_recv()
        for t in range(self.taps):
            whole = (self.grad[t, self.rows_of(at.y, at.core), :].astype(F32) + w.rc[at.y, t].astype(F32)
                     + w.ry[t].astype(F32)).astype(BF)
            for half in range(2):
                w.sl[half, SL * t : SL * t + SL, :] = whole[:, 128 * half : 128 * half + 128]
        self.waits = []
        for s in range(1, at.team):
            p = (at.rank + s) % at.team
            self.waits.append(self.links.remote(self.piece(w.sl, p), w.rr.at[s], at.mate(p)))

    def spread(self):
        at, w = self.at, self.work
        for copy in self.waits:
            copy.wait_recv()
        total = self.piece(w.sl, at.rank)[...].astype(F32)
        for s in range(1, at.team):
            total = total + w.rr[s].astype(F32)
        w.pc[...] = total.astype(BF)
        if at.teams > 1:
            copies = [self.links.here(w.pc, w.rt.at[at.lead])]
            for s in range(1, at.teams):
                other = (at.lead + s) % at.teams
                copies.append(self.links.remote(w.pc, w.rt.at[at.lead], at.device(other * at.team + at.rank)))
            copies[0].wait()
            for copy in copies[1:]:
                copy.wait_recv()
                copy.wait_send()
                self.links.sent = [c for c in self.links.sent if c is not copy]
            total = w.rt[0].astype(F32)
            for s in range(1, at.teams):
                total = total + w.rt[s].astype(F32)
            w.pc[...] = total.astype(BF)
        target = self.piece(self.out, at.rank)
        self.own = self.links.here(w.pc, target)
        self.waits = []
        for s in range(1, at.team):
            self.waits.append(self.links.remote(w.pc, target, at.mate((at.rank + s) % at.team)))

    def finish(self):
        self.own.wait()
        for copy in self.waits:
            copy.wait_recv()


ITEMS = (("ga", 4), ("gb", 9), ("gc", 3), ("gd", 3), ("ge", 3))


def mega(n_dp, names, *refs):
    r = SimpleNamespace(**dict(zip(names, refs)))
    team, teams = block_sizes(n_dp)
    dp, chan = lax.axis_index("dp"), lax.axis_index("chan")
    core, y = chan % 2, chan // 2
    sibling, across, corner = (dp, 2 * y + 1 - core), (dp, 2 * (1 - y) + core), (dp, 2 * (1 - y) + 1 - core)
    quads = (sibling, across, corner)
    rank, lead = dp % team, dp // team
    at = SimpleNamespace(
        core=core, y=y, sibling=sibling, across=across, team=team, teams=teams, rank=rank, lead=lead,
        mate=lambda p: (lead * team + p, chan), device=lambda p: (p, chan))
    links = Links(r.send, r.recv, r.own)

    def others():
        return [(lax.rem(dp + s, n_dp), chan) for s in range(1, n_dp)]

    loads = SimpleNamespace(x=links.here(r.x, r.xl), dy=links.here(r.dy, r.dyl))
    barrier = pltpu.get_barrier_semaphore()
    for device in quads:
        pl.semaphore_signal(barrier, inc=1, device_id=device, device_id_type=MESH)
    for device in others():
        pl.semaphore_signal(barrier, inc=1, device_id=device, device_id_type=MESH)
    mine = pl.ds(pl.multiple_of(SL * chan, SL), SL)
    fill = [
        links.here(r.w1, r.w1g.at[:, mine, :]), links.here(r.we, r.weg.at[mine, :]),
        links.here(r.w2, r.w2g.at[:, mine, :]), links.here(r.wq, r.wqg.at[0:3, mine, :]),
        links.here(r.wo, r.wqg.at[3, mine, :])]

    at_row = lax.broadcasted_iota(jnp.int32, (C, C), 0) // (C // GROUPS)
    at_col = lax.broadcasted_iota(jnp.int32, (C, C), 1) // (C // GROUPS)
    r.bd[...] = jnp.where(at_row == at_col, 1.0, 0.0).astype(BF)
    for ref in (r.a1, r.a2, r.dd):
        for gap in range(3):
            ref[gap * STEP : gap * STEP + GAP, :] = jnp.zeros((GAP, 3 * C), BF)
    row8 = lax.broadcasted_iota(jnp.int32, (8, 128), 0)
    times = jnp.zeros((8, 128), F32)
    for i in range(8):
        times = jnp.where(row8 == i, r.ts[i].astype(F32), times)
    r.tl[...] = times
    r.pg[chan] = r.par[...]

    def pack(src, dst):
        for k in range(CHAN):
            for half in range(2):
                rows = slice(128 * half, 128 * half + 128)
                both = jnp.concatenate([src[2 * k, rows, :].astype(F32), src[2 * k + 1, rows, :].astype(F32)], axis=1)
                dst[k, rows, :] = both.astype(BF)

    loads.x.wait()
    pack(r.xl, r.xp)
    r.xg[chan] = r.xp[chan]
    pl.semaphore_wait(barrier, CHAN - 1 + n_dp - 1)

    moves_x = [links.remote(r.xp.at[d[1]], r.xg.at[chan], d) for d in quads]
    moves_par = [links.remote(r.par, r.pg.at[chan], d) for d in quads]

    def share(src, dst):
        return [links.remote(src, dst, d) for d in (sibling, across)]

    def relay(moves, piece):
        moves[1].wait_recv()
        moves.append(links.remote(piece, piece, sibling))

    def landed(moves):
        moves[0].wait_recv()
        moves[2].wait_recv()

    far = pl.ds(pl.multiple_of(SL * (2 * (1 - y) + core), SL), SL)

    def share_conv(w, g):
        return [share(w.at[3 * row : 3 * row + 3], g.at[3 * row : 3 * row + 3, mine, :]) for row in range(3)]

    moves_w1 = share_conv(r.w1, r.w1g)
    moves_we = share(r.we, r.weg.at[mine, :])
    moves_w2 = share_conv(r.w2, r.w2g)
    moves_wq = share(r.wq, r.wqg.at[0:3, mine, :])
    moves_wo = share(r.wo, r.wqg.at[3, mine, :])
    loads.dy.wait()
    pack(r.dyl, r.dyp)
    r.dyg[chan] = r.dyp[chan]
    moves_dy = [links.remote(r.dyp.at[d[1]], r.dyg.at[chan], d) for d in quads]
    tall_own = links.here(r.tl, r.tall.at[dp])
    moves_t = [links.remote(r.tl, r.tall.at[dp], d) for d in others()]

    steps = r.table.shape[0]
    own_t = jnp.broadcast_to(times[:, 0:1], (8, steps))
    hot = jnp.where(own_t == lax.broadcasted_iota(jnp.int32, (8, steps), 1).astype(F32), 1.0, 0.0)
    hot = jnp.concatenate([hot, jnp.zeros((8, steps), F32)], axis=0).astype(BF)
    temb = dot(hot, r.table[...])
    tsil = (temb * sigmoid(temb)).astype(BF)

    bd = r.bd[...]
    for copy in moves_x + moves_par:
        copy.wait_recv()
    for b in range(2):
        first, _ = unpack(r.pg[2 * b], r.pg[2 * b + 1])
        r.pa[:, 128 * b : 128 * b + 128] = first
    par = r.pa[...]
    gain1, shift1, gain2, shift2, gain3, shift3 = [par[i : i + 1] for i in range(6)]

    def spread_out(src, at, dst, scale=None):
        for b in range(2):
            pair = unpack(src[2 * b, pl.ds(at, CH), :].astype(F32), src[2 * b + 1, pl.ds(at, CH), :].astype(F32))
            for m in range(2):
                value = pair[m] if scale is None else pair[m] * scale[m]
                dst[pl.ds(pl.multiple_of(at + m * ROWS, CH), CH), 128 * b : 128 * b + 128] = value.astype(dst.dtype)

    def open_x(i, held):
        spread_out(r.xg, chunk_at(i), r.xf)
        return held

    lax.fori_loop(0, ROWS // CH, open_x, 0)

    def rows_of(m, at):
        return pl.ds(pl.multiple_of(at + m * ROWS, CH), CH)

    def rows_gap(m, at):
        return pl.ds(pl.multiple_of(at + m * STEP, 16), CH)

    def to_shift(dst):
        def emit(m, at, u):
            write_shift(dst, m, at, u * sigmoid(u), True)
        return emit

    rstd1 = norm_forward(lambda m, at: r.xf[rows_of(m, at), :], r.n1, gain1, shift1, bd, to_shift(r.a1))
    for copy in fill:
        copy.wait()
    for row in range(3):
        relay(moves_w1[row], r.w1g.at[3 * row : 3 * row + 3, far, :])
    relay(moves_we, r.weg.at[far, :])
    conv_forward(r.a1, r.w1g, r.h, lambda row: landed(moves_w1[row]))
    landed(moves_we)
    for row in range(3):
        relay(moves_w2[row], r.w2g.at[3 * row : 3 * row + 3, far, :])
    r.emb[0:16, :] = dot_nt(tsil, r.weg[...])
    emb = [r.emb[pl.ds(2 * chan + m, 1), :] for m in range(2)]
    we_out = links.here(r.weg, r.weo)

    rstd2 = norm_forward(lambda m, at: r.h[rows_gap(m, at), :] + emb[m], r.n2, gain2, shift2, bd, to_shift(r.a2))
    relay(moves_wq, r.wqg.at[0:3, far, :])
    relay(moves_wo, r.wqg.at[3, far, :])
    conv_forward(r.a2, r.w2g, r.h, lambda row: landed(moves_w2[row]))

    def load_resid(m, at):
        return r.xf[rows_of(m, at), :] + r.h[rows_gap(m, at), :]

    def to_a3(m, at, u):
        r.a3[rows_of(m, at), :] = u.astype(BF)

    rstd3 = norm_forward(load_resid, r.n3, gain3, shift3, bd, to_a3)
    landed(moves_wq)
    landed(moves_wo)
    for j, ref in enumerate((r.q, r.k, r.v)):
        ref[...] = dot_nt(r.a3[...], r.wqg[j]).astype(BF)
    for copy in moves_dy:
        copy.wait_recv()
    count = r.cnt[0]
    live = [jnp.where(2 * chan + m < count, 1.0, 0.0).astype(F32) for m in range(2)]

    def open_dy(i, held):
        spread_out(r.dyg, chunk_at(i), r.g, live)
        return held

    lax.fori_loop(0, ROWS // CH, open_dy, 0)
    scale = C ** (-0.5)
    half = [slice(0, ROWS), slice(ROWS, 2 * ROWS)]
    for m in range(2):
        s = dot_nt(r.q[half[m], :], r.k[half[m], :]) * scale
        p = jnp.exp(s - jnp.max(s, axis=1, keepdims=True))
        p = p * (1.0 / jnp.sum(p, axis=1, keepdims=True))
        r.p[half[m], :] = p
        r.pb[half[m], :] = p.astype(BF)
        r.o[half[m], :] = dot(p.astype(BF), r.v[half[m], :]).astype(BF)
    r.big[...] = dot_nt(r.o[...], r.wqg[3])

    def pack_out(at, pair, dst):
        for b in range(2):
            even, odd = unpack(*(v[:, 128 * b : 128 * b + 128] for v in pair))
            dst[2 * b, pl.ds(at, CH), :] = even.astype(BF)
            dst[2 * b + 1, pl.ds(at, CH), :] = odd.astype(BF)

    def to_y(i, held):
        at = chunk_at(i)
        pack_out(at, [(load_resid(m, at) + r.big[rows_of(m, at), :]) * live[m] for m in range(2)], r.yp)
        return held

    lax.fori_loop(0, ROWS // CH, to_y, 0)
    own_y = links.here(r.yp.at[chan], r.yo.at[chan])
    moves_y = [links.remote(r.yp.at[d[1]], r.yo.at[chan], d) for d in quads]

    for m in range(2):
        r.turn[m] = r.g[half[m], :].T
    r.dqo[3] = (dot(r.turn[0], r.o[half[0], :]) + dot(r.turn[1], r.o[half[1], :])).astype(BF)
    r.do[...] = dot(r.g[...], r.wqg[3]).astype(BF)
    for m in range(2):
        dp_m = dot_nt(r.do[half[m], :], r.v[half[m], :])
        p = r.p[half[m], :]
        ds = (p * (dp_m - jnp.sum(p * dp_m, axis=1, keepdims=True)) * scale).astype(BF)
        r.dv[half[m], :] = dot(r.pb[half[m], :].T, r.do[half[m], :]).astype(BF)
        r.dq[half[m], :] = dot(ds, r.k[half[m], :]).astype(BF)
        r.dk[half[m], :] = dot(ds.T, r.q[half[m], :]).astype(BF)
    for j, ref in enumerate((r.dq, r.dk, r.dv)):
        parts = [dot(ref[half[m], :].T, r.a3[half[m], :]) for m in range(2)]
        r.dqo[j] = (parts[0] + parts[1]).astype(BF)
    work = lambda name: SimpleNamespace(**{k: getattr(r, name + "_" + k) for k in ("rc", "sy", "ry", "sl", "rr", "pc", "rt")})
    red = SimpleNamespace()
    red.a = Reduction(at, links, r.dqo, r.ga, work("ga"))
    red.a.core()
    for m in range(2):
        total = None
        for j, ref in enumerate((r.dq, r.dk, r.dv)):
            part = dot(ref[half[m], :], r.wqg[j])
            total = part if total is None else total + part
        r.h[m * STEP : m * STEP + ROWS, :] = total
    red.a.cross()

    def to_dres(m, at, dv, held):
        value = r.g[rows_of(m, at), :].astype(F32) + dv
        r.dres[rows_of(m, at), :] = value
        write_shift(r.dd, m, at, value, False)
        return held

    passes(norm_back(r.h, r.n3, gain3, shift3, rstd3, bd, False, r.e, 4, to_dres))

    def turn():
        for m in range(2):
            r.turn[m] = r.dd[GAP + STEP * m : GAP + STEP * m + ROWS, C : 2 * C].T

    turn()
    for row in range(3):
        conv_weight(r.a2, r.turn, r.dw2, row)
    red.b = Reduction(at, links, r.dw2, r.gb, work("gb"))
    red.b.core()
    red.a.scatter()
    conv_back(r.dd, r.w2g, r.h)
    red.b.cross()

    def to_dh1(m, at, dv, held):
        write_shift(r.dd, m, at, dv, False)
        return held + fold(dv)

    demb = passes(norm_back(r.h, r.n2, gain2, shift2, rstd2, bd, True, r.e, 2, to_dh1), zero_pair())
    for m in range(2):
        r.dm[chan, m : m + 1, :] = col(demb[m]).astype(BF).astype(F32)
    moves_dm = [links.remote(r.dm.at[chan], r.dm.at[chan], d) for d in quads]
    turn()
    tail = []
    for row, name in enumerate(("gc", "gd", "ge")):
        conv_weight(r.a1, r.turn, r.dw1, row)
        item = Reduction(at, links, r.dw1.at[3 * row : 3 * row + 3], getattr(r, name), work(name))
        item.core()
        tail.append(item)
    red.a.spread()
    red.b.scatter()
    for item in tail:
        item.cross()
    for copy in moves_dm:
        copy.wait_recv()
    for j in range(CHAN):
        r.dl[2 * j : 2 * j + 2, :] = r.dm[j, 0:2, :]
    own_dm = links.here(r.dl, r.rows.at[dp])
    moves_rows = [links.remote(r.dl, r.rows.at[dp], d) for d in others()]
    conv_back(r.dd, r.w1g, r.h)

    def to_maps(i, held):
        at = chunk_at(i)
        pair = [back1(m, at, 0) for m in range(2)]
        pack_out(at, pair, r.mp)
        return held

    back1 = norm_back(r.h, r.n1, gain1, shift1, rstd1, bd, True, r.e, 0,
                      lambda m, at, dv, held: r.dres[rows_of(m, at), :] + dv)
    lax.fori_loop(0, ROWS // CH, to_maps, 0)
    own_mp = links.here(r.mp.at[chan], r.mo.at[chan])
    moves_mp = [links.remote(r.mp.at[d[1]], r.mo.at[chan], d) for d in quads]
    for b in range(2):
        block = r.e[:, 128 * b : 128 * b + 128]
        r.es[2 * b] = block
        r.es[2 * b + 1] = pltpu.roll(block, SL, 1)
    r.er[chan] = r.es[chan]
    moves_e = [links.remote(r.es.at[d[1]], r.er.at[chan], d) for d in quads]
    for item in tail:
        item.scatter()
    red.b.spread()
    for copy in moves_e:
        copy.wait_recv()
    r.et[...] = r.er[0] + r.er[1] + r.er[2] + r.er[3]
    own_e = links.here(r.et, r.ext.at[dp])
    moves_ext = [links.remote(r.et, r.ext.at[dp], d) for d in others()]
    for item in tail:
        item.spread()
    for item in [red.a, red.b] + tail:
        item.finish()
    for copy in (own_y, own_dm, own_mp, own_e, we_out, tall_own):
        copy.wait()
    for copy in moves_y + moves_mp + moves_rows + moves_ext + moves_t:
        copy.wait_recv()
    links.close()


def finish(n_dp, rows, tall, ext, ga, gb, gc, gd, ge, yo, mo, weg, table,
           y_out, dm_out, dt_out, d1_out, d2_out, de_out, dq_out, do_out, e0, e1, e2, e3, e4, e5, turned):
    maps = 8 * n_dp
    chan = lax.axis_index("chan")
    steps = table.shape[0]
    dem32 = rows[...].reshape(maps, C)
    dem = dem32.astype(BF)
    times = tall[...].reshape(maps, 128)
    wide = jnp.broadcast_to(times[:, 0:1], (maps, steps))
    hot = jnp.where(wide == lax.broadcasted_iota(jnp.int32, (maps, steps), 1).astype(F32), 1.0, 0.0)
    temb = dot(hot.astype(BF), table[...])
    s = sigmoid(temb)
    tsil = (temb * s).astype(BF)
    turned[...] = dem32.T
    own = turned[pl.ds(pl.multiple_of(SL * chan, SL), SL), :].astype(BF)
    de_out[...] = dot(own, tsil)
    dtemb = dot(dem, weg[...]) * (s * (1.0 + temb * (1.0 - s)))
    high = dtemb.astype(BF)
    low = (dtemb - high.astype(F32)).astype(BF)
    both = jnp.concatenate([high, low], axis=0)
    lanes = times.T[0:1, :]
    tall_hot = jnp.where(lax.broadcasted_iota(jnp.int32, (steps, maps), 0).astype(F32) == lanes, 1.0, 0.0)
    tall_hot = jnp.concatenate([tall_hot, tall_hot], axis=1).astype(BF)
    dt_out[...] = dot(tall_hot, both)

    def whole(src, dst, taps):
        for i, t in enumerate(taps):
            for half in range(2):
                dst[i, :, 128 * half : 128 * half + 128] = src[half, SL * t : SL * t + SL, :].astype(F32)

    whole(ga, dq_out, range(3))
    whole(ga, do_out, [3])
    whole(gb, d2_out, range(9))
    for row, src in enumerate((gc, gd, ge)):
        whole(src, d1_out.at[3 * row : 3 * row + 3], range(3))
    total = ext[0]
    for i in range(1, n_dp):
        total = total + ext[i]
    for i, out in enumerate((e0, e1, e2, e3, e4, e5)):
        out[...] = total[i : i + 1, 0:SL]
    for src, dst in ((yo, y_out), (mo, dm_out)):
        for j in range(CHAN):
            block = src[j].astype(F32)
            dst[2 * j] = block[:, 0:SL].astype(BF)
            dst[2 * j + 1] = pltpu.roll(block, SL, 1)[:, 0:SL].astype(BF)


def per_device(x_maps, timesteps, counts, emb_table, w_first, w_second, w_embed, w_qkv, w_out, gain_one, shift_one,
               gain_two, shift_two, gain_three, shift_three, cotangent, *, n_dp):
    team, teams = block_sizes(n_dp)
    slots, side, _, _ = x_maps.shape
    emb = w_embed.shape[0]
    steps = emb_table.shape[0]
    par = jnp.stack([gain_one, shift_one, gain_two, shift_two, gain_three, shift_three]).astype(F32)
    par = jnp.pad(par, ((0, 2), (0, 128 - SL)))
    inputs = dict(
        x=x_maps.reshape(slots, side * side, SL), dy=cotangent.reshape(slots, side * side, SL),
        ts=timesteps, cnt=counts, table=emb_table,
        w1=jnp.swapaxes(w_first, 2, 3).reshape(9, SL, C), w2=jnp.swapaxes(w_second, 2, 3).reshape(9, SL, C),
        we=w_embed.T, wq=jnp.transpose(w_qkv, (1, 2, 0)), wo=w_out.T, par=par)
    anywhere = pl.BlockSpec(memory_space=pl.ANY)
    vmem = pl.BlockSpec(memory_space=pltpu.VMEM)
    smem = pl.BlockSpec(memory_space=pltpu.SMEM)
    where = dict(ts=smem, cnt=smem, table=vmem, par=vmem)

    def of(shape, dtype):
        return jax.ShapeDtypeStruct(shape, dtype)

    outputs = dict(
        yo=of((CHAN, ROWS, 128), BF), mo=of((CHAN, ROWS, 128), BF),
        rows=of((n_dp, 8, C), F32), tall=of((n_dp, 8, 128), F32), ext=of((n_dp, 8, 128), F32), weo=of((C, emb), BF))
    outputs.update({name: of((2, SL * taps, 128), BF) for name, taps in ITEMS})
    v = pltpu.VMEM
    maps2 = 2 * ROWS
    scratch = dict(
        xl=v((slots, ROWS, SL), BF), dyl=v((slots, ROWS, SL), BF),
        xp=v((CHAN, ROWS, 128), BF), dyp=v((CHAN, ROWS, 128), BF),
        xg=v((CHAN, ROWS, 128), BF), dyg=v((CHAN, ROWS, 128), BF),
        yp=v((CHAN, ROWS, 128), BF), mp=v((CHAN, ROWS, 128), BF),
        w1g=v((9, C, C), BF), w2g=v((9, C, C), BF), weg=v((C, emb), BF), wqg=v((4, C, C), BF),
        bd=v((C, C), BF), tl=v((8, 128), F32), pg=v((CHAN, 8, 128), F32), pa=v((8, C), F32), emb=v((16, C), F32),
        a1=v((TALL + 2 * GAP, 3 * C), BF), a2=v((TALL + 2 * GAP, 3 * C), BF), dd=v((TALL + 2 * GAP, 3 * C), BF),
        h=v((TALL, C), F32), xf=v((maps2, C), F32), n1=v((maps2, C), F32), n2=v((maps2, C), F32),
        n3=v((maps2, C), F32), dres=v((maps2, C), F32), big=v((maps2, C), F32), p=v((maps2, C), F32),
        e=v((8, C), F32), es=v((CHAN, 8, 128), F32), er=v((CHAN, 8, 128), F32), et=v((8, 128), F32),
        dm=v((CHAN, 8, C), F32), dl=v((8, C), F32), turn=v((2, ROWS, C), BF),
        dw1=v((9, C, C), BF), dw2=v((9, C, C), BF), dqo=v((4, C, C), BF))
    for name in ("a3", "q", "k", "v", "pb", "o", "g", "do", "dq", "dk", "dv"):
        scratch[name] = v((maps2, C), BF)
    for name, taps in ITEMS:
        span = SL * taps // (team // 2)
        scratch.update({
            name + "_rc": v((2, taps, SL, C), BF), name + "_sy": v((taps, SL, C), BF), name + "_ry": v((taps, SL, C), BF),
            name + "_sl": v((2, SL * taps, 128), BF), name + "_rr": v((team, span, 128), BF),
            name + "_pc": v((span, 128), BF), name + "_rt": v((teams, span, 128), BF)})
    n_remote = 64 + 3 * (n_dp - 1) + len(ITEMS) * (3 + 2 * (team - 1) + teams - 1)
    scratch.update(
        send=pltpu.SemaphoreType.DMA((n_remote,)), recv=pltpu.SemaphoreType.DMA((n_remote,)),
        own=pltpu.SemaphoreType.DMA((32,)))
    names = list(inputs) + list(outputs) + list(scratch)
    got = pl.pallas_call(
        functools.partial(mega, n_dp, names),
        out_shape=tuple(outputs.values()),
        in_specs=[where.get(name, anywhere) for name in inputs],
        out_specs=tuple(anywhere for _ in outputs),
        scratch_shapes=list(scratch.values()),
        compiler_params=pltpu.CompilerParams(collective_id=0, has_side_effects=True, vmem_limit_bytes=56 << 20),
        name="blocks",
    )(*inputs.values())
    got = dict(zip(outputs, got))
    ends = [got[name] for name in ("rows", "tall", "ext", "ga", "gb", "gc", "gd", "ge", "yo", "mo", "weo")] + [emb_table]
    flat = of((1, SL), F32)
    out = pl.pallas_call(
        functools.partial(finish, n_dp),
        out_shape=(of((slots, ROWS, SL), BF), of((slots, ROWS, SL), BF), of((steps, emb), F32), of((9, SL, C), F32),
                   of((9, SL, C), F32), of((SL, emb), F32), of((3, SL, C), F32), of((1, SL, C), F32)) + (flat,) * 6,
        in_specs=[vmem] * len(ends),
        out_specs=(vmem,) * 14,
        scratch_shapes=[v((C, 8 * n_dp), F32)],
        compiler_params=pltpu.CompilerParams(vmem_limit_bytes=48 << 20),
        name="finish",
    )(*ends)
    y, dm, dt, d1, d2, de, dq, do = out[:8]
    return (
        y.reshape(x_maps.shape), dm.reshape(x_maps.shape), dt,
        jnp.swapaxes(d1.reshape(3, 3, SL, C), 2, 3), jnp.swapaxes(d2.reshape(3, 3, SL, C), 2, 3),
        de.T, jnp.transpose(dq, (2, 0, 1)), do.reshape(SL, C).T) + tuple(e.reshape(SL) for e in out[8:])


def solution(mesh):
    weights = (P(None, None, None, "chan"), P(None, None, None, "chan"), P(None, "chan"), P(None, None, "chan"),
               P(None, "chan")) + (P("chan"),) * 6
    maps = P("dp", None, None, "chan")
    return jax.shard_map(
        functools.partial(per_device, n_dp=mesh.shape["dp"]), mesh=mesh,
        in_specs=(maps, P("dp"), P("dp"), P()) + weights + (maps,),
        out_specs=(maps, maps, P()) + weights, check_vma=False)
```

time: 1600 us -> 99.9 us (0.06); the launches traced: 1580 us -> 99.3 us
  waiting for transfers between devices: 519 us -> 0 us
  local copies, waits for them, and re-layouts: 432 us -> 10.5 us
  matrix products: 286 us -> 0 us
  blocking collectives: 277 us -> 0 us
  Pallas kernels: 0 us -> 86.7 us
  other arithmetic: 39.2 us -> 0.6 us
    psum x6 -> x0, waiting for transfers between devices: 338 us -> none  [the longest x4 127 us: score_total(): return lax.psum(values.astype(jnp.bfloat16), 'chan').astype(jnp.float32)]
    dot_general x284 -> x0, matrix products: 286 us -> none  [the longest x72 133 us: conv_backward(): jnp.einsum('nhwd,cd->nhwc', grad_out, weight[row, col], preferred_element...]
    all_gather x16 -> x0, blocking collectives: 255 us -> none  [widen(): return lax.all_gather(values, 'chan', axis=3, tiled=True)]
    while x776 -> x0, local copies, waits for them, and re-layouts: 189 us -> none
    while x36 -> x0, waiting for transfers between devices: 180 us -> none
    scatter-add x56 -> x0, local copies, waits for them, and re-layouts: 147 us -> none  [conv_backward(): dpad.at[:, row:row + side, col:col + side, :]]
    pallas_call x0 -> x2, Pallas kernels: none -> 86.7 us  [the longest x1 83.8 us: per_device(): pl.pallas_call(functools.partial(mega, n_dp, names), out_shape=tuple(outp...]
    all_gather x16 -> x0, local copies, waits for them, and re-layouts: 39 us -> none  [widen(): return lax.all_gather(values, 'chan', axis=3, tiled=True)]
  transfers between devices with their start and end apart: 22 -> 0, of which waited for: 18 -> 0; matrix products, arithmetic and copies ran while one was open for 9% -> 0% of each run, Pallas kernels for 0% -> 0%
where the time goes in v1:
time: 99.9 us; the launch traced here: 99.3 us
  Pallas kernels  86.7 us (87%)
  local copies, waits for them, and re-layouts  10.5 us (11%)
  between operations  1.42 us (1%)
    pallas_call x1, Pallas kernels, per_device(): pl.pallas_call(functools.partial(mega, n_dp, names), out_shape=tuple(outp...  83.8 us
    unnamed x24, local copies, waits for them, and re-layouts  9.74 us
    pallas_call x1, Pallas kernels, per_device(): pl.pallas_call(functools.partial(finish, n_dp), out_shape=(of((slots, ROW...  2.98 us

profile of v1, /device:TPU:0, one launch (start us, length us, event | category | flops | bytes accessed | tf_op | source)
XLA Modules:
  0.0 99.3 jit_solution(13146440726708678057)
XLA Ops:
  0.6 0.0 copy-start
  1.4 0.8 stack.27
  2.2 0.6 pad_convert_fusion.refs_10_
  2.8 83.8 %blocks.1 = (bf16[4,256,128]{2,1,0:T(8,128)(2,1)}, bf16[4,256,128]{2,1,0:T(8,128)(2,1)}, f32[8,8,256]{2,1,0:T(8,128)}, f32[8,8,128]{2,1,0:T(8,128)}, f32[8,8,128...) custom-call(bf16[8,256,64]{2,1,0:T(8,128)(2,1)} %bitcast.36, ...), custom_call_target="tpu_custom_call" | custom-call | tf_op jit(solution)/shard_map/blocks/pallas_call | solution.py:692
  86.5 0.0 copy-done
  86.5 0.0 copy-start.1
  86.5 1.0 copy-done.1
  87.5 0.0 copy-start.2
  87.5 0.9 copy-done.2
  88.4 0.0 copy-start.3
  88.4 0.9 copy-done.3
  89.4 0.0 copy-start.4
  89.4 0.9 copy-done.4
  90.3 0.0 copy-start.5
  90.3 0.9 copy-done.5
  91.2 0.0 copy-start.6
  91.3 0.9 copy-done.6
  92.1 0.0 copy-start.7
  92.1 0.9 copy-done.7
  93.0 0.0 copy-start.8
  93.0 0.9 copy-done.8
  93.9 0.0 copy-start.9
  93.9 0.8 copy-done.9
  94.8 0.0 copy-start.10
  94.8 0.8 copy-done.10
  95.5 0.0 copy-start.11
  95.5 0.8 copy-done.11
  96.3 3.0 %finish.1 = (bf16[8,256,64]{2,1,0:T(8,128)(2,1)}, bf16[8,256,64]{2,1,0:T(8,128)(2,1)}, f32[1000,512]{1,0:T(8,128)}, f32[9,64,256]{2,1,0:T(8,128)}, f32[9,64,256]...) custom-call(f32[8,8,256]{2,1,0:T(8,128)S(1)} %copy-done.9, ...), custom_call_target="tpu_custom_call" | custom-call | tf_op jit(solution)/shard_map/finish/pallas_call | solution.py:704
Async XLA Ops:
  0.6 85.9 %copy-start = (bf16[1000,512]{1,0:T(8,128)(2,1)S(1)}, bf16[1000,512]{1,0:T(8,128)(2,1)}, u32[]{:S(2)}) copy-start(bf16[1000,512]{1,0:T(8,128)(2,1)} %table.1) | copy-start | bytes 3072004
  86.5 1.0 copy-start.1
  87.5 0.9 copy-start.2
  88.4 0.9 copy-start.3
  89.4 0.9 copy-start.4
  90.3 0.9 copy-start.5
  91.2 0.9 copy-start.6
  92.1 0.9 copy-start.7
  93.0 0.9 copy-start.8
  93.9 0.8 copy-start.9
  94.8 0.8 copy-start.10
  95.5 0.8 copy-start.11

commit v2 on v1

v2 whole, which is shorter than its diff:
```python
import functools
from types import SimpleNamespace

import jax
import jax.numpy as jnp
from jax import lax
from jax.experimental import pallas as pl
from jax.experimental.pallas import tpu as pltpu
from jax.sharding import PartitionSpec as P

F32 = jnp.float32
BF = jnp.bfloat16
MESH = pl.DeviceIdType.MESH
EPS = 1e-06
GROUPS = 32
CHAN = 4
ROWS = 256
C = 256
SL = C // CHAN
GAP = 16
STEP = ROWS + GAP
TALL = 2 * ROWS + GAP
CH = 32
COUNT = ROWS * (C // GROUPS)


def dot(a, b):
    return jnp.dot(a, b, preferred_element_type=F32)


def dot_nt(a, b):
    return lax.dot_general(a, b, (((1,), (1,)), ((), ())), preferred_element_type=F32)


def sigmoid(u):
    return 0.5 * jnp.tanh(0.5 * u) + 0.5


def fold(v):
    return v.reshape(v.shape[0] // 8, 8, v.shape[1]).sum(axis=0)


def group_total(rows, bd):
    at = lax.broadcasted_iota(jnp.int32, (8, C), 0)
    stack = jnp.zeros((8, C), F32)
    for i, row in enumerate(rows):
        stack = jnp.where(at == i, row, stack)
    high = stack.astype(BF).astype(F32)
    rest = stack - high
    mid = rest.astype(BF).astype(F32)
    parts = jnp.concatenate([high, mid, rest - mid, jnp.zeros((8, C), F32)], axis=0)
    total = dot(parts.astype(BF), bd)
    total = total[0:8] + total[8:16] + total[16:24]
    return [total[i : i + 1] for i in range(len(rows))]


def chunk_at(i):
    return pl.multiple_of(i * CH, CH)


def passes(body, carry=None):
    carry = (0, 0) if carry is None else carry

    def step(i, held):
        return tuple(body(m, chunk_at(i), held[m]) for m in range(2))

    return lax.fori_loop(0, ROWS // CH, step, carry)


def zero_pair():
    return (jnp.zeros((8, C), F32), jnp.zeros((8, C), F32))


def col(v):
    return jnp.sum(v, axis=0, keepdims=True)


def write_shift(dst, m, at, value, forward):
    place = lax.broadcasted_iota(jnp.int32, (CH, C), 0) % 16
    before = jnp.where(place == 0, 0.0, pltpu.roll(value, 1, 0))
    after = jnp.where(place == 15, 0.0, pltpu.roll(value, CH - 1, 0))
    first, last = (before, after) if forward else (after, before)
    rows = pl.ds(pl.multiple_of(at + (GAP + m * STEP), 16), CH)
    dst[rows, 0:C] = first.astype(BF)
    dst[rows, C : 2 * C] = value.astype(BF)
    dst[rows, 2 * C : 3 * C] = last.astype(BF)


def norm_forward(load, n_ref, gain, shift, bd, emit):
    def sums(m, at, held):
        return held + fold(load(m, at))

    total = passes(sums, zero_pair())
    mean = group_total([col(t) for t in total], bd)
    mean = [v * (1.0 / COUNT) for v in mean]

    def squares(m, at, held):
        d = load(m, at) - mean[m]
        return held + fold(d * d)

    total = passes(squares, zero_pair())
    var = group_total([col(t) for t in total], bd)
    rstd = [lax.rsqrt(v * (1.0 / COUNT) + EPS) for v in var]

    def last(m, at, held):
        n = (load(m, at) - mean[m]) * rstd[m]
        n_ref[pl.ds(pl.multiple_of(at + m * ROWS, CH), CH), :] = n
        emit(m, at, n * gain + shift)
        return held

    passes(last)
    return rstd


def norm_back(d_ref, n_ref, gain, shift, rstd, bd, active, e_ref, e_at, emit):
    def rows(m, at):
        return pl.ds(pl.multiple_of(at + m * STEP, 16), CH)

    def first(m, at, held):
        d = d_ref[rows(m, at), :]
        n = n_ref[pl.ds(pl.multiple_of(at + m * ROWS, CH), CH), :]
        if active:
            u = n * gain + shift
            s = sigmoid(u)
            d = d * (s * (1.0 + u * (1.0 - s)))
            d_ref[rows(m, at), :] = d
        return (held[0] + fold(d), held[1] + fold(d * n))

    total = passes(first, (zero_pair(), zero_pair()))
    ones = [col(t[0]) for t in total]
    twos = [col(t[1]) for t in total]
    e_ref[e_at : e_at + 1, :] = twos[0] + twos[1]
    e_ref[e_at + 1 : e_at + 2, :] = ones[0] + ones[1]
    means = group_total([gain * v for v in ones + twos], bd)
    means = [v * (1.0 / COUNT) for v in means]

    def second(m, at, held):
        d = d_ref[rows(m, at), :]
        n = n_ref[pl.ds(pl.multiple_of(at + m * ROWS, CH), CH), :]
        return emit(m, at, rstd[m] * (d * gain - means[m] - n * means[2 + m]), held)

    return second


def unpack(low, high):
    lane = lax.broadcasted_iota(jnp.int32, low.shape, 1)
    first = jnp.where(lane < SL, low, pltpu.roll(high, SL, 1))
    second = jnp.where(lane < SL, pltpu.roll(low, SL, 1), high)
    return first, second


def conv_forward(a_ref, w_ref, h_ref, ready):
    for row in range(3):
        ready(row)
        total = None
        for c in range(3):
            part = dot_nt(a_ref[16 * row : 16 * row + TALL, C * c : C * c + C], w_ref[3 * row + c])
            total = part if total is None else total + part
        h_ref[...] = total if row == 0 else h_ref[...] + total


def conv_back(d_ref, w_ref, h_ref):
    for row in range(3):
        at = 16 * (2 - row)
        w = w_ref[3 * row : 3 * row + 3].reshape(3 * C, C)
        part = dot(d_ref[at : at + TALL, :], w)
        h_ref[...] = part if row == 0 else h_ref[...] + part


def conv_weight(a_ref, turned, dw_ref, row):
    for c in range(3):
        total = None
        for m in range(2):
            at = 16 * row + STEP * m
            part = dot(turned[m], a_ref[at : at + ROWS, C * c : C * c + C])
            total = part if total is None else total + part
        dw_ref[3 * row + c] = total.astype(BF)


class Links:
    def __init__(self, send, recv, own):
        self.send, self.recv, self.own = send, recv, own
        self.used, self.local = 0, 0
        self.sent = []

    def remote(self, src, dst, device):
        at = self.used
        self.used += 1
        copy = pltpu.make_async_remote_copy(
            src_ref=src, dst_ref=dst, send_sem=self.send.at[at], recv_sem=self.recv.at[at],
            device_id=device, device_id_type=MESH)
        copy.start()
        self.sent.append(copy)
        return copy

    def here(self, src, dst):
        copy = pltpu.make_async_copy(src, dst, self.own.at[self.local])
        self.local += 1
        copy.start()
        return copy

    def close(self):
        for copy in self.sent:
            copy.wait_send()


def block_sizes(n_dp):
    team = min(8, n_dp)
    return team, n_dp // team


def aligned(start, size):
    return pl.ds(pl.multiple_of(start, size), size)


class Reduction:
    def __init__(self, at, links, grad, out, work):
        self.at, self.links, self.grad, self.out, self.w = at, links, grad, out, work
        self.taps = grad.shape[0]
        self.span = SL * self.taps // (at.team // 2)

    def core(self):
        at = self.at
        self.waits = [
            self.links.remote(self.grad.at[:, aligned(SL * (2 * y + 1 - at.core), SL), :], self.w.rc.at[y], at.sibling)
            for y in range(2)]

    def cross(self):
        at, w = self.at, self.w
        for copy in self.waits:
            copy.wait_recv()
        for y in range(2):
            for t in range(self.taps):
                mine = self.grad[t, aligned(SL * (2 * y + at.core), SL), :].astype(F32)
                total = (mine + w.rc[y, t].astype(F32)).astype(BF)
                for half in range(2):
                    w.sx[y, half, SL * t : SL * t + SL, :] = total[:, 128 * half : 128 * half + 128]
        y, b = at.y, at.bit
        self.waits = [
            self.links.remote(w.sx.at[1 - y, b], w.ry.at[0], at.across),
            self.links.remote(w.sx.at[1 - y, 1 - b], w.ry.at[2], at.oblique),
            self.links.remote(w.sx.at[y, 1 - b], w.ry.at[1], at.beside)]

    def piece(self, ref, p):
        return ref.at[aligned(self.span * p, self.span), :]

    def scatter(self):
        at, w = self.at, self.w
        for copy in self.waits:
            copy.wait_recv()
        total = w.sx[at.y, at.bit].astype(F32)
        for i in range(3):
            total = total + w.ry[i].astype(F32)
        w.hs[...] = total.astype(BF)
        self.waits = []
        for s in range(1, at.team // 2):
            p = (at.rank // 2 + s) % (at.team // 2)
            self.waits.append(self.links.remote(self.piece(w.hs, p), w.rz.at[s], at.mate(2 * p + at.bit)))

    def spread(self):
        at, w = self.at, self.w
        for copy in self.waits:
            copy.wait_recv()
        place = at.rank // 2
        total = self.piece(w.hs, place)[...].astype(F32)
        for s in range(1, at.team // 2):
            total = total + w.rz[s].astype(F32)
        w.pc[...] = total.astype(BF)
        if at.teams > 1:
            copies = [self.links.here(w.pc, w.rt.at[at.lead])]
            for s in range(1, at.teams):
                other = (at.lead + s) % at.teams
                copies.append(self.links.remote(w.pc, w.rt.at[at.lead], at.device(other * at.team + at.rank)))
            copies[0].wait()
            for copy in copies[1:]:
                copy.wait_recv()
                copy.wait_send()
                self.links.sent = [c for c in self.links.sent if c is not copy]
            total = w.rt[0].astype(F32)
            for s in range(1, at.teams):
                total = total + w.rt[s].astype(F32)
            w.pc[...] = total.astype(BF)
        target = self.piece(self.out.at[at.bit], place)
        self.own = self.links.here(w.pc, target)
        self.waits = []
        for s in range(1, at.team):
            self.waits.append(self.links.remote(w.pc, target, at.mate((at.rank + s) % at.team)))

    def finish(self):
        self.own.wait()
        for copy in self.waits:
            copy.wait_recv()


ITEMS = (("ga", 4), ("gb0", 3), ("gb1", 3), ("gb2", 3), ("gc0", 3), ("gc1", 3), ("gc2", 3))
GAINS = ("gain1", "shift1", "gain2", "shift2", "gain3", "shift3")


def mega(n_dp, names, *refs):
    r = SimpleNamespace(**dict(zip(names, refs)))
    team, teams = block_sizes(n_dp)
    dp, chan = lax.axis_index("dp"), lax.axis_index("chan")
    core, y, bit = chan % 2, chan // 2, dp % 2
    sibling, across, corner = (dp, 2 * y + 1 - core), (dp, 2 * (1 - y) + core), (dp, 2 * (1 - y) + 1 - core)
    beside, oblique = (dp + 1 - 2 * bit, chan), (dp + 1 - 2 * bit, 2 * (1 - y) + core)
    quads = (sibling, across, corner)
    rank, lead = dp % team, dp // team
    at = SimpleNamespace(
        core=core, y=y, bit=bit, sibling=sibling, across=across, beside=beside, oblique=oblique,
        team=team, teams=teams, rank=rank, lead=lead,
        mate=lambda p: (lead * team + p, chan), device=lambda p: (p, chan))
    links = Links(r.send, r.recv, r.own)

    def others():
        return [(lax.rem(dp + s, n_dp), chan) for s in range(1, n_dp)]

    barrier = pltpu.get_barrier_semaphore()
    for device in quads + (oblique,) + tuple(others()):
        pl.semaphore_signal(barrier, inc=1, device_id=device, device_id_type=MESH)
    load_x, load_dy = links.here(r.x, r.xl), links.here(r.dy, r.dyl)
    load_par = [links.here(getattr(r, name), r.pin.at[i]) for i, name in enumerate(GAINS)]
    load_ts, load_cnt, load_table = links.here(r.ts, r.tss), links.here(r.cnt, r.cns), links.here(r.table, r.tab)
    mine = aligned(SL * chan, SL)
    fill = [
        links.here(r.w1, r.w1g.at[:, mine, :]), links.here(r.w2, r.w2g.at[:, mine, :]),
        links.here(r.we, r.weg.at[:, mine, :]),
        links.here(r.wq, r.wqg.at[0:3, mine, :]), links.here(r.wo, r.wqg.at[3:4, mine, :])]

    def pack(src, dst):
        for k in range(CHAN):
            for half in range(2):
                rows = slice(128 * half, 128 * half + 128)
                both = jnp.concatenate([src[2 * k, rows, :].astype(F32), src[2 * k + 1, rows, :].astype(F32)], axis=1)
                dst[k, rows, :] = both.astype(BF)

    load_x.wait()
    pack(r.xl, r.xp)
    for copy in load_par:
        copy.wait()
    r.par[...] = jnp.zeros((8, 128), F32)
    for i in range(len(GAINS)):
        r.par[i : i + 1, 0:SL] = r.pin[i].astype(F32)
    pl.semaphore_wait(barrier, CHAN + n_dp - 1)

    part = 32 * bit
    far = SL * (2 * (1 - y) + core)

    class Share:
        def __init__(self, w, g):
            self.w, self.g, self.moves = w, g, {}
            self.moves["across"] = links.remote(
                w.at[:, aligned(part, 32), :], g.at[:, aligned(SL * chan + part, 32), :], across)

        def own(self):
            self.moves["own"] = links.remote(self.w, self.g.at[:, mine, :], sibling)

        def hand(self, name, rows, device):
            piece = self.g.at[:, aligned(rows, 32), :]
            self.moves[name] = links.remote(piece, piece, device)

        def relay(self):
            self.moves["across"].wait_recv()
            self.hand("beside", far + part, beside)
            self.hand("first", far + part, sibling)

        def relay_again(self):
            self.moves["beside"].wait_recv()
            self.hand("second", far + 32 - part, sibling)

        def landed(self):
            for name in ("own", "first", "second"):
                self.moves[name].wait_recv()

    def rows3(ref, row):
        return ref.at[3 * row : 3 * row + 3]

    one = [Share(rows3(r.w1, row), rows3(r.w1g, row)) for row in range(3)]
    moves_x = [links.remote(r.xp.at[d[1]], r.xg.at[chan], d) for d in quads]
    moves_par = [links.remote(r.par, r.pg.at[chan], d) for d in quads]
    mix = Share(r.we, r.weg)
    two = [Share(rows3(r.w2, row), rows3(r.w2g, row)) for row in range(3)]
    out = [Share(r.wq, r.wqg.at[0:3]), Share(r.wo, r.wqg.at[3:4])]
    for share in one + [mix] + two + out:
        share.own()

    at_row = lax.broadcasted_iota(jnp.int32, (C, C), 0) // (C // GROUPS)
    at_col = lax.broadcasted_iota(jnp.int32, (C, C), 1) // (C // GROUPS)
    r.bd[...] = jnp.where(at_row == at_col, 1.0, 0.0).astype(BF)
    for ref in (r.a1, r.a2, r.dd):
        for gap in range(3):
            ref[gap * STEP : gap * STEP + GAP, :] = jnp.zeros((GAP, 3 * C), BF)
    r.xg[chan] = r.xp[chan]
    r.pg[chan] = r.par[...]
    load_ts.wait()
    row8 = lax.broadcasted_iota(jnp.int32, (8, 128), 0)
    times = jnp.zeros((8, 128), F32)
    for i in range(8):
        times = jnp.where(row8 == i, r.tss[i].astype(F32), times)
    r.tl[...] = times
    r.ta[dp] = times
    moves_t = [links.remote(r.tl, r.ta.at[dp], d) for d in others()]
    load_dy.wait()
    pack(r.dyl, r.dyp)
    r.dyg[chan] = r.dyp[chan]
    steps = r.table.shape[0]
    load_table.wait()

    def embeddings(times):
        count = times.shape[0]
        wide = jnp.broadcast_to(times[:, 0:1], (count, steps))
        hot = jnp.where(wide == lax.broadcasted_iota(jnp.int32, (count, steps), 1).astype(F32), 1.0, 0.0)
        temb = dot(hot.astype(BF), r.tab[...])
        s = sigmoid(temb)
        return temb, s, (temb * s).astype(BF)

    _, _, tsil = embeddings(jnp.concatenate([times, times], axis=0))
    for share in one:
        share.relay()

    bd = r.bd[...]
    for copy in moves_x + moves_par:
        copy.wait_recv()
    for b in range(2):
        first, _ = unpack(r.pg[2 * b], r.pg[2 * b + 1])
        r.pa[:, 128 * b : 128 * b + 128] = first
    par = r.pa[...]
    gain1, shift1, gain2, shift2, gain3, shift3 = [par[i : i + 1] for i in range(6)]

    def spread_out(src, at, dst, scale=None):
        for b in range(2):
            pair = unpack(src[2 * b, pl.ds(at, CH), :].astype(F32), src[2 * b + 1, pl.ds(at, CH), :].astype(F32))
            for m in range(2):
                value = pair[m] if scale is None else pair[m] * scale[m]
                dst[pl.ds(pl.multiple_of(at + m * ROWS, CH), CH), 128 * b : 128 * b + 128] = value.astype(dst.dtype)

    def open_x(i, held):
        spread_out(r.xg, chunk_at(i), r.xf)
        return held

    lax.fori_loop(0, ROWS // CH, open_x, 0)

    def rows_of(m, at):
        return pl.ds(pl.multiple_of(at + m * ROWS, CH), CH)

    def rows_gap(m, at):
        return pl.ds(pl.multiple_of(at + m * STEP, 16), CH)

    def to_shift(dst):
        def emit(m, at, u):
            write_shift(dst, m, at, u * sigmoid(u), True)
        return emit

    rstd1 = norm_forward(lambda m, at: r.xf[rows_of(m, at), :], r.n1, gain1, shift1, bd, to_shift(r.a1))
    for share in one:
        share.relay_again()
    moves_dy = [links.remote(r.dyp.at[d[1]], r.dyg.at[chan], d) for d in quads]
    mix.relay()
    two[0].relay()
    for copy in fill:
        copy.wait()
    conv_forward(r.a1, r.w1g, r.h, lambda row: one[row].landed())
    mix.relay_again()
    two[0].relay_again()
    for share in two[1:] + out:
        share.relay()
    mix.landed()
    r.emb[0:16, :] = dot_nt(tsil, r.weg[0])
    emb = [r.emb[pl.ds(2 * chan + m, 1), :] for m in range(2)]

    rstd2 = norm_forward(lambda m, at: r.h[rows_gap(m, at), :] + emb[m], r.n2, gain2, shift2, bd, to_shift(r.a2))
    for share in two[1:] + out:
        share.relay_again()
    conv_forward(r.a2, r.w2g, r.h, lambda row: two[row].landed())

    def load_resid(m, at):
        return r.xf[rows_of(m, at), :] + r.h[rows_gap(m, at), :]

    def to_a3(m, at, u):
        r.a3[rows_of(m, at), :] = u.astype(BF)

    rstd3 = norm_forward(load_resid, r.n3, gain3, shift3, bd, to_a3)
    for share in out:
        share.landed()
    for j, ref in enumerate((r.q, r.k, r.v)):
        ref[...] = dot_nt(r.a3[...], r.wqg[j]).astype(BF)
    load_cnt.wait()
    count = r.cns[0]
    live = [jnp.where(2 * chan + m < count, 1.0, 0.0).astype(F32) for m in range(2)]
    scale = C ** (-0.5)
    half = [slice(0, ROWS), slice(ROWS, 2 * ROWS)]
    for m in range(2):
        s = dot_nt(r.q[half[m], :], r.k[half[m], :]) * scale
        p = jnp.exp(s - jnp.max(s, axis=1, keepdims=True))
        p = p * (1.0 / jnp.sum(p, axis=1, keepdims=True))
        r.p[half[m], :] = p
        r.pb[half[m], :] = p.astype(BF)
        r.o[half[m], :] = dot(p.astype(BF), r.v[half[m], :]).astype(BF)
    r.big[...] = dot_nt(r.o[...], r.wqg[3])

    def pack_out(at, pair, dst):
        for b in range(2):
            even, odd = unpack(*(v[:, 128 * b : 128 * b + 128] for v in pair))
            dst[2 * b, pl.ds(at, CH), :] = even.astype(BF)
            dst[2 * b + 1, pl.ds(at, CH), :] = odd.astype(BF)

    def to_y(i, held):
        at = chunk_at(i)
        pack_out(at, [(load_resid(m, at) + r.big[rows_of(m, at), :]) * live[m] for m in range(2)], r.yp)
        return held

    lax.fori_loop(0, ROWS // CH, to_y, 0)
    own_y = links.here(r.yp.at[chan], r.yo.at[chan])
    moves_y = [links.remote(r.yp.at[d[1]], r.yo.at[chan], d) for d in quads]

    for copy in moves_dy:
        copy.wait_recv()

    def open_dy(i, held):
        spread_out(r.dyg, chunk_at(i), r.g, live)
        return held

    lax.fori_loop(0, ROWS // CH, open_dy, 0)
    for m in range(2):
        r.turn[m] = r.g[half[m], :].T
    r.dqo[3] = (dot(r.turn[0], r.o[half[0], :]) + dot(r.turn[1], r.o[half[1], :])).astype(BF)
    r.do[...] = dot(r.g[...], r.wqg[3]).astype(BF)
    for m in range(2):
        dp_m = dot_nt(r.do[half[m], :], r.v[half[m], :])
        p = r.p[half[m], :]
        ds = (p * (dp_m - jnp.sum(p * dp_m, axis=1, keepdims=True)) * scale).astype(BF)
        r.dv[half[m], :] = dot(r.pb[half[m], :].T, r.do[half[m], :]).astype(BF)
        r.dq[half[m], :] = dot(ds, r.k[half[m], :]).astype(BF)
        r.dk[half[m], :] = dot(ds.T, r.q[half[m], :]).astype(BF)
    for j, ref in enumerate((r.dq, r.dk, r.dv)):
        parts = [dot(ref[half[m], :].T, r.a3[half[m], :]) for m in range(2)]
        r.dqo[j] = (parts[0] + parts[1]).astype(BF)

    def reduction(name, grad):
        work = SimpleNamespace(**{k: getattr(r, name + "_" + k) for k in ("rc", "sx", "ry", "hs", "rz", "pc", "rt")})
        item = Reduction(at, links, grad, getattr(r, name), work)
        item.core()
        return item

    attn = reduction("ga", r.dqo)
    for m in range(2):
        total = None
        for j, ref in enumerate((r.dq, r.dk, r.dv)):
            part_j = dot(ref[half[m], :], r.wqg[j])
            total = part_j if total is None else total + part_j
        r.h[m * STEP : m * STEP + ROWS, :] = total
    attn.cross()

    def to_dres(m, at, dv, held):
        value = r.g[rows_of(m, at), :].astype(F32) + dv
        r.dres[rows_of(m, at), :] = value
        write_shift(r.dd, m, at, value, False)
        return held

    passes(norm_back(r.h, r.n3, gain3, shift3, rstd3, bd, False, r.e, 4, to_dres))

    def turn():
        for m in range(2):
            r.turn[m] = r.dd[GAP + STEP * m : GAP + STEP * m + ROWS, C : 2 * C].T

    turn()
    second = []
    for row in range(3):
        conv_weight(r.a2, r.turn, r.dw2, row)
        second.append(reduction(f"gb{row}", rows3(r.dw2, row)))
    second[0].cross()
    conv_back(r.dd, r.w2g, r.h)
    second[1].cross()
    second[2].cross()
    attn.scatter()

    def to_dh1(m, at, dv, held):
        write_shift(r.dd, m, at, dv, False)
        return held + fold(dv)

    demb = passes(norm_back(r.h, r.n2, gain2, shift2, rstd2, bd, True, r.e, 2, to_dh1), zero_pair())
    for m in range(2):
        r.dm[chan, m : m + 1, :] = col(demb[m]).astype(BF).astype(F32)
    moves_dm = [links.remote(r.dm.at[chan], r.dm.at[chan], d) for d in quads]
    turn()
    first = []
    for row in range(3):
        conv_weight(r.a1, r.turn, r.dw1, row)
        first.append(reduction(f"gc{row}", rows3(r.dw1, row)))
        if row > 0:
            first[row - 1].cross()
    second[0].scatter()
    conv_back(r.dd, r.w1g, r.h)
    first[2].cross()
    attn.spread()
    second[1].scatter()
    second[2].scatter()
    for copy in moves_dm:
        copy.wait_recv()
    for j in range(CHAN):
        r.dl[2 * j : 2 * j + 2, :] = r.dm[j, 0:2, :]
    r.ra[dp] = r.dl[...]
    moves_rows = [links.remote(r.dl, r.ra.at[dp], d) for d in others()]
    back1 = norm_back(r.h, r.n1, gain1, shift1, rstd1, bd, True, r.e, 0,
                      lambda m, at, dv, held: r.dres[rows_of(m, at), :] + dv)

    def to_maps(i, held):
        at = chunk_at(i)
        pack_out(at, [back1(m, at, 0) for m in range(2)], r.mp)
        return held

    lax.fori_loop(0, ROWS // CH, to_maps, 0)
    own_mp = links.here(r.mp.at[chan], r.mo.at[chan])
    moves_mp = [links.remote(r.mp.at[d[1]], r.mo.at[chan], d) for d in quads]
    for b in range(2):
        block = r.e[:, 128 * b : 128 * b + 128]
        r.es[2 * b] = block
        r.es[2 * b + 1] = pltpu.roll(block, SL, 1)
    r.er[chan] = r.es[chan]
    moves_e = [links.remote(r.es.at[d[1]], r.er.at[chan], d) for d in quads]
    second[0].spread()
    first[0].scatter()
    second[1].spread()
    second[2].spread()
    first[1].scatter()
    first[2].scatter()
    for copy in moves_e:
        copy.wait_recv()
    r.et[...] = r.er[0] + r.er[1] + r.er[2] + r.er[3]
    own_e = links.here(r.et, r.ext.at[dp])
    moves_ext = [links.remote(r.et, r.ext.at[dp], d) for d in others()]
    first[0].spread()
    for copy in moves_t + moves_rows:
        copy.wait_recv()
    maps = 8 * n_dp
    temb, s, tsil = embeddings(r.ta[...].reshape(maps, 128))
    rows = r.ra[...].reshape(maps, C)
    r.rt[...] = rows.T
    r.dew[...] = dot(r.rt[mine, :].astype(BF), tsil)
    dtemb = dot(rows.astype(BF), r.weg[0]) * (s * (1.0 + temb * (1.0 - s)))
    high = dtemb.astype(BF)
    r.bw[0:maps, :] = high
    r.bw[maps:, :] = (dtemb - high.astype(F32)).astype(BF)
    ends = [links.here(r.dew, r.de), links.here(r.bw, r.both), links.here(r.ta, r.tall)]
    first[1].spread()
    first[2].spread()
    for item in [attn] + second + first:
        item.finish()
    for copy in [own_y, own_mp, own_e] + ends:
        copy.wait()
    for copy in moves_y + moves_mp + moves_ext:
        copy.wait_recv()
    links.close()


def finish(n_dp, names, *refs):
    r = SimpleNamespace(**dict(zip(names, refs)))
    maps = 8 * n_dp
    steps = r.dt.shape[0]
    links = Links(None, None, r.own)
    items = [name for name, _ in ITEMS]
    load = {name: links.here(getattr(r, name), getattr(r, name + "_v"))
            for name in ["tall", "both", "yo", "mo"] + items + ["ext"]}
    stores = [links.here(r.de, r.de_out)]

    def out(src, dst):
        stores.append(links.here(src, dst))

    load["tall"].wait()
    load["both"].wait()
    lanes = r.tall_v[...].reshape(maps, 128).T[0:1, :]
    lanes = jnp.concatenate([lanes, lanes], axis=1)
    for start in range(0, steps, 256):
        size = min(256, steps - start)
        ids = lax.broadcasted_iota(jnp.int32, (size, 2 * maps), 0).astype(F32) + float(start)
        hot = jnp.where(ids == lanes, 1.0, 0.0).astype(BF)
        r.dt_v[start : start + size, :] = dot(hot, r.both_v[...])
        out(r.dt_v.at[start : start + size], r.dt.at[start : start + size])

    def unpack_maps(name, dst, dst_v):
        load[name].wait()
        src = getattr(r, name + "_v")
        for j in range(CHAN):
            block = src[j].astype(F32)
            dst_v[2 * j] = block[:, 0:SL].astype(BF)
            dst_v[2 * j + 1] = pltpu.roll(block, SL, 1)[:, 0:SL].astype(BF)
        out(dst_v, dst)

    def whole(name, dst_v, base, taps):
        src = getattr(r, name + "_v")
        for i, t in enumerate(taps):
            for half in range(2):
                dst_v[base + i, :, 128 * half : 128 * half + 128] = src[half, SL * t : SL * t + SL, :].astype(F32)

    unpack_maps("yo", r.y, r.y_v)
    unpack_maps("mo", r.dm, r.dm_v)
    load["ga"].wait()
    whole("ga", r.dq_v, 0, range(3))
    out(r.dq_v, r.dq)
    whole("ga", r.do_v, 0, [3])
    out(r.do_v, r.do)
    for kind, dst_v, dst in (("gb", r.d2_v, r.d2), ("gc", r.d1_v, r.d1)):
        for row in range(3):
            load[f"{kind}{row}"].wait()
            whole(f"{kind}{row}", dst_v, 3 * row, range(3))
            out(dst_v.at[3 * row : 3 * row + 3], dst.at[3 * row : 3 * row + 3])
    load["ext"].wait()
    total = r.ext_v[0]
    for i in range(1, n_dp):
        total = total + r.ext_v[i]
    for i in range(6):
        r.gains_v[i] = total[i : i + 1, 0:SL]
        out(r.gains_v.at[i], getattr(r, f"e{i}"))
    for copy in stores:
        copy.wait()


def per_device(x_maps, timesteps, counts, emb_table, w_first, w_second, w_embed, w_qkv, w_out, gain_one, shift_one,
               gain_two, shift_two, gain_three, shift_three, cotangent, *, n_dp):
    team, teams = block_sizes(n_dp)
    slots, side, _, _ = x_maps.shape
    emb = w_embed.shape[0]
    steps = emb_table.shape[0]
    inputs = dict(
        x=x_maps.reshape(slots, side * side, SL), dy=cotangent.reshape(slots, side * side, SL),
        ts=timesteps, cnt=counts, table=emb_table,
        w1=jnp.swapaxes(w_first, 2, 3).reshape(9, SL, C), w2=jnp.swapaxes(w_second, 2, 3).reshape(9, SL, C),
        we=w_embed.T[None], wq=jnp.transpose(w_qkv, (1, 2, 0)), wo=w_out.T[None])
    gains = (gain_one, shift_one, gain_two, shift_two, gain_three, shift_three)
    inputs.update({name: v.reshape(1, SL) for name, v in zip(GAINS, gains)})
    anywhere = pl.BlockSpec(memory_space=pl.ANY)

    def of(shape, dtype):
        return jax.ShapeDtypeStruct(shape, dtype)

    maps = 8 * n_dp
    middle = dict(
        yo=of((CHAN, ROWS, 128), BF), mo=of((CHAN, ROWS, 128), BF), tall=of((n_dp, 8, 128), F32),
        ext=of((n_dp, 8, 128), F32), both=of((2 * maps, emb), BF), de=of((SL, emb), F32))
    middle.update({name: of((2, SL * taps, 128), BF) for name, taps in ITEMS})
    v = pltpu.VMEM
    maps2 = 2 * ROWS
    scratch = dict(
        xl=v((slots, ROWS, SL), BF), dyl=v((slots, ROWS, SL), BF), pin=v((len(GAINS), 1, SL), BF),
        tss=pltpu.SMEM((slots,), jnp.int32), cns=pltpu.SMEM((1,), jnp.int32), tab=v((steps, emb), BF),
        xp=v((CHAN, ROWS, 128), BF), dyp=v((CHAN, ROWS, 128), BF),
        xg=v((CHAN, ROWS, 128), BF), dyg=v((CHAN, ROWS, 128), BF),
        yp=v((CHAN, ROWS, 128), BF), mp=v((CHAN, ROWS, 128), BF),
        w1g=v((9, C, C), BF), w2g=v((9, C, C), BF), weg=v((1, C, emb), BF), wqg=v((4, C, C), BF),
        bd=v((C, C), BF), tl=v((8, 128), F32), ta=v((n_dp, 8, 128), F32), par=v((8, 128), F32),
        pg=v((CHAN, 8, 128), F32), pa=v((8, C), F32), emb=v((16, C), F32),
        a1=v((TALL + 2 * GAP, 3 * C), BF), a2=v((TALL + 2 * GAP, 3 * C), BF), dd=v((TALL + 2 * GAP, 3 * C), BF),
        h=v((TALL, C), F32), xf=v((maps2, C), F32), n1=v((maps2, C), F32), n2=v((maps2, C), F32),
        n3=v((maps2, C), F32), dres=v((maps2, C), F32), big=v((maps2, C), F32), p=v((maps2, C), F32),
        e=v((8, C), F32), es=v((CHAN, 8, 128), F32), er=v((CHAN, 8, 128), F32), et=v((8, 128), F32),
        dm=v((CHAN, 8, C), F32), dl=v((8, C), F32), ra=v((n_dp, 8, C), F32), rt=v((C, maps), F32),
        dew=v((SL, emb), F32), bw=v((2 * maps, emb), BF), turn=v((2, ROWS, C), BF),
        dw1=v((9, C, C), BF), dw2=v((9, C, C), BF), dqo=v((4, C, C), BF))
    for name in ("a3", "q", "k", "v", "pb", "o", "g", "do", "dq", "dk", "dv"):
        scratch[name] = v((maps2, C), BF)
    for name, taps in ITEMS:
        rows, span = SL * taps, SL * taps // (team // 2)
        scratch.update({
            name + "_rc": v((2, taps, SL, C), BF), name + "_sx": v((2, 2, rows, 128), BF),
            name + "_ry": v((3, rows, 128), BF), name + "_hs": v((rows, 128), BF),
            name + "_rz": v((team // 2, span, 128), BF), name + "_pc": v((span, 128), BF),
            name + "_rt": v((teams, span, 128), BF)})
    n_remote = 72 + 3 * (n_dp - 1) + len(ITEMS) * (5 + team // 2 + team + teams)
    scratch.update(
        send=pltpu.SemaphoreType.DMA((n_remote,)), recv=pltpu.SemaphoreType.DMA((n_remote,)),
        own=pltpu.SemaphoreType.DMA((48,)))
    got = pl.pallas_call(
        functools.partial(mega, n_dp, list(inputs) + list(middle) + list(scratch)),
        out_shape=tuple(middle.values()),
        in_specs=[anywhere] * len(inputs),
        out_specs=(anywhere,) * len(middle),
        scratch_shapes=list(scratch.values()),
        compiler_params=pltpu.CompilerParams(collective_id=0, has_side_effects=True, vmem_limit_bytes=60 << 20),
        name="blocks",
    )(*inputs.values())
    results = dict(
        y=of((slots, ROWS, SL), BF), dm=of((slots, ROWS, SL), BF), dt=of((steps, emb), F32), d1=of((9, SL, C), F32),
        d2=of((9, SL, C), F32), de_out=of((SL, emb), F32), dq=of((3, SL, C), F32), do=of((1, SL, C), F32))
    results.update({f"e{i}": of((1, SL), F32) for i in range(6)})
    scratch = {name + "_v": v(o.shape, o.dtype) for name, o in middle.items() if name != "de"}
    scratch.update({name + "_v": v(o.shape, o.dtype) for name, o in results.items() if name[0] != "e"})
    scratch.update(gains_v=v((6, 1, SL), F32), own=pltpu.SemaphoreType.DMA((48,)))
    got = pl.pallas_call(
        functools.partial(finish, n_dp, list(middle) + list(results) + list(scratch)),
        out_shape=tuple(results.values()),
        in_specs=[anywhere] * len(middle),
        out_specs=(anywhere,) * len(results),
        scratch_shapes=list(scratch.values()),
        compiler_params=pltpu.CompilerParams(vmem_limit_bytes=60 << 20),
        name="finish",
    )(*got)
    got = dict(zip(results, got))
    return (
        got["y"].reshape(x_maps.shape), got["dm"].reshape(x_maps.shape), got["dt"],
        jnp.swapaxes(got["d1"].reshape(3, 3, SL, C), 2, 3), jnp.swapaxes(got["d2"].reshape(3, 3, SL, C), 2, 3),
        got["de_out"].T, jnp.transpose(got["dq"], (2, 0, 1)), got["do"].reshape(SL, C).T,
    ) + tuple(got[f"e{i}"].reshape(SL) for i in range(6))


def solution(mesh):
    weights = (P(None, None, None, "chan"), P(None, None, None, "chan"), P(None, "chan"), P(None, None, "chan"),
               P(None, "chan")) + (P("chan"),) * 6
    maps = P("dp", None, None, "chan")
    return jax.shard_map(
        functools.partial(per_device, n_dp=mesh.shape["dp"]), mesh=mesh,
        in_specs=(maps, P("dp"), P("dp"), P()) + weights + (maps,),
        out_specs=(maps, maps, P()) + weights, check_vma=False)
```

time: 99.9 us -> 78.7 us (0.79)
  local copies, waits for them, and re-layouts: 10.5 us -> 0 us
  Pallas kernels: 86.7 us -> 77.2 us
    unnamed x24 -> x0, local copies, waits for them, and re-layouts: 9.74 us -> none
    pallas_call x2, Pallas kernels: 86.7 us -> 77.2 us  [the longest x1 71.6 us: per_device(): pl.pallas_call(functools.partial(mega, n_dp, list(inputs) + list(middle)...]
where the time goes in v2:
time: 78.7 us; the launch traced here: 78.5 us
  Pallas kernels  77.2 us (98%)
  between operations  1.3 us (2%)
    pallas_call x1, Pallas kernels, per_device(): pl.pallas_call(functools.partial(mega, n_dp, list(inputs) + list(middle)...  71.6 us
    pallas_call x1, Pallas kernels, per_device(): pl.pallas_call(functools.partial(finish, n_dp, list(middle) + list(result...  5.56 us

profile of v2, /device:TPU:0, one launch (start us, length us, event | category | flops | bytes accessed | tf_op | source)
XLA Modules:
  0.0 78.5 jit_solution(3576154686474551436)
XLA Ops:
  1.3 71.6 %blocks.1 = (bf16[4,256,128]{2,1,0:T(8,128)(2,1)}, bf16[4,256,128]{2,1,0:T(8,128)(2,1)}, f32[8,8,128]{2,1,0:T(8,128)}, f32[8,8,128]{2,1,0:T(8,128)}, bf16[128,51...) custom-call(bf16[8,256,64]{2,1,0:T(8,128)(2,1)} %bitcast.40, ...), custom_call_target="tpu_custom_call" | custom-call | tf_op jit(solution)/shard_map/blocks/pallas_call | solution.py:771
  72.9 5.6 %finish.1 = (bf16[8,256,64]{2,1,0:T(8,128)(2,1)}, bf16[8,256,64]{2,1,0:T(8,128)(2,1)}, f32[1000,512]{1,0:T(8,128)}, f32[9,64,256]{2,1,0:T(8,128)}, f32[9,64,256]...) custom-call(bf16[4,256,128]{2,1,0:T(8,128)(2,1)} %get-tuple-element., ...), custom_call_target="tpu_custom_call" | custom-call | tf_op jit(solution)/shard_map/finish/pallas_call | solution.py:787

commit v3 on v2

--- a/solution.py
+++ b/solution.py
@@ -86,7 +86,7 @@
     dst[rows, 2 * C : 3 * C] = last.astype(BF)
 
 
-def norm_forward(load, n_ref, gain, shift, bd, emit):
+def norm_forward(load, n_ref, gain, shift, bd, emit, midway=None):
     def sums(m, at, held):
         return held + fold(load(m, at))
 
@@ -101,6 +101,8 @@
     total = passes(squares, zero_pair())
     var = group_total([col(t) for t in total], bd)
     rstd = [lax.rsqrt(v * (1.0 / COUNT) + EPS) for v in var]
+    if midway is not None:
+        midway()
 
     def last(m, at, held):
         n = (load(m, at) - mean[m]) * rstd[m]
@@ -149,22 +151,24 @@
     return first, second
 
 
-def conv_forward(a_ref, w_ref, h_ref, ready):
-    for row in range(3):
+def conv_forward(a_ref, w_ref, h_ref, ready, order):
+    for row in order:
         ready(row)
         total = None
         for c in range(3):
             part = dot_nt(a_ref[16 * row : 16 * row + TALL, C * c : C * c + C], w_ref[3 * row + c])
             total = part if total is None else total + part
-        h_ref[...] = total if row == 0 else h_ref[...] + total
-
-
-def conv_back(d_ref, w_ref, h_ref):
+        h_ref[...] = total if row == order[0] else h_ref[...] + total
+
+
+def conv_back(d_ref, w_ref, h_ref, between=None):
     for row in range(3):
         at = 16 * (2 - row)
         w = w_ref[3 * row : 3 * row + 3].reshape(3 * C, C)
         part = dot(d_ref[at : at + TALL, :], w)
         h_ref[...] = part if row == 0 else h_ref[...] + part
+        if between is not None:
+            between(row)
 
 
 def conv_weight(a_ref, turned, dw_ref, row):
@@ -177,21 +181,48 @@
         dw_ref[3 * row + c] = total.astype(BF)
 
 
+class Group:
+    def __init__(self, links):
+        self.links, self.at, self.rows = links, links.used, 0
+        links.used += 1
+
+    def remote(self, src, dst, device):
+        links, rows = self.links, rows_in(src)
+        if links.sending + rows > links.idle.shape[0]:
+            links.ended.append((links.senders, links.sending))
+            links.senders, links.sending = links.senders + 1, 0
+        links.sending += rows
+        self.rows += rows
+        pltpu.make_async_remote_copy(
+            src_ref=src, dst_ref=dst, send_sem=links.send.at[links.senders], recv_sem=links.recv.at[self.at],
+            device_id=device, device_id_type=MESH).start()
+
+    def wait(self):
+        self.links.wait_rows(self.links.recv.at[self.at], self.rows)
+
+
+def rows_in(ref):
+    size = ref.dtype.itemsize
+    for n in ref.shape:
+        size *= n
+    return size // 256
+
+
 class Links:
-    def __init__(self, send, recv, own):
-        self.send, self.recv, self.own = send, recv, own
-        self.used, self.local = 0, 0
-        self.sent = []
-
-    def remote(self, src, dst, device):
-        at = self.used
-        self.used += 1
-        copy = pltpu.make_async_remote_copy(
-            src_ref=src, dst_ref=dst, send_sem=self.send.at[at], recv_sem=self.recv.at[at],
-            device_id=device, device_id_type=MESH)
-        copy.start()
-        self.sent.append(copy)
-        return copy
+    def __init__(self, send, recv, own, idle):
+        self.send, self.recv, self.own, self.idle = send, recv, own, idle
+        self.used, self.local, self.senders, self.sending = 0, 0, 0, 0
+        self.ended = []
+
+    def wait_rows(self, semaphore, rows):
+        view = self.idle.at[0:rows]
+        pltpu.make_async_copy(view, view, semaphore).wait()
+
+    def group(self, copies=()):
+        group = Group(self)
+        for src, dst, device in copies:
+            group.remote(src, dst, device)
+        return group
 
     def here(self, src, dst):
         copy = pltpu.make_async_copy(src, dst, self.own.at[self.local])
@@ -200,8 +231,8 @@
         return copy
 
     def close(self):
-        for copy in self.sent:
-            copy.wait_send()
+        for at, rows in self.ended + [(self.senders, self.sending)]:
+            self.wait_rows(self.send.at[at], rows)
 
 
 def block_sizes(n_dp):
@@ -213,86 +244,215 @@
     return pl.ds(pl.multiple_of(start, size), size)
 
 
+def reduction_scratch(taps, order, spread, team, teams):
+    rows, span = SL * taps, SL * taps // (team // 2)
+    left = rows if spread is None else span
+    shapes = dict(rc=(2, taps, SL, C), s0=(2, 2, rows, 128), pc=(1, 1, left, 128), rt=(teams, 1, 1, left, 128))
+    if spread is None:
+        shapes.update({f"c{i}": (1, 1, rows, 128) for i in range(3)})
+    size = dict(y=2, x=2, z=team // 2)
+    for k, axes in enumerate(order):
+        peers = 1
+        for axis in axes:
+            peers *= size[axis]
+            size[axis] = 1
+        shape = (size["y"], size["x"], size["z"] * span, 128)
+        shapes[f"r{k}"] = (max(peers - 1, 1),) + shape
+        shapes[f"s{k + 1}"] = shape
+    buffers = {name: pltpu.VMEM(shape, BF) for name, shape in shapes.items()}
+    if spread is None:
+        buffers.update(cs=pltpu.SemaphoreType.DMA((3,)), cr=pltpu.SemaphoreType.DMA((3,)))
+    return buffers
+
+
 class Reduction:
-    def __init__(self, at, links, grad, out, work):
+    def __init__(self, at, links, grad, out, work, order, spread):
         self.at, self.links, self.grad, self.out, self.w = at, links, grad, out, work
+        self.order, self.spread = order, spread
         self.taps = grad.shape[0]
         self.span = SL * self.taps // (at.team // 2)
-
-    def core(self):
-        at = self.at
-        self.waits = [
-            self.links.remote(self.grad.at[:, aligned(SL * (2 * y + 1 - at.core), SL), :], self.w.rc.at[y], at.sibling)
-            for y in range(2)]
-
-    def cross(self):
+        self.size = dict(y=2, x=2, z=at.team // 2)
+        self.stage = -1
+        self.whole = dict(y=True, x=True, z=True)
+        w = self.w
+        self.group = links.group([
+            (grad.at[:, aligned(SL * (2 * y + 1 - at.core), SL), :], w.rc.at[y], at.sibling) for y in range(2)])
+
+    def view(self, ref, place):
+        parts = []
+        for axis in "yx":
+            parts.append(pl.ds(place[axis], 1) if axis in place and self.whole[axis] else slice(None))
+        if "z" in place and self.whole["z"]:
+            parts.append(aligned(self.span * place["z"], self.span))
+        else:
+            parts.append(slice(None))
+        return ref.at[tuple(parts)]
+
+    def peers(self, axes):
+        steps = [{}]
+        for axis in axes:
+            steps = [{**step, axis: s} for step in steps for s in range(self.size[axis])]
+        for step in steps[1:]:
+            yield {axis: (self.at.place[axis] + s) % self.size[axis] for axis, s in step.items()}
+
+    def send(self):
+        axes = self.order[self.stage]
+        current, arriving = getattr(self.w, f"s{self.stage}"), getattr(self.w, f"r{self.stage}")
+        self.group = self.links.group([
+            (self.view(current, place), arriving.at[slot], self.at.peer(place))
+            for slot, place in enumerate(self.peers(axes))])
+
+    def collect(self):
         at, w = self.at, self.w
-        for copy in self.waits:
-            copy.wait_recv()
-        for y in range(2):
-            for t in range(self.taps):
-                mine = self.grad[t, aligned(SL * (2 * y + at.core), SL), :].astype(F32)
-                total = (mine + w.rc[y, t].astype(F32)).astype(BF)
-                for half in range(2):
-                    w.sx[y, half, SL * t : SL * t + SL, :] = total[:, 128 * half : 128 * half + 128]
-        y, b = at.y, at.bit
-        self.waits = [
-            self.links.remote(w.sx.at[1 - y, b], w.ry.at[0], at.across),
-            self.links.remote(w.sx.at[1 - y, 1 - b], w.ry.at[2], at.oblique),
-            self.links.remote(w.sx.at[y, 1 - b], w.ry.at[1], at.beside)]
-
-    def piece(self, ref, p):
-        return ref.at[aligned(self.span * p, self.span), :]
-
-    def scatter(self):
+        if self.group.rows:
+            self.group.wait()
+        if self.stage < 0:
+            for y in range(2):
+                for t in range(self.taps):
+                    mine = self.grad[t, aligned(SL * (2 * y + at.core), SL), :].astype(F32)
+                    total = (mine + w.rc[y, t].astype(F32)).astype(BF)
+                    for half in range(2):
+                        w.s0[y, half, SL * t : SL * t + SL, :] = total[:, 128 * half : 128 * half + 128]
+            return
+        axes = self.order[self.stage]
+        current, arriving = getattr(w, f"s{self.stage}"), getattr(w, f"r{self.stage}")
+        total = self.view(current, {axis: at.place[axis] for axis in axes})[...].astype(F32)
+        for slot in range(len(list(self.peers(axes)))):
+            total = total + arriving[slot].astype(F32)
+        getattr(w, f"s{self.stage + 1}")[...] = total.astype(BF)
+        for axis in axes:
+            self.whole[axis] = False
+
+    def across_teams(self, piece):
         at, w = self.at, self.w
-        for copy in self.waits:
-            copy.wait_recv()
-        total = w.sx[at.y, at.bit].astype(F32)
-        for i in range(3):
-            total = total + w.ry[i].astype(F32)
-        w.hs[...] = total.astype(BF)
-        self.waits = []
-        for s in range(1, at.team // 2):
-            p = (at.rank // 2 + s) % (at.team // 2)
-            self.waits.append(self.links.remote(self.piece(w.hs, p), w.rz.at[s], at.mate(2 * p + at.bit)))
-
-    def spread(self):
-        at, w = self.at, self.w
-        for copy in self.waits:
-            copy.wait_recv()
-        place = at.rank // 2
-        total = self.piece(w.hs, place)[...].astype(F32)
-        for s in range(1, at.team // 2):
-            total = total + w.rz[s].astype(F32)
+        own = self.links.here(piece, w.rt.at[at.lead])
+        group = self.links.group([
+            (piece, w.rt.at[at.lead], at.device((at.lead + s) % at.teams * at.team + at.rank))
+            for s in range(1, at.teams)])
+        own.wait()
+        group.wait()
+        total = w.rt[0].astype(F32)
+        for s in range(1, at.teams):
+            total = total + w.rt[s].astype(F32)
         w.pc[...] = total.astype(BF)
-        if at.teams > 1:
-            copies = [self.links.here(w.pc, w.rt.at[at.lead])]
-            for s in range(1, at.teams):
-                other = (at.lead + s) % at.teams
-                copies.append(self.links.remote(w.pc, w.rt.at[at.lead], at.device(other * at.team + at.rank)))
-            copies[0].wait()
-            for copy in copies[1:]:
-                copy.wait_recv()
-                copy.wait_send()
-                self.links.sent = [c for c in self.links.sent if c is not copy]
-            total = w.rt[0].astype(F32)
-            for s in range(1, at.teams):
-                total = total + w.rt[s].astype(F32)
-            w.pc[...] = total.astype(BF)
-        target = self.piece(self.out.at[at.bit], place)
-        self.own = self.links.here(w.pc, target)
-        self.waits = []
-        for s in range(1, at.team):
-            self.waits.append(self.links.remote(w.pc, target, at.mate((at.rank + s) % at.team)))
+        return w.pc
+
+    def region(self, axes):
+        place = self.at.place
+        rows = slice(None) if "z" in axes else aligned(self.span * place["z"], self.span)
+        return self.out.at[:, pl.ds(place["x"], 1), rows]
+
+    def advance(self):
+        last = len(self.order)
+        if self.stage < last:
+            self.collect()
+        self.stage += 1
+        if self.stage < last:
+            self.send()
+            return
+        axes = self.spread[self.stage - last]
+        if self.stage == last:
+            source = getattr(self.w, f"s{last}")
+            if self.at.teams > 1:
+                source = self.across_teams(source)
+            target = self.region("")
+            self.own = self.links.here(source, target)
+        else:
+            if self.stage == last + 1:
+                self.own.wait()
+            if self.group.rows:
+                self.group.wait()
+            source = target = self.region("".join(self.spread[: self.stage - last]))
+        self.group = self.links.group([(source, target, self.at.peer(place)) for place in self.peers(axes)])
 
     def finish(self):
-        self.own.wait()
-        for copy in self.waits:
-            copy.wait_recv()
-
-
-ITEMS = (("ga", 4), ("gb0", 3), ("gb1", 3), ("gb2", 3), ("gc0", 3), ("gc1", 3), ("gc2", 3))
+        if self.spread is None or len(self.spread) == 1:
+            self.own.wait()
+        if self.group.rows:
+            self.group.wait()
+
+
+class Chain(Reduction):
+    def copy(self, step, src, dst, z):
+        w = self.w
+        return pltpu.make_async_remote_copy(
+            src_ref=src, dst_ref=dst, send_sem=w.cs.at[step], recv_sem=w.cr.at[step],
+            device_id=self.at.peer(dict(z=z)), device_id_type=MESH)
+
+    def prepare(self):
+        z, w = self.at.place["z"], self.w
+        total = getattr(w, f"s{len(self.order)}")
+        count = self.size["z"]
+        self.end = (z == 0) | (z == count - 1)
+        self.inner = jnp.logical_not(self.end)
+        middle = jnp.where(z < 2, 1, 2)
+        self.inward = self.copy(0, total, w.c0, middle)
+        self.swap = self.copy(1, w.c1, w.c2, count - 1 - z)
+        self.outward = self.copy(2, w.pc, w.pc, jnp.where(z < 2, 0, 3))
+        return total
+
+    def advance(self):
+        w, last = self.w, len(self.order)
+        if self.stage < last - 1:
+            self.collect()
+            self.stage += 1
+            self.send()
+            return
+        long, alone = self.size["z"] == 4, self.size["z"] == 1
+        if self.stage == last - 1:
+            self.collect()
+            total = self.prepare()
+            if long:
+                pl.when(self.end)(self.inward.start)
+            else:
+                w.c1[...] = total[...]
+        elif self.stage == last:
+            if long:
+                @pl.when(self.inner)
+                def _():
+                    self.inward.wait_recv()
+                    total = getattr(w, f"s{last}")[...].astype(F32) + w.c0[...].astype(F32)
+                    w.c1[...] = total.astype(BF)
+                    self.swap.start()
+            elif not alone:
+                self.swap.start()
+        elif self.stage == last + 1:
+            def join():
+                self.swap.wait_recv()
+                w.pc[...] = (w.c1[...].astype(F32) + w.c2[...].astype(F32)).astype(BF)
+
+            if long:
+                @pl.when(self.inner)
+                def _():
+                    join()
+                    self.outward.start()
+            elif alone:
+                w.pc[...] = w.c1[...]
+            else:
+                join()
+        else:
+            if long:
+                pl.when(self.end)(self.outward.wait_recv)
+                pl.when(self.end)(self.inward.wait_send)
+
+                @pl.when(self.inner)
+                def _():
+                    self.swap.wait_send()
+                    self.outward.wait_send()
+            elif not alone:
+                self.swap.wait_send()
+            source = self.across_teams(w.pc) if self.at.teams > 1 else w.pc
+            target = self.region("z")
+            self.own = self.links.here(source, target)
+            self.group = self.links.group([(source, target, self.at.peer(place)) for place in self.peers("x")])
+        self.stage += 1
+
+
+YX, XY, YXZ, XYZ = ("y", "x"), ("x", "y"), ("y", "x", "z"), ("x", "y", "z")
+STEPS, ONCE = ("z", "x"), ("zx",)
+ITEMS = {
+    "ga": (4, YX, None), "gb0": (3, XY, None), "gb1": (3, YX, None), "gb2": (3, YX, None),
+    "gc0": (3, YXZ, STEPS), "gc1": (3, XYZ, STEPS), "gc2": (3, YXZ, ONCE)}
 GAINS = ("gain1", "shift1", "gain2", "shift2", "gain3", "shift3")
 
 
@@ -305,11 +465,15 @@
     beside, oblique = (dp + 1 - 2 * bit, chan), (dp + 1 - 2 * bit, 2 * (1 - y) + core)
     quads = (sibling, across, corner)
     rank, lead = dp % team, dp // team
-    at = SimpleNamespace(
-        core=core, y=y, bit=bit, sibling=sibling, across=across, beside=beside, oblique=oblique,
-        team=team, teams=teams, rank=rank, lead=lead,
-        mate=lambda p: (lead * team + p, chan), device=lambda p: (p, chan))
-    links = Links(r.send, r.recv, r.own)
+    own_place = dict(y=y, x=bit, z=rank // 2)
+
+    def peer(place):
+        place = {**own_place, **place}
+        return (lead * team + 2 * place["z"] + place["x"], 2 * place["y"] + core)
+
+    at = SimpleNamespace(core=core, sibling=sibling, team=team, teams=teams, rank=rank, lead=lead, place=own_place,
+                         peer=peer, device=lambda p: (p, chan))
+    links = Links(r.send, r.recv, r.own, r.idle)
 
     def others():
         return [(lax.rem(dp + s, n_dp), chan) for s in range(1, n_dp)]
@@ -317,9 +481,9 @@
     barrier = pltpu.get_barrier_semaphore()
     for device in quads + (oblique,) + tuple(others()):
         pl.semaphore_signal(barrier, inc=1, device_id=device, device_id_type=MESH)
-    load_x, load_dy = links.here(r.x, r.xl), links.here(r.dy, r.dyl)
+    load_x, load_ts, load_table = links.here(r.x, r.xl), links.here(r.ts, r.tss), links.here(r.table, r.tab)
     load_par = [links.here(getattr(r, name), r.pin.at[i]) for i, name in enumerate(GAINS)]
-    load_ts, load_cnt, load_table = links.here(r.ts, r.tss), links.here(r.cnt, r.cns), links.here(r.table, r.tab)
+    load_we, load_dy, load_cnt = links.here(r.we, r.wel), links.here(r.dy, r.dyl), links.here(r.cnt, r.cns)
     mine = aligned(SL * chan, SL)
     fill = [
         links.here(r.w1, r.w1g.at[:, mine, :]), links.here(r.w2, r.w2g.at[:, mine, :]),
@@ -346,43 +510,77 @@
     far = SL * (2 * (1 - y) + core)
 
     class Share:
-        def __init__(self, w, g):
-            self.w, self.g, self.moves = w, g, {}
-            self.moves["across"] = links.remote(
-                w.at[:, aligned(part, 32), :], g.at[:, aligned(SL * chan + part, 32), :], across)
+        def __init__(self, w, g, half):
+            self.w, self.g, self.half = w, g, half
+            self.from_sibling = links.group()
+            rows = (part, 32) if half else (0, SL)
+            self.over = links.group([
+                (w.at[:, aligned(*rows), :], g.at[:, aligned(SL * chan + rows[0], rows[1]), :], across)])
 
         def own(self):
-            self.moves["own"] = links.remote(self.w, self.g.at[:, mine, :], sibling)
-
-        def hand(self, name, rows, device):
-            piece = self.g.at[:, aligned(rows, 32), :]
-            self.moves[name] = links.remote(piece, piece, device)
+            self.from_sibling.remote(self.w, self.g.at[:, mine, :], sibling)
 
         def relay(self):
-            self.moves["across"].wait_recv()
-            self.hand("beside", far + part, beside)
-            self.hand("first", far + part, sibling)
+            self.over.wait()
+            if self.half:
+                piece = self.g.at[:, aligned(far + part, 32), :]
+                self.around = links.group([(piece, piece, beside)])
+            else:
+                piece = self.g.at[:, aligned(far, SL), :]
+            self.from_sibling.remote(piece, piece, sibling)
 
         def relay_again(self):
-            self.moves["beside"].wait_recv()
-            self.hand("second", far + 32 - part, sibling)
+            self.around.wait()
+            piece = self.g.at[:, aligned(far + 32 - part, 32), :]
+            self.from_sibling.remote(piece, piece, sibling)
 
         def landed(self):
-            for name in ("own", "first", "second"):
-                self.moves[name].wait_recv()
+            self.from_sibling.wait()
 
     def rows3(ref, row):
         return ref.at[3 * row : 3 * row + 3]
 
-    one = [Share(rows3(r.w1, row), rows3(r.w1g, row)) for row in range(3)]
-    moves_x = [links.remote(r.xp.at[d[1]], r.xg.at[chan], d) for d in quads]
-    moves_par = [links.remote(r.par, r.pg.at[chan], d) for d in quads]
-    mix = Share(r.we, r.weg)
-    two = [Share(rows3(r.w2, row), rows3(r.w2g, row)) for row in range(3)]
-    out = [Share(r.wq, r.wqg.at[0:3]), Share(r.wo, r.wqg.at[3:4])]
-    for share in one + [mix] + two + out:
+    one = [Share(rows3(r.w1, row), rows3(r.w1g, row), True) for row in range(3)]
+    for share in one:
         share.own()
-
+    moves_x = links.group(
+        [(r.xp.at[d[1]], r.xg.at[chan], d) for d in quads] + [(r.par, r.pg.at[chan], d) for d in quads])
+
+    load_ts.wait()
+    row8 = lax.broadcasted_iota(jnp.int32, (8, 128), 0)
+    times = jnp.zeros((8, 128), F32)
+    for i in range(8):
+        times = jnp.where(row8 == i, r.tss[i].astype(F32), times)
+    r.tl[...] = times
+    r.ta[dp] = times
+    steps = r.table.shape[0]
+    load_table.wait()
+
+    def embeddings(times):
+        count = times.shape[0]
+        wide = jnp.broadcast_to(times[:, 0:1], (count, steps))
+        hot = jnp.where(wide == lax.broadcasted_iota(jnp.int32, (count, steps), 1).astype(F32), 1.0, 0.0)
+        temb = dot(hot.astype(BF), r.tab[...])
+        s = sigmoid(temb)
+        return temb, s, (temb * s).astype(BF)
+
+    _, _, tsil = embeddings(jnp.concatenate([times, times], axis=0))
+    load_we.wait()
+    r.el[...] = jnp.zeros((8, 128), F32)
+    r.el[:, 0:SL] = dot_nt(tsil, r.wel[0])[0:8]
+    r.eg[chan] = r.el[...]
+    moves_emb = links.group([(r.el, r.eg.at[chan], d) for d in quads])
+    two = [Share(rows3(r.w2, row), rows3(r.w2g, row), row < 2) for row in range(3)]
+    out = [Share(r.wq, r.wqg.at[0:3], False), Share(r.wo, r.wqg.at[3:4], False)]
+    for share in two + out:
+        share.own()
+    load_dy.wait()
+    pack(r.dyl, r.dyp)
+    moves_late = links.group([(r.tl, r.ta.at[dp], d) for d in others()])
+    r.dyg[chan] = r.dyp[chan]
+    moves_dy = links.group([(r.dyp.at[d[1]], r.dyg.at[chan], d) for d in quads])
+    mix = Share(r.we, r.weg, False)
+    mix.own()
     at_row = lax.broadcasted_iota(jnp.int32, (C, C), 0) // (C // GROUPS)
     at_col = lax.broadcasted_iota(jnp.int32, (C, C), 1) // (C // GROUPS)
     r.bd[...] = jnp.where(at_row == at_col, 1.0, 0.0).astype(BF)
@@ -391,35 +589,13 @@
             ref[gap * STEP : gap * STEP + GAP, :] = jnp.zeros((GAP, 3 * C), BF)
     r.xg[chan] = r.xp[chan]
     r.pg[chan] = r.par[...]
-    load_ts.wait()
-    row8 = lax.broadcasted_iota(jnp.int32, (8, 128), 0)
-    times = jnp.zeros((8, 128), F32)
-    for i in range(8):
-        times = jnp.where(row8 == i, r.tss[i].astype(F32), times)
-    r.tl[...] = times
-    r.ta[dp] = times
-    moves_t = [links.remote(r.tl, r.ta.at[dp], d) for d in others()]
-    load_dy.wait()
-    pack(r.dyl, r.dyp)
-    r.dyg[chan] = r.dyp[chan]
-    steps = r.table.shape[0]
-    load_table.wait()
-
-    def embeddings(times):
-        count = times.shape[0]
-        wide = jnp.broadcast_to(times[:, 0:1], (count, steps))
-        hot = jnp.where(wide == lax.broadcasted_iota(jnp.int32, (count, steps), 1).astype(F32), 1.0, 0.0)
-        temb = dot(hot.astype(BF), r.tab[...])
-        s = sigmoid(temb)
-        return temb, s, (temb * s).astype(BF)
-
-    _, _, tsil = embeddings(jnp.concatenate([times, times], axis=0))
     for share in one:
         share.relay()
+    one[0].relay_again()
+    one[1].relay_again()
 
     bd = r.bd[...]
-    for copy in moves_x + moves_par:
-        copy.wait_recv()
+    moves_x.wait()
     for b in range(2):
         first, _ = unpack(r.pg[2 * b], r.pg[2 * b + 1])
         r.pa[:, 128 * b : 128 * b + 128] = first
@@ -450,27 +626,36 @@
             write_shift(dst, m, at, u * sigmoid(u), True)
         return emit
 
-    rstd1 = norm_forward(lambda m, at: r.xf[rows_of(m, at), :], r.n1, gain1, shift1, bd, to_shift(r.a1))
-    for share in one:
-        share.relay_again()
-    moves_dy = [links.remote(r.dyp.at[d[1]], r.dyg.at[chan], d) for d in quads]
-    mix.relay()
-    two[0].relay()
+    rstd1 = norm_forward(lambda m, at: r.xf[rows_of(m, at), :], r.n1, gain1, shift1, bd, to_shift(r.a1),
+                         one[2].relay_again)
     for copy in fill:
         copy.wait()
-    conv_forward(r.a1, r.w1g, r.h, lambda row: one[row].landed())
-    mix.relay_again()
+
+    def ready_one(row):
+        if row == 2:
+            two[0].relay()
+        one[row].landed()
+
+    conv_forward(r.a1, r.w1g, r.h, ready_one, (0, 1, 2))
+    two[1].relay()
+    moves_emb.wait()
+    for b in range(2):
+        first, _ = unpack(r.eg[2 * b], r.eg[2 * b + 1])
+        r.emb[:, 128 * b : 128 * b + 128] = first
+    emb = [r.emb[pl.ds(2 * chan + m, 1), :] for m in range(2)]
+    rstd2 = norm_forward(lambda m, at: r.h[rows_gap(m, at), :] + emb[m], r.n2, gain2, shift2, bd, to_shift(r.a2))
+    two[2].relay()
     two[0].relay_again()
-    for share in two[1:] + out:
-        share.relay()
-    mix.landed()
-    r.emb[0:16, :] = dot_nt(tsil, r.weg[0])
-    emb = [r.emb[pl.ds(2 * chan + m, 1), :] for m in range(2)]
-
-    rstd2 = norm_forward(lambda m, at: r.h[rows_gap(m, at), :] + emb[m], r.n2, gain2, shift2, bd, to_shift(r.a2))
-    for share in two[1:] + out:
-        share.relay_again()
-    conv_forward(r.a2, r.w2g, r.h, lambda row: two[row].landed())
+
+    def ready_two(row):
+        if row == 0:
+            two[1].relay_again()
+        if row == 1:
+            for share in out:
+                share.relay()
+        two[row].landed()
+
+    conv_forward(r.a2, r.w2g, r.h, ready_two, (2, 0, 1))
 
     def load_resid(m, at):
         return r.xf[rows_of(m, at), :] + r.h[rows_gap(m, at), :]
@@ -479,10 +664,10 @@
         r.a3[rows_of(m, at), :] = u.astype(BF)
 
     rstd3 = norm_forward(load_resid, r.n3, gain3, shift3, bd, to_a3)
-    for share in out:
-        share.landed()
+    out[0].landed()
     for j, ref in enumerate((r.q, r.k, r.v)):
         ref[...] = dot_nt(r.a3[...], r.wqg[j]).astype(BF)
+    mix.relay()
     load_cnt.wait()
     count = r.cns[0]
     live = [jnp.where(2 * chan + m < count, 1.0, 0.0).astype(F32) for m in range(2)]
@@ -495,6 +680,7 @@
         r.p[half[m], :] = p
         r.pb[half[m], :] = p.astype(BF)
         r.o[half[m], :] = dot(p.astype(BF), r.v[half[m], :]).astype(BF)
+    out[1].landed()
     r.big[...] = dot_nt(r.o[...], r.wqg[3])
 
     def pack_out(at, pair, dst):
@@ -510,10 +696,9 @@
 
     lax.fori_loop(0, ROWS // CH, to_y, 0)
     own_y = links.here(r.yp.at[chan], r.yo.at[chan])
-    moves_y = [links.remote(r.yp.at[d[1]], r.yo.at[chan], d) for d in quads]
-
-    for copy in moves_dy:
-        copy.wait_recv()
+    moves_out = links.group([(r.yp.at[d[1]], r.yo.at[chan], d) for d in quads])
+
+    moves_dy.wait()
 
     def open_dy(i, held):
         spread_out(r.dyg, chunk_at(i), r.g, live)
@@ -536,19 +721,19 @@
         r.dqo[j] = (parts[0] + parts[1]).astype(BF)
 
     def reduction(name, grad):
-        work = SimpleNamespace(**{k: getattr(r, name + "_" + k) for k in ("rc", "sx", "ry", "hs", "rz", "pc", "rt")})
-        item = Reduction(at, links, grad, getattr(r, name), work)
-        item.core()
-        return item
-
-    attn = reduction("ga", r.dqo)
+        _, order, spread = ITEMS[name]
+        work = SimpleNamespace(**{k[len(name) + 1 :]: getattr(r, k) for k in names if k.startswith(name + "_")})
+        kind = Chain if spread is None else Reduction
+        return kind(at, links, grad, getattr(r, name), work, order, spread)
+
+    ga = reduction("ga", r.dqo)
     for m in range(2):
         total = None
         for j, ref in enumerate((r.dq, r.dk, r.dv)):
             part_j = dot(ref[half[m], :], r.wqg[j])
             total = part_j if total is None else total + part_j
         r.h[m * STEP : m * STEP + ROWS, :] = total
-    attn.cross()
+    ga.advance()
 
     def to_dres(m, at, dv, held):
         value = r.g[rows_of(m, at), :].astype(F32) + dv
@@ -563,15 +748,18 @@
             r.turn[m] = r.dd[GAP + STEP * m : GAP + STEP * m + ROWS, C : 2 * C].T
 
     turn()
-    second = []
+    gb = []
     for row in range(3):
         conv_weight(r.a2, r.turn, r.dw2, row)
-        second.append(reduction(f"gb{row}", rows3(r.dw2, row)))
-    second[0].cross()
-    conv_back(r.dd, r.w2g, r.h)
-    second[1].cross()
-    second[2].cross()
-    attn.scatter()
+        gb.append(reduction(f"gb{row}", rows3(r.dw2, row)))
+    def between(row):
+        if row == 0:
+            gb[0].advance()
+            gb[1].advance()
+        if row == 1:
+            gb[2].advance()
+
+    conv_back(r.dd, r.w2g, r.h, between)
 
     def to_dh1(m, at, dv, held):
         write_shift(r.dd, m, at, dv, False)
@@ -580,26 +768,20 @@
     demb = passes(norm_back(r.h, r.n2, gain2, shift2, rstd2, bd, True, r.e, 2, to_dh1), zero_pair())
     for m in range(2):
         r.dm[chan, m : m + 1, :] = col(demb[m]).astype(BF).astype(F32)
-    moves_dm = [links.remote(r.dm.at[chan], r.dm.at[chan], d) for d in quads]
+    moves_dm = links.group([(r.dm.at[chan], r.dm.at[chan], d) for d in quads])
     turn()
-    first = []
+    gc = []
     for row in range(3):
         conv_weight(r.a1, r.turn, r.dw1, row)
-        first.append(reduction(f"gc{row}", rows3(r.dw1, row)))
-        if row > 0:
-            first[row - 1].cross()
-    second[0].scatter()
+        gc.append(reduction(f"gc{row}", rows3(r.dw1, row)))
+        if row == 1:
+            gc[0].advance()
+            ga.advance()
+    for item in (gb[0], gc[1], gb[1], gc[2]):
+        item.advance()
     conv_back(r.dd, r.w1g, r.h)
-    first[2].cross()
-    attn.spread()
-    second[1].scatter()
-    second[2].scatter()
-    for copy in moves_dm:
-        copy.wait_recv()
-    for j in range(CHAN):
-        r.dl[2 * j : 2 * j + 2, :] = r.dm[j, 0:2, :]
-    r.ra[dp] = r.dl[...]
-    moves_rows = [links.remote(r.dl, r.ra.at[dp], d) for d in others()]
+    for item in (ga, gb[2]):
+        item.advance()
     back1 = norm_back(r.h, r.n1, gain1, shift1, rstd1, bd, True, r.e, 0,
                       lambda m, at, dv, held: r.dres[rows_of(m, at), :] + dv)
 
@@ -610,27 +792,31 @@
 
     lax.fori_loop(0, ROWS // CH, to_maps, 0)
     own_mp = links.here(r.mp.at[chan], r.mo.at[chan])
-    moves_mp = [links.remote(r.mp.at[d[1]], r.mo.at[chan], d) for d in quads]
+    for d in quads:
+        moves_out.remote(r.mp.at[d[1]], r.mo.at[chan], d)
+    moves_dm.wait()
+    for j in range(CHAN):
+        r.dl[2 * j : 2 * j + 2, :] = r.dm[j, 0:2, :]
+    r.ra[dp] = r.dl[...]
+    for d in others():
+        moves_late.remote(r.dl, r.ra.at[dp], d)
     for b in range(2):
         block = r.e[:, 128 * b : 128 * b + 128]
         r.es[2 * b] = block
         r.es[2 * b + 1] = pltpu.roll(block, SL, 1)
     r.er[chan] = r.es[chan]
-    moves_e = [links.remote(r.es.at[d[1]], r.er.at[chan], d) for d in quads]
-    second[0].spread()
-    first[0].scatter()
-    second[1].spread()
-    second[2].spread()
-    first[1].scatter()
-    first[2].scatter()
-    for copy in moves_e:
-        copy.wait_recv()
+    moves_e = links.group([(r.es.at[d[1]], r.er.at[chan], d) for d in quads])
+    for item in (gb[1], gc[0], gc[1], gb[0], gb[2], ga, gb[1], gc[2], gc[0], gc[1], gb[0], gb[2]):
+        item.advance()
+    moves_e.wait()
     r.et[...] = r.er[0] + r.er[1] + r.er[2] + r.er[3]
     own_e = links.here(r.et, r.ext.at[dp])
-    moves_ext = [links.remote(r.et, r.ext.at[dp], d) for d in others()]
-    first[0].spread()
-    for copy in moves_t + moves_rows:
-        copy.wait_recv()
+    for d in others():
+        moves_out.remote(r.et, r.ext.at[dp], d)
+    for item in (ga, gb[1], gc[2]):
+        item.advance()
+    mix.landed()
+    moves_late.wait()
     maps = 8 * n_dp
     temb, s, tsil = embeddings(r.ta[...].reshape(maps, 128))
     rows = r.ra[...].reshape(maps, C)
@@ -641,14 +827,13 @@
     r.bw[0:maps, :] = high
     r.bw[maps:, :] = (dtemb - high.astype(F32)).astype(BF)
     ends = [links.here(r.dew, r.de), links.here(r.bw, r.both), links.here(r.ta, r.tall)]
-    first[1].spread()
-    first[2].spread()
-    for item in [attn] + second + first:
+    for item in (gc[0], gb[0], gb[2], gc[1], gb[1], ga, gc[2], gb[0], gb[2], gc[0], gc[1]):
+        item.advance()
+    for item in [ga] + gb + gc:
         item.finish()
     for copy in [own_y, own_mp, own_e] + ends:
         copy.wait()
-    for copy in moves_y + moves_mp + moves_ext:
-        copy.wait_recv()
+    moves_out.wait()
     links.close()
 
 
@@ -656,8 +841,8 @@
     r = SimpleNamespace(**dict(zip(names, refs)))
     maps = 8 * n_dp
     steps = r.dt.shape[0]
-    links = Links(None, None, r.own)
-    items = [name for name, _ in ITEMS]
+    links = Links(None, None, r.own, None)
+    items = list(ITEMS)
     load = {name: links.here(getattr(r, name), getattr(r, name + "_v"))
             for name in ["tall", "both", "yo", "mo"] + items + ["ext"]}
     stores = [links.here(r.de, r.de_out)]
@@ -689,7 +874,7 @@
         src = getattr(r, name + "_v")
         for i, t in enumerate(taps):
             for half in range(2):
-                dst_v[base + i, :, 128 * half : 128 * half + 128] = src[half, SL * t : SL * t + SL, :].astype(F32)
+                dst_v[base + i, :, 128 * half : 128 * half + 128] = src[0, half, SL * t : SL * t + SL, :].astype(F32)
 
     unpack_maps("yo", r.y, r.y_v)
     unpack_maps("mo", r.dm, r.dm_v)
@@ -736,7 +921,7 @@
     middle = dict(
         yo=of((CHAN, ROWS, 128), BF), mo=of((CHAN, ROWS, 128), BF), tall=of((n_dp, 8, 128), F32),
         ext=of((n_dp, 8, 128), F32), both=of((2 * maps, emb), BF), de=of((SL, emb), F32))
-    middle.update({name: of((2, SL * taps, 128), BF) for name, taps in ITEMS})
+    middle.update({name: of((1, 2, SL * item[0], 128), BF) for name, item in ITEMS.items()})
     v = pltpu.VMEM
     maps2 = 2 * ROWS
     scratch = dict(
@@ -747,7 +932,8 @@
         yp=v((CHAN, ROWS, 128), BF), mp=v((CHAN, ROWS, 128), BF),
         w1g=v((9, C, C), BF), w2g=v((9, C, C), BF), weg=v((1, C, emb), BF), wqg=v((4, C, C), BF),
         bd=v((C, C), BF), tl=v((8, 128), F32), ta=v((n_dp, 8, 128), F32), par=v((8, 128), F32),
-        pg=v((CHAN, 8, 128), F32), pa=v((8, C), F32), emb=v((16, C), F32),
+        pg=v((CHAN, 8, 128), F32), pa=v((8, C), F32), emb=v((8, C), F32),
+        wel=v((1, SL, emb), BF), el=v((8, 128), F32), eg=v((CHAN, 8, 128), F32),
         a1=v((TALL + 2 * GAP, 3 * C), BF), a2=v((TALL + 2 * GAP, 3 * C), BF), dd=v((TALL + 2 * GAP, 3 * C), BF),
         h=v((TALL, C), F32), xf=v((maps2, C), F32), n1=v((maps2, C), F32), n2=v((maps2, C), F32),
         n3=v((maps2, C), F32), dres=v((maps2, C), F32), big=v((maps2, C), F32), p=v((maps2, C), F32),
@@ -757,17 +943,13 @@
         dw1=v((9, C, C), BF), dw2=v((9, C, C), BF), dqo=v((4, C, C), BF))
     for name in ("a3", "q", "k", "v", "pb", "o", "g", "do", "dq", "dk", "dv"):
         scratch[name] = v((maps2, C), BF)
-    for name, taps in ITEMS:
-        rows, span = SL * taps, SL * taps // (team // 2)
-        scratch.update({
-            name + "_rc": v((2, taps, SL, C), BF), name + "_sx": v((2, 2, rows, 128), BF),
-            name + "_ry": v((3, rows, 128), BF), name + "_hs": v((rows, 128), BF),
-            name + "_rz": v((team // 2, span, 128), BF), name + "_pc": v((span, 128), BF),
-            name + "_rt": v((teams, span, 128), BF)})
-    n_remote = 72 + 3 * (n_dp - 1) + len(ITEMS) * (5 + team // 2 + team + teams)
+    for name, (taps, order, spread) in ITEMS.items():
+        buffers = reduction_scratch(taps, order, spread, team, teams)
+        scratch.update({name + "_" + k: b for k, b in buffers.items()})
+    groups = 48 + len(ITEMS) * 7
     scratch.update(
-        send=pltpu.SemaphoreType.DMA((n_remote,)), recv=pltpu.SemaphoreType.DMA((n_remote,)),
-        own=pltpu.SemaphoreType.DMA((48,)))
+        idle=v((4096, 128), BF), send=pltpu.SemaphoreType.DMA((24,)), recv=pltpu.SemaphoreType.DMA((groups,)),
+        own=pltpu.SemaphoreType.DMA((40,)))
     got = pl.pallas_call(
         functools.partial(mega, n_dp, list(inputs) + list(middle) + list(scratch)),
         out_shape=tuple(middle.values()),

time: 78.7 us -> 72.6 us (0.922)
  Pallas kernels: 77.2 us -> 71.2 us
    pallas_call x1, Pallas kernels: 71.6 us -> 65.6 us  [per_device(): pl.pallas_call(functools.partial(mega, n_dp, list(inputs) + list(middle)...]
where the time goes in v3:
time: 72.6 us; the launch traced here: 72.5 us
  Pallas kernels  71.2 us (98%)
  between operations  1.3 us (2%)
    pallas_call x1, Pallas kernels, per_device(): pl.pallas_call(functools.partial(mega, n_dp, list(inputs) + list(middle)...  65.6 us
    pallas_call x1, Pallas kernels, per_device(): pl.pallas_call(functools.partial(finish, n_dp, list(middle) + list(result...  5.56 us

profile of v3, /device:TPU:0, one launch (start us, length us, event | category | flops | bytes accessed | tf_op | source)
XLA Modules:
  0.0 72.5 jit_solution(354905544972564780)
XLA Ops:
  1.3 65.6 %blocks.1 = (bf16[4,256,128]{2,1,0:T(8,128)(2,1)}, bf16[4,256,128]{2,1,0:T(8,128)(2,1)}, f32[8,8,128]{2,1,0:T(8,128)}, f32[8,8,128]{2,1,0:T(8,128)}, bf16[128,51...) custom-call(bf16[8,256,64]{2,1,0:T(8,128)(2,1)} %bitcast.40, ...), custom_call_target="tpu_custom_call" | custom-call | tf_op jit(solution)/shard_map/blocks/pallas_call | solution.py:953
  66.9 5.6 %finish.1 = (bf16[8,256,64]{2,1,0:T(8,128)(2,1)}, bf16[8,256,64]{2,1,0:T(8,128)(2,1)}, f32[1000,512]{1,0:T(8,128)}, f32[9,64,256]{2,1,0:T(8,128)}, f32[9,64,256]...) custom-call(bf16[4,256,128]{2,1,0:T(8,128)(2,1)} %get-tuple-element., ...), custom_call_target="tpu_custom_call" | custom-call | tf_op jit(solution)/shard_map/finish/pallas_call | solution.py:969

commit v4 on v3

--- a/solution.py
+++ b/solution.py
@@ -86,11 +86,13 @@
     dst[rows, 2 * C : 3 * C] = last.astype(BF)
 
 
-def norm_forward(load, n_ref, gain, shift, bd, emit, midway=None):
+def norm_forward(load, n_ref, gain, shift, bd, emit, first=None, early=None, midway=None):
     def sums(m, at, held):
-        return held + fold(load(m, at))
+        return held + fold((first or load)(m, at))
 
     total = passes(sums, zero_pair())
+    if early is not None:
+        early()
     mean = group_total([col(t) for t in total], bd)
     mean = [v * (1.0 / COUNT) for v in mean]
 
@@ -151,24 +153,28 @@
     return first, second
 
 
-def conv_forward(a_ref, w_ref, h_ref, ready, order):
-    for row in order:
-        ready(row)
+BLOCKS = ((0, STEP), (STEP, ROWS))
+
+
+def conv_forward(a_ref, w_ref, h_ref, rows, add):
+    for start, size in BLOCKS:
         total = None
-        for c in range(3):
-            part = dot_nt(a_ref[16 * row : 16 * row + TALL, C * c : C * c + C], w_ref[3 * row + c])
+        for row in rows:
+            for c in range(3):
+                at = 16 * row + start
+                part = dot_nt(a_ref[at : at + size, C * c : C * c + C], w_ref[3 * row + c])
+                total = part if total is None else total + part
+        h_ref[start : start + size, :] = total + h_ref[start : start + size, :] if add else total
+
+
+def conv_back(d_ref, w_ref, h_ref):
+    for start, size in BLOCKS:
+        total = None
+        for row in range(3):
+            at = 16 * (2 - row) + start
+            part = dot(d_ref[at : at + size, :], w_ref[3 * row : 3 * row + 3].reshape(3 * C, C))
             total = part if total is None else total + part
-        h_ref[...] = total if row == order[0] else h_ref[...] + total
-
-
-def conv_back(d_ref, w_ref, h_ref, between=None):
-    for row in range(3):
-        at = 16 * (2 - row)
-        w = w_ref[3 * row : 3 * row + 3].reshape(3 * C, C)
-        part = dot(d_ref[at : at + TALL, :], w)
-        h_ref[...] = part if row == 0 else h_ref[...] + part
-        if between is not None:
-            between(row)
+        h_ref[start : start + size, :] = total
 
 
 def conv_weight(a_ref, turned, dw_ref, row):
@@ -201,6 +207,19 @@
         self.links.wait_rows(self.links.recv.at[self.at], self.rows)
 
 
+class LocalGroup:
+    def __init__(self, links):
+        self.links, self.at, self.rows = links, links.local, 0
+        links.local += 1
+
+    def copy(self, src, dst):
+        self.rows += rows_in(src)
+        pltpu.make_async_copy(src, dst, self.links.own.at[self.at]).start()
+
+    def wait(self):
+        self.links.wait_rows(self.links.own.at[self.at], self.rows)
+
+
 def rows_in(ref):
     size = ref.dtype.itemsize
     for n in ref.shape:
@@ -230,6 +249,12 @@
         copy.start()
         return copy
 
+    def here_all(self, copies=()):
+        group = LocalGroup(self)
+        for src, dst in copies:
+            group.copy(src, dst)
+        return group
+
     def close(self):
         for at, rows in self.ended + [(self.senders, self.sending)]:
             self.wait_rows(self.send.at[at], rows)
@@ -244,68 +269,43 @@
     return pl.ds(pl.multiple_of(start, size), size)
 
 
-def reduction_scratch(taps, order, spread, team, teams):
-    rows, span = SL * taps, SL * taps // (team // 2)
-    left = rows if spread is None else span
-    shapes = dict(rc=(2, taps, SL, C), s0=(2, 2, rows, 128), pc=(1, 1, left, 128), rt=(teams, 1, 1, left, 128))
-    if spread is None:
-        shapes.update({f"c{i}": (1, 1, rows, 128) for i in range(3)})
-    size = dict(y=2, x=2, z=team // 2)
-    for k, axes in enumerate(order):
-        peers = 1
-        for axis in axes:
-            peers *= size[axis]
-            size[axis] = 1
-        shape = (size["y"], size["x"], size["z"] * span, 128)
-        shapes[f"r{k}"] = (max(peers - 1, 1),) + shape
-        shapes[f"s{k + 1}"] = shape
+def reduction_scratch(taps, order, kind, teams):
+    rows = SL * taps
+    part = (1, 1, rows, 128)
+    shapes = dict(rc=(2, taps, SL, C), s0=(2, 2, rows, 128), pc=part, rt=(teams,) + part)
+    shapes.update({name: part for name in ("c0", "c1", "c2", "p0", "p1", "t0", "t1")})
+    size = dict(y=2, x=2)
+    for k, axis in enumerate(order):
+        size[axis] = 1
+        shapes[f"r{k}"] = shapes[f"s{k + 1}"] = (size["y"], size["x"], rows, 128)
     buffers = {name: pltpu.VMEM(shape, BF) for name, shape in shapes.items()}
-    if spread is None:
-        buffers.update(cs=pltpu.SemaphoreType.DMA((3,)), cr=pltpu.SemaphoreType.DMA((3,)))
+    if kind is Chain:
+        buffers.update(cs=pltpu.SemaphoreType.DMA((4,)))
     return buffers
 
 
 class Reduction:
-    def __init__(self, at, links, grad, out, work, order, spread):
-        self.at, self.links, self.grad, self.out, self.w = at, links, grad, out, work
-        self.order, self.spread = order, spread
+    def __init__(self, at, links, grad, out, work, order):
+        self.at, self.links, self.grad, self.out, self.w, self.order = at, links, grad, out, work, order
         self.taps = grad.shape[0]
-        self.span = SL * self.taps // (at.team // 2)
         self.size = dict(y=2, x=2, z=at.team // 2)
         self.stage = -1
-        self.whole = dict(y=True, x=True, z=True)
-        w = self.w
+        self.whole = dict(y=True, x=True)
         self.group = links.group([
-            (grad.at[:, aligned(SL * (2 * y + 1 - at.core), SL), :], w.rc.at[y], at.sibling) for y in range(2)])
-
-    def view(self, ref, place):
-        parts = []
-        for axis in "yx":
-            parts.append(pl.ds(place[axis], 1) if axis in place and self.whole[axis] else slice(None))
-        if "z" in place and self.whole["z"]:
-            parts.append(aligned(self.span * place["z"], self.span))
-        else:
-            parts.append(slice(None))
-        return ref.at[tuple(parts)]
-
-    def peers(self, axes):
-        steps = [{}]
-        for axis in axes:
-            steps = [{**step, axis: s} for step in steps for s in range(self.size[axis])]
-        for step in steps[1:]:
-            yield {axis: (self.at.place[axis] + s) % self.size[axis] for axis, s in step.items()}
+            (grad.at[:, aligned(SL * (2 * y + 1 - at.core), SL), :], self.w.rc.at[y], at.sibling) for y in range(2)])
+
+    def view(self, ref, axis, index):
+        return ref.at[pl.ds(index, 1)] if axis == "y" else ref.at[:, pl.ds(index, 1)]
 
     def send(self):
-        axes = self.order[self.stage]
+        axis = self.order[self.stage]
+        other = 1 - self.at.place[axis]
         current, arriving = getattr(self.w, f"s{self.stage}"), getattr(self.w, f"r{self.stage}")
-        self.group = self.links.group([
-            (self.view(current, place), arriving.at[slot], self.at.peer(place))
-            for slot, place in enumerate(self.peers(axes))])
+        self.group = self.links.group([(self.view(current, axis, other), arriving, self.at.peer({axis: other}))])
 
     def collect(self):
         at, w = self.at, self.w
-        if self.group.rows:
-            self.group.wait()
+        self.group.wait()
         if self.stage < 0:
             for y in range(2):
                 for t in range(self.taps):
@@ -314,14 +314,10 @@
                     for half in range(2):
                         w.s0[y, half, SL * t : SL * t + SL, :] = total[:, 128 * half : 128 * half + 128]
             return
-        axes = self.order[self.stage]
-        current, arriving = getattr(w, f"s{self.stage}"), getattr(w, f"r{self.stage}")
-        total = self.view(current, {axis: at.place[axis] for axis in axes})[...].astype(F32)
-        for slot in range(len(list(self.peers(axes)))):
-            total = total + arriving[slot].astype(F32)
+        axis = self.order[self.stage]
+        mine = self.view(getattr(w, f"s{self.stage}"), axis, at.place[axis])[...].astype(F32)
+        total = mine + getattr(w, f"r{self.stage}")[...].astype(F32)
         getattr(w, f"s{self.stage + 1}")[...] = total.astype(BF)
-        for axis in axes:
-            self.whole[axis] = False
 
     def across_teams(self, piece):
         at, w = self.at, self.w
@@ -337,86 +333,58 @@
         w.pc[...] = total.astype(BF)
         return w.pc
 
-    def region(self, axes):
-        place = self.at.place
-        rows = slice(None) if "z" in axes else aligned(self.span * place["z"], self.span)
-        return self.out.at[:, pl.ds(place["x"], 1), rows]
+    def share(self, source):
+        source = self.across_teams(source) if self.at.teams > 1 else source
+        target = self.out.at[:, pl.ds(self.at.place["x"], 1)]
+        self.at.results.copy(source, target)
+        self.group = self.links.group([(source, target, self.at.peer(dict(x=1 - self.at.place["x"])))])
 
     def advance(self):
-        last = len(self.order)
+        last = len(self.order) - 1
+        if self.stage <= last:
+            self.collect()
         if self.stage < last:
-            self.collect()
-        self.stage += 1
-        if self.stage < last:
+            self.stage += 1
             self.send()
-            return
-        axes = self.spread[self.stage - last]
-        if self.stage == last:
-            source = getattr(self.w, f"s{last}")
-            if self.at.teams > 1:
-                source = self.across_teams(source)
-            target = self.region("")
-            self.own = self.links.here(source, target)
         else:
-            if self.stage == last + 1:
-                self.own.wait()
-            if self.group.rows:
-                self.group.wait()
-            source = target = self.region("".join(self.spread[: self.stage - last]))
-        self.group = self.links.group([(source, target, self.at.peer(place)) for place in self.peers(axes)])
+            self.along_z(self.stage - last, getattr(self.w, f"s{last + 1}"))
+            self.stage += 1
 
     def finish(self):
-        if self.spread is None or len(self.spread) == 1:
-            self.own.wait()
-        if self.group.rows:
-            self.group.wait()
+        self.group.wait()
 
 
 class Chain(Reduction):
-    def copy(self, step, src, dst, z):
+    def copy(self, sent, got, src, dst, z):
         w = self.w
         return pltpu.make_async_remote_copy(
-            src_ref=src, dst_ref=dst, send_sem=w.cs.at[step], recv_sem=w.cr.at[step],
+            src_ref=src, dst_ref=dst, send_sem=w.cs.at[sent], recv_sem=w.cs.at[2 + got],
             device_id=self.at.peer(dict(z=z)), device_id_type=MESH)
 
-    def prepare(self):
-        z, w = self.at.place["z"], self.w
-        total = getattr(w, f"s{len(self.order)}")
-        count = self.size["z"]
-        self.end = (z == 0) | (z == count - 1)
-        self.inner = jnp.logical_not(self.end)
-        middle = jnp.where(z < 2, 1, 2)
-        self.inward = self.copy(0, total, w.c0, middle)
-        self.swap = self.copy(1, w.c1, w.c2, count - 1 - z)
-        self.outward = self.copy(2, w.pc, w.pc, jnp.where(z < 2, 0, 3))
-        return total
-
-    def advance(self):
-        w, last = self.w, len(self.order)
-        if self.stage < last - 1:
-            self.collect()
-            self.stage += 1
-            self.send()
-            return
-        long, alone = self.size["z"] == 4, self.size["z"] == 1
-        if self.stage == last - 1:
-            self.collect()
-            total = self.prepare()
+    def along_z(self, step, total):
+        w, count = self.w, self.size["z"]
+        long, alone = count == 4, count == 1
+        if step == 0:
+            z = self.at.place["z"]
+            self.end = (z == 0) | (z == count - 1)
+            self.inner = jnp.logical_not(self.end)
+            self.inward = self.copy(0, 0, total, w.c0, jnp.where(z < 2, 1, 2))
+            self.swap = self.copy(0, 1, w.c1, w.c2, count - 1 - z)
+            self.outward = self.copy(1, 0, w.pc, w.pc, jnp.where(z < 2, 0, 3))
             if long:
                 pl.when(self.end)(self.inward.start)
             else:
                 w.c1[...] = total[...]
-        elif self.stage == last:
+        elif step == 1:
             if long:
                 @pl.when(self.inner)
                 def _():
                     self.inward.wait_recv()
-                    total = getattr(w, f"s{last}")[...].astype(F32) + w.c0[...].astype(F32)
-                    w.c1[...] = total.astype(BF)
+                    w.c1[...] = (total[...].astype(F32) + w.c0[...].astype(F32)).astype(BF)
                     self.swap.start()
             elif not alone:
                 self.swap.start()
-        elif self.stage == last + 1:
+        elif step == 2:
             def join():
                 self.swap.wait_recv()
                 w.pc[...] = (w.c1[...].astype(F32) + w.c2[...].astype(F32)).astype(BF)
@@ -432,8 +400,10 @@
                 join()
         else:
             if long:
-                pl.when(self.end)(self.outward.wait_recv)
-                pl.when(self.end)(self.inward.wait_send)
+                @pl.when(self.end)
+                def _():
+                    self.outward.wait_recv()
+                    self.inward.wait_send()
 
                 @pl.when(self.inner)
                 def _():
@@ -441,18 +411,33 @@
                     self.outward.wait_send()
             elif not alone:
                 self.swap.wait_send()
-            source = self.across_teams(w.pc) if self.at.teams > 1 else w.pc
-            target = self.region("z")
-            self.own = self.links.here(source, target)
-            self.group = self.links.group([(source, target, self.at.peer(place)) for place in self.peers("x")])
-        self.stage += 1
-
-
-YX, XY, YXZ, XYZ = ("y", "x"), ("x", "y"), ("y", "x", "z"), ("x", "y", "z")
-STEPS, ONCE = ("z", "x"), ("zx",)
+            self.share(w.pc)
+
+
+class Pairs(Reduction):
+    def along_z(self, step, total):
+        w, z = self.w, self.at.place["z"]
+        partners = [z + 1 - 2 * (z % 2), (z + 2) % 4]
+        partners[self.size["z"] // 2 :] = [None] * (2 - self.size["z"] // 2)
+        if step == 0:
+            self.held = total
+        elif partners[step - 1] is not None:
+            self.group.wait()
+            total = self.held[...].astype(F32) + getattr(w, f"p{step - 1}")[...].astype(F32)
+            self.held = getattr(w, f"t{step - 1}")
+            self.held[...] = total.astype(BF)
+        if step == len(partners):
+            self.share(self.held)
+        elif partners[step] is not None:
+            self.group = self.links.group([
+                (self.held, getattr(w, f"p{step}"), self.at.peer(dict(z=partners[step])))])
+
+
+YX, XY = ("y", "x"), ("x", "y")
 ITEMS = {
-    "ga": (4, YX, None), "gb0": (3, XY, None), "gb1": (3, YX, None), "gb2": (3, YX, None),
-    "gc0": (3, YXZ, STEPS), "gc1": (3, XYZ, STEPS), "gc2": (3, YXZ, ONCE)}
+    "ga0": (4, XY, Chain), "gb0": (3, YX, Chain), "gb1": (3, XY, Chain), "gb2": (3, XY, Chain),
+    "gc0": (4, XY, Pairs), "gc1": (3, XY, Pairs), "gc2": (2, YX, Pairs)}
+SENDS, GROUPS_OF_COPIES = 8, 72
 GAINS = ("gain1", "shift1", "gain2", "shift2", "gain3", "shift3")
 
 
@@ -474,6 +459,7 @@
     at = SimpleNamespace(core=core, sibling=sibling, team=team, teams=teams, rank=rank, lead=lead, place=own_place,
                          peer=peer, device=lambda p: (p, chan))
     links = Links(r.send, r.recv, r.own, r.idle)
+    at.results = links.here_all()
 
     def others():
         return [(lax.rem(dp + s, n_dp), chan) for s in range(1, n_dp)]
@@ -482,13 +468,13 @@
     for device in quads + (oblique,) + tuple(others()):
         pl.semaphore_signal(barrier, inc=1, device_id=device, device_id_type=MESH)
     load_x, load_ts, load_table = links.here(r.x, r.xl), links.here(r.ts, r.tss), links.here(r.table, r.tab)
-    load_par = [links.here(getattr(r, name), r.pin.at[i]) for i, name in enumerate(GAINS)]
+    for i, name in enumerate(GAINS):
+        pltpu.make_async_copy(getattr(r, name), r.pin.at[i], r.gains).start()
     load_we, load_dy, load_cnt = links.here(r.we, r.wel), links.here(r.dy, r.dyl), links.here(r.cnt, r.cns)
     mine = aligned(SL * chan, SL)
-    fill = [
-        links.here(r.w1, r.w1g.at[:, mine, :]), links.here(r.w2, r.w2g.at[:, mine, :]),
-        links.here(r.we, r.weg.at[:, mine, :]),
-        links.here(r.wq, r.wqg.at[0:3, mine, :]), links.here(r.wo, r.wqg.at[3:4, mine, :])]
+    fill = links.here_all([
+        (r.w1, r.w1g.at[:, mine, :]), (r.w2, r.w2g.at[:, mine, :]), (r.we, r.weg.at[:, mine, :]),
+        (r.wq, r.wqg.at[0:3, mine, :]), (r.wo, r.wqg.at[3:4, mine, :])])
 
     def pack(src, dst):
         for k in range(CHAN):
@@ -499,8 +485,7 @@
 
     load_x.wait()
     pack(r.xl, r.xp)
-    for copy in load_par:
-        copy.wait()
+    pltpu.make_async_copy(r.pin, r.pin, r.gains).wait()
     r.par[...] = jnp.zeros((8, 128), F32)
     for i in range(len(GAINS)):
         r.par[i : i + 1, 0:SL] = r.pin[i].astype(F32)
@@ -543,8 +528,6 @@
     one = [Share(rows3(r.w1, row), rows3(r.w1g, row), True) for row in range(3)]
     for share in one:
         share.own()
-    moves_x = links.group(
-        [(r.xp.at[d[1]], r.xg.at[chan], d) for d in quads] + [(r.par, r.pg.at[chan], d) for d in quads])
 
     load_ts.wait()
     row8 = lax.broadcasted_iota(jnp.int32, (8, 128), 0)
@@ -569,30 +552,35 @@
     r.el[...] = jnp.zeros((8, 128), F32)
     r.el[:, 0:SL] = dot_nt(tsil, r.wel[0])[0:8]
     r.eg[chan] = r.el[...]
+    moves_x = links.group(
+        [(r.xp.at[d[1]], r.xg.at[chan], d) for d in quads] + [(r.par, r.pg.at[chan], d) for d in quads])
     moves_emb = links.group([(r.el, r.eg.at[chan], d) for d in quads])
-    two = [Share(rows3(r.w2, row), rows3(r.w2g, row), row < 2) for row in range(3)]
-    out = [Share(r.wq, r.wqg.at[0:3], False), Share(r.wo, r.wqg.at[3:4], False)]
-    for share in two + out:
-        share.own()
-    load_dy.wait()
-    pack(r.dyl, r.dyp)
-    moves_late = links.group([(r.tl, r.ta.at[dp], d) for d in others()])
-    r.dyg[chan] = r.dyp[chan]
-    moves_dy = links.group([(r.dyp.at[d[1]], r.dyg.at[chan], d) for d in quads])
-    mix = Share(r.we, r.weg, False)
-    mix.own()
+    r.xg[chan] = r.xp[chan]
+    r.pg[chan] = r.par[...]
     at_row = lax.broadcasted_iota(jnp.int32, (C, C), 0) // (C // GROUPS)
     at_col = lax.broadcasted_iota(jnp.int32, (C, C), 1) // (C // GROUPS)
     r.bd[...] = jnp.where(at_row == at_col, 1.0, 0.0).astype(BF)
     for ref in (r.a1, r.a2, r.dd):
         for gap in range(3):
             ref[gap * STEP : gap * STEP + GAP, :] = jnp.zeros((GAP, 3 * C), BF)
-    r.xg[chan] = r.xp[chan]
-    r.pg[chan] = r.par[...]
-    for share in one:
-        share.relay()
+    load_dy.wait()
+    pack(r.dyl, r.dyp)
+    r.dyg[chan] = r.dyp[chan]
+    two = []
+    for row in range(3):
+        one[row].relay()
+        two.append(Share(rows3(r.w2, row), rows3(r.w2g, row), row < 2))
+        two[row].own()
     one[0].relay_again()
+    out = [Share(r.wq, r.wqg.at[0:3], False), Share(r.wo, r.wqg.at[3:4], False)]
+    for share in out:
+        share.own()
     one[1].relay_again()
+    moves_dy = links.group([(r.dyp.at[d[1]], r.dyg.at[chan], d) for d in quads])
+    one[2].relay_again()
+    mix = Share(r.we, r.weg, False)
+    mix.own()
+    moves_late = links.group([(r.tl, r.ta.at[dp], d) for d in others()])
 
     bd = r.bd[...]
     moves_x.wait()
@@ -627,47 +615,44 @@
         return emit
 
     rstd1 = norm_forward(lambda m, at: r.xf[rows_of(m, at), :], r.n1, gain1, shift1, bd, to_shift(r.a1),
-                         one[2].relay_again)
-    for copy in fill:
-        copy.wait()
-
-    def ready_one(row):
-        if row == 2:
-            two[0].relay()
-        one[row].landed()
-
-    conv_forward(r.a1, r.w1g, r.h, ready_one, (0, 1, 2))
-    two[1].relay()
+                         early=two[0].relay, midway=two[1].relay)
+    fill.wait()
+
+    for share in one:
+        share.landed()
+    conv_forward(r.a1, r.w1g, r.h, (0, 1, 2), False)
     moves_emb.wait()
     for b in range(2):
         first, _ = unpack(r.eg[2 * b], r.eg[2 * b + 1])
         r.emb[:, 128 * b : 128 * b + 128] = first
     emb = [r.emb[pl.ds(2 * chan + m, 1), :] for m in range(2)]
-    rstd2 = norm_forward(lambda m, at: r.h[rows_gap(m, at), :] + emb[m], r.n2, gain2, shift2, bd, to_shift(r.a2))
-    two[2].relay()
+    rstd2 = norm_forward(lambda m, at: r.h[rows_gap(m, at), :] + emb[m], r.n2, gain2, shift2, bd, to_shift(r.a2),
+                         midway=two[2].relay)
     two[0].relay_again()
-
-    def ready_two(row):
-        if row == 0:
-            two[1].relay_again()
-        if row == 1:
-            for share in out:
-                share.relay()
-        two[row].landed()
-
-    conv_forward(r.a2, r.w2g, r.h, ready_two, (2, 0, 1))
+    two[1].relay_again()
+    two[0].landed()
+    two[2].landed()
+    conv_forward(r.a2, r.w2g, r.h, (0, 2), False)
+    for share in out:
+        share.relay()
+    two[1].landed()
+    conv_forward(r.a2, r.w2g, r.h, (1,), True)
 
     def load_resid(m, at):
-        return r.xf[rows_of(m, at), :] + r.h[rows_gap(m, at), :]
+        return r.xf[rows_of(m, at), :]
+
+    def make_resid(m, at):
+        value = r.xf[rows_of(m, at), :] + r.h[rows_gap(m, at), :]
+        r.xf[rows_of(m, at), :] = value
+        return value
 
     def to_a3(m, at, u):
         r.a3[rows_of(m, at), :] = u.astype(BF)
 
-    rstd3 = norm_forward(load_resid, r.n3, gain3, shift3, bd, to_a3)
+    rstd3 = norm_forward(load_resid, r.n3, gain3, shift3, bd, to_a3, first=make_resid)
     out[0].landed()
     for j, ref in enumerate((r.q, r.k, r.v)):
         ref[...] = dot_nt(r.a3[...], r.wqg[j]).astype(BF)
-    mix.relay()
     load_cnt.wait()
     count = r.cns[0]
     live = [jnp.where(2 * chan + m < count, 1.0, 0.0).astype(F32) for m in range(2)]
@@ -680,25 +665,9 @@
         r.p[half[m], :] = p
         r.pb[half[m], :] = p.astype(BF)
         r.o[half[m], :] = dot(p.astype(BF), r.v[half[m], :]).astype(BF)
+
+    moves_dy.wait()
     out[1].landed()
-    r.big[...] = dot_nt(r.o[...], r.wqg[3])
-
-    def pack_out(at, pair, dst):
-        for b in range(2):
-            even, odd = unpack(*(v[:, 128 * b : 128 * b + 128] for v in pair))
-            dst[2 * b, pl.ds(at, CH), :] = even.astype(BF)
-            dst[2 * b + 1, pl.ds(at, CH), :] = odd.astype(BF)
-
-    def to_y(i, held):
-        at = chunk_at(i)
-        pack_out(at, [(load_resid(m, at) + r.big[rows_of(m, at), :]) * live[m] for m in range(2)], r.yp)
-        return held
-
-    lax.fori_loop(0, ROWS // CH, to_y, 0)
-    own_y = links.here(r.yp.at[chan], r.yo.at[chan])
-    moves_out = links.group([(r.yp.at[d[1]], r.yo.at[chan], d) for d in quads])
-
-    moves_dy.wait()
 
     def open_dy(i, held):
         spread_out(r.dyg, chunk_at(i), r.g, live)
@@ -720,20 +689,27 @@
         parts = [dot(ref[half[m], :].T, r.a3[half[m], :]) for m in range(2)]
         r.dqo[j] = (parts[0] + parts[1]).astype(BF)
 
-    def reduction(name, grad):
-        _, order, spread = ITEMS[name]
-        work = SimpleNamespace(**{k[len(name) + 1 :]: getattr(r, k) for k in names if k.startswith(name + "_")})
-        kind = Chain if spread is None else Reduction
-        return kind(at, links, grad, getattr(r, name), work, order, spread)
-
-    ga = reduction("ga", r.dqo)
+    items = []
+
+    def reduce(letter, grad):
+        start = 0
+        for name, (taps, order, kind) in ITEMS.items():
+            if name[1] == letter:
+                work = SimpleNamespace(**{k[4:]: getattr(r, k) for k in names if k.startswith(name + "_")})
+                items.append(kind(at, links, grad.at[start : start + taps], getattr(r, name), work, order))
+                start += taps
+
+    def go(*which):
+        for i in which:
+            items[i].advance()
+
+    reduce("a", r.dqo)
     for m in range(2):
         total = None
         for j, ref in enumerate((r.dq, r.dk, r.dv)):
             part_j = dot(ref[half[m], :], r.wqg[j])
             total = part_j if total is None else total + part_j
         r.h[m * STEP : m * STEP + ROWS, :] = total
-    ga.advance()
 
     def to_dres(m, at, dv, held):
         value = r.g[rows_of(m, at), :].astype(F32) + dv
@@ -742,24 +718,19 @@
         return held
 
     passes(norm_back(r.h, r.n3, gain3, shift3, rstd3, bd, False, r.e, 4, to_dres))
+    go(0)
 
     def turn():
         for m in range(2):
             r.turn[m] = r.dd[GAP + STEP * m : GAP + STEP * m + ROWS, C : 2 * C].T
 
     turn()
-    gb = []
     for row in range(3):
         conv_weight(r.a2, r.turn, r.dw2, row)
-        gb.append(reduction(f"gb{row}", rows3(r.dw2, row)))
-    def between(row):
-        if row == 0:
-            gb[0].advance()
-            gb[1].advance()
-        if row == 1:
-            gb[2].advance()
-
-    conv_back(r.dd, r.w2g, r.h, between)
+    reduce("b", r.dw2)
+    conv_back(r.dd, r.w2g, r.h)
+    go(1, 2, 3)
+    mix.relay()
 
     def to_dh1(m, at, dv, held):
         write_shift(r.dd, m, at, dv, False)
@@ -770,69 +741,94 @@
         r.dm[chan, m : m + 1, :] = col(demb[m]).astype(BF).astype(F32)
     moves_dm = links.group([(r.dm.at[chan], r.dm.at[chan], d) for d in quads])
     turn()
-    gc = []
     for row in range(3):
         conv_weight(r.a1, r.turn, r.dw1, row)
-        gc.append(reduction(f"gc{row}", rows3(r.dw1, row)))
-        if row == 1:
-            gc[0].advance()
-            ga.advance()
-    for item in (gb[0], gc[1], gb[1], gc[2]):
-        item.advance()
-    conv_back(r.dd, r.w1g, r.h)
-    for item in (ga, gb[2]):
-        item.advance()
-    back1 = norm_back(r.h, r.n1, gain1, shift1, rstd1, bd, True, r.e, 0,
-                      lambda m, at, dv, held: r.dres[rows_of(m, at), :] + dv)
-
-    def to_maps(i, held):
+    reduce("c", r.dw1)
+    r.big[...] = dot_nt(r.o[...], r.wqg[3])
+
+    def pack_out(at, pair, dst):
+        for b in range(2):
+            even, odd = unpack(*(v[:, 128 * b : 128 * b + 128] for v in pair))
+            dst[2 * b, pl.ds(at, CH), :] = even.astype(BF)
+            dst[2 * b + 1, pl.ds(at, CH), :] = odd.astype(BF)
+
+    def to_y(i, held):
         at = chunk_at(i)
-        pack_out(at, [back1(m, at, 0) for m in range(2)], r.mp)
+        pack_out(at, [(load_resid(m, at) + r.big[rows_of(m, at), :]) * live[m] for m in range(2)], r.yp)
         return held
 
-    lax.fori_loop(0, ROWS // CH, to_maps, 0)
-    own_mp = links.here(r.mp.at[chan], r.mo.at[chan])
-    for d in quads:
-        moves_out.remote(r.mp.at[d[1]], r.mo.at[chan], d)
-    moves_dm.wait()
-    for j in range(CHAN):
-        r.dl[2 * j : 2 * j + 2, :] = r.dm[j, 0:2, :]
-    r.ra[dp] = r.dl[...]
-    for d in others():
-        moves_late.remote(r.dl, r.ra.at[dp], d)
-    for b in range(2):
-        block = r.e[:, 128 * b : 128 * b + 128]
-        r.es[2 * b] = block
-        r.es[2 * b + 1] = pltpu.roll(block, SL, 1)
-    r.er[chan] = r.es[chan]
-    moves_e = links.group([(r.es.at[d[1]], r.er.at[chan], d) for d in quads])
-    for item in (gb[1], gc[0], gc[1], gb[0], gb[2], ga, gb[1], gc[2], gc[0], gc[1], gb[0], gb[2]):
-        item.advance()
-    moves_e.wait()
-    r.et[...] = r.er[0] + r.er[1] + r.er[2] + r.er[3]
-    own_e = links.here(r.et, r.ext.at[dp])
-    for d in others():
-        moves_out.remote(r.et, r.ext.at[dp], d)
-    for item in (ga, gb[1], gc[2]):
-        item.advance()
-    mix.landed()
-    moves_late.wait()
-    maps = 8 * n_dp
-    temb, s, tsil = embeddings(r.ta[...].reshape(maps, 128))
-    rows = r.ra[...].reshape(maps, C)
-    r.rt[...] = rows.T
-    r.dew[...] = dot(r.rt[mine, :].astype(BF), tsil)
-    dtemb = dot(rows.astype(BF), r.weg[0]) * (s * (1.0 + temb * (1.0 - s)))
-    high = dtemb.astype(BF)
-    r.bw[0:maps, :] = high
-    r.bw[maps:, :] = (dtemb - high.astype(F32)).astype(BF)
-    ends = [links.here(r.dew, r.de), links.here(r.bw, r.both), links.here(r.ta, r.tall)]
-    for item in (gc[0], gb[0], gb[2], gc[1], gb[1], ga, gc[2], gb[0], gb[2], gc[0], gc[1]):
-        item.advance()
-    for item in [ga] + gb + gc:
+    lax.fori_loop(0, ROWS // CH, to_y, 0)
+
+    def data_one():
+        conv_back(r.dd, r.w1g, r.h)
+
+    def norm_one():
+        back1 = norm_back(r.h, r.n1, gain1, shift1, rstd1, bd, True, r.e, 0,
+                          lambda m, at, dv, held: r.dres[rows_of(m, at), :] + dv)
+
+        def to_maps(i, held):
+            at = chunk_at(i)
+            pack_out(at, [back1(m, at, 0) for m in range(2)], r.mp)
+            return held
+
+        lax.fori_loop(0, ROWS // CH, to_maps, 0)
+        moves_dm.wait()
+        for j in range(CHAN):
+            r.dl[2 * j : 2 * j + 2, :] = r.dm[j, 0:2, :]
+        r.ra[dp] = r.dl[...]
+        for d in others():
+            moves_late.remote(r.dl, r.ra.at[dp], d)
+        for b in range(2):
+            block = r.e[:, 128 * b : 128 * b + 128]
+            r.es[2 * b] = block
+            r.es[2 * b + 1] = pltpu.roll(block, SL, 1)
+        r.er[chan] = r.es[chan]
+        for d in quads:
+            moves_e.remote(r.es.at[d[1]], r.er.at[chan], d)
+
+    def send_maps():
+        for src, dst in ((r.yp, r.yo), (r.mp, r.mo)):
+            at.results.copy(src.at[chan], dst.at[chan])
+            for d in quads:
+                moves_out.remote(src.at[d[1]], dst.at[chan], d)
+
+    def send_gains():
+        moves_e.wait()
+        r.et[...] = r.er[0] + r.er[1] + r.er[2] + r.er[3]
+        at.results.copy(r.et, r.ext.at[dp])
+        for d in others():
+            moves_out.remote(r.et, r.ext.at[dp], d)
+
+    def embedding():
+        mix.landed()
+        moves_late.wait()
+        maps = 8 * n_dp
+        temb, s, tsil = embeddings(r.ta[...].reshape(maps, 128))
+        rows = r.ra[...].reshape(maps, C)
+        r.rt[...] = rows.T
+        r.dew[...] = dot(r.rt[mine, :].astype(BF), tsil)
+        dtemb = dot(rows.astype(BF), r.weg[0]) * (s * (1.0 + temb * (1.0 - s)))
+        high = dtemb.astype(BF)
+        r.bw[0:maps, :] = high
+        r.bw[maps:, :] = (dtemb - high.astype(F32)).astype(BF)
+        for src, dst in ((r.dew, r.de), (r.bw, r.both), (r.ta, r.tall)):
+            at.results.copy(src, dst)
+
+    moves_e, moves_out = links.group(), links.group()
+    go(0, 4, 5, 6)
+    data_one()
+    go(2, 1)
+    norm_one()
+    go(3, 0, 6, 4, 2, 3, 0, 5)
+    send_maps()
+    go(1)
+    send_gains()
+    go(6, 2, 4, 3, 5, 0, 1, 6)
+    embedding()
+    go(2, 4, 3, 5, 0, 1, 2, 6, 3, 1, 4, 5)
+    for item in items:
         item.finish()
-    for copy in [own_y, own_mp, own_e] + ends:
-        copy.wait()
+    at.results.wait()
     moves_out.wait()
     links.close()
 
@@ -844,8 +840,8 @@
     links = Links(None, None, r.own, None)
     items = list(ITEMS)
     load = {name: links.here(getattr(r, name), getattr(r, name + "_v"))
-            for name in ["tall", "both", "yo", "mo"] + items + ["ext"]}
-    stores = [links.here(r.de, r.de_out)]
+            for name in ["tall", "both", "yo", "mo", "de"] + items + ["ext"]}
+    stores = []
 
     def out(src, dst):
         stores.append(links.here(src, dst))
@@ -878,16 +874,21 @@
 
     unpack_maps("yo", r.y, r.y_v)
     unpack_maps("mo", r.dm, r.dm_v)
-    load["ga"].wait()
-    whole("ga", r.dq_v, 0, range(3))
+    load["de"].wait()
+    out(r.de_v, r.de_out)
+    load["ga0"].wait()
+    whole("ga0", r.dq_v, 0, range(3))
     out(r.dq_v, r.dq)
-    whole("ga", r.do_v, 0, [3])
+    whole("ga0", r.do_v, 0, [3])
     out(r.do_v, r.do)
-    for kind, dst_v, dst in (("gb", r.d2_v, r.d2), ("gc", r.d1_v, r.d1)):
-        for row in range(3):
-            load[f"{kind}{row}"].wait()
-            whole(f"{kind}{row}", dst_v, 3 * row, range(3))
-            out(dst_v.at[3 * row : 3 * row + 3], dst.at[3 * row : 3 * row + 3])
+    for letter, dst_v, dst in (("b", r.d2_v, r.d2), ("c", r.d1_v, r.d1)):
+        start = 0
+        for name, (taps, _, _) in ITEMS.items():
+            if name[1] == letter:
+                load[name].wait()
+                whole(name, dst_v, start, range(taps))
+                out(dst_v.at[start : start + taps], dst.at[start : start + taps])
+                start += taps
     load["ext"].wait()
     total = r.ext_v[0]
     for i in range(1, n_dp):
@@ -943,13 +944,14 @@
         dw1=v((9, C, C), BF), dw2=v((9, C, C), BF), dqo=v((4, C, C), BF))
     for name in ("a3", "q", "k", "v", "pb", "o", "g", "do", "dq", "dk", "dv"):
         scratch[name] = v((maps2, C), BF)
-    for name, (taps, order, spread) in ITEMS.items():
-        buffers = reduction_scratch(taps, order, spread, team, teams)
+    for name, (taps, order, kind) in ITEMS.items():
+        buffers = reduction_scratch(taps, order, kind, teams)
         scratch.update({name + "_" + k: b for k, b in buffers.items()})
-    groups = 48 + len(ITEMS) * 7
+    several = len(ITEMS) if teams > 1 else 0
     scratch.update(
-        idle=v((4096, 128), BF), send=pltpu.SemaphoreType.DMA((24,)), recv=pltpu.SemaphoreType.DMA((groups,)),
-        own=pltpu.SemaphoreType.DMA((40,)))
+        idle=v((4096, 128), BF), send=pltpu.SemaphoreType.DMA((SENDS + several,)),
+        recv=pltpu.SemaphoreType.DMA((GROUPS_OF_COPIES + several,)), own=pltpu.SemaphoreType.DMA((9 + several,)),
+        gains=pltpu.SemaphoreType.DMA(()))
     got = pl.pallas_call(
         functools.partial(mega, n_dp, list(inputs) + list(middle) + list(scratch)),
         out_shape=tuple(middle.values()),
@@ -963,7 +965,7 @@
         y=of((slots, ROWS, SL), BF), dm=of((slots, ROWS, SL), BF), dt=of((steps, emb), F32), d1=of((9, SL, C), F32),
         d2=of((9, SL, C), F32), de_out=of((SL, emb), F32), dq=of((3, SL, C), F32), do=of((1, SL, C), F32))
     results.update({f"e{i}": of((1, SL), F32) for i in range(6)})
-    scratch = {name + "_v": v(o.shape, o.dtype) for name, o in middle.items() if name != "de"}
+    scratch = {name + "_v": v(o.shape, o.dtype) for name, o in middle.items()}
     scratch.update({name + "_v": v(o.shape, o.dtype) for name, o in results.items() if name[0] != "e"})
     scratch.update(gains_v=v((6, 1, SL), F32), own=pltpu.SemaphoreType.DMA((48,)))
     got = pl.pallas_call(

time: 72.6 us -> 69.4 us (0.956)
  Pallas kernels: 71.2 us -> 67.9 us
    pallas_call x1, Pallas kernels: 5.56 us -> 3.84 us  [per_device(): pl.pallas_call(functools.partial(finish, n_dp, list(middle) + list(result...]
    pallas_call x1, Pallas kernels: 65.6 us -> 64 us  [per_device(): pl.pallas_call(functools.partial(mega, n_dp, list(inputs) + list(middle)...]
where the time goes in v4:
time: 69.4 us; the launch traced here: 69.2 us
  Pallas kernels  67.9 us (98%)
  between operations  1.3 us (2%)
    pallas_call x1, Pallas kernels, per_device(): pl.pallas_call(functools.partial(mega, n_dp, list(inputs) + list(middle)...  64 us
    pallas_call x1, Pallas kernels, per_device(): pl.pallas_call(functools.partial(finish, n_dp, list(middle) + list(result...  3.84 us

profile of v4, /device:TPU:0, one launch (start us, length us, event | category | flops | bytes accessed | tf_op | source)
XLA Modules:
  0.0 69.2 jit_solution(6560197310568699653)
XLA Ops:
  1.3 64.0 %blocks.1 = (bf16[4,256,128]{2,1,0:T(8,128)(2,1)}, bf16[4,256,128]{2,1,0:T(8,128)(2,1)}, f32[8,8,128]{2,1,0:T(8,128)}, f32[8,8,128]{2,1,0:T(8,128)}, bf16[128,51...) custom-call(bf16[8,256,64]{2,1,0:T(8,128)(2,1)} %bitcast.40, ...), custom_call_target="tpu_custom_call" | custom-call | tf_op jit(solution)/shard_map/blocks/pallas_call | solution.py:955
  65.3 3.8 %finish.1 = (bf16[8,256,64]{2,1,0:T(8,128)(2,1)}, bf16[8,256,64]{2,1,0:T(8,128)(2,1)}, f32[1000,512]{1,0:T(8,128)}, f32[9,64,256]{2,1,0:T(8,128)}, f32[9,64,256]...) custom-call(bf16[4,256,128]{2,1,0:T(8,128)(2,1)} %get-tuple-element., ...), custom_call_target="tpu_custom_call" | custom-call | tf_op jit(solution)/shard_map/finish/pallas_call | solution.py:971

commit v5 on v4

--- a/solution.py
+++ b/solution.py
@@ -20,7 +20,7 @@
 GAP = 16
 STEP = ROWS + GAP
 TALL = 2 * ROWS + GAP
-CH = 32
+CH = 128
 COUNT = ROWS * (C // GROUPS)
 
 
@@ -435,8 +435,14 @@
 
 YX, XY = ("y", "x"), ("x", "y")
 ITEMS = {
-    "ga0": (4, XY, Chain), "gb0": (3, YX, Chain), "gb1": (3, XY, Chain), "gb2": (3, XY, Chain),
-    "gc0": (4, XY, Pairs), "gc1": (3, XY, Pairs), "gc2": (2, YX, Pairs)}
+    "ga0": (4, YX, Chain),
+    "gb0": (3, YX, Chain),
+    "gb1": (3, YX, Chain),
+    "gb2": (3, XY, Chain),
+    "gc0": (3, YX, Pairs),
+    "gc1": (3, YX, Pairs),
+    "gc2": (3, XY, Pairs),
+}
 SENDS, GROUPS_OF_COPIES = 8, 72
 GAINS = ("gain1", "shift1", "gain2", "shift2", "gain3", "shift3")
 
@@ -729,14 +735,15 @@
         conv_weight(r.a2, r.turn, r.dw2, row)
     reduce("b", r.dw2)
     conv_back(r.dd, r.w2g, r.h)
-    go(1, 2, 3)
     mix.relay()
 
     def to_dh1(m, at, dv, held):
         write_shift(r.dd, m, at, dv, False)
         return held + fold(dv)
 
-    demb = passes(norm_back(r.h, r.n2, gain2, shift2, rstd2, bd, True, r.e, 2, to_dh1), zero_pair())
+    second = norm_back(r.h, r.n2, gain2, shift2, rstd2, bd, True, r.e, 2, to_dh1)
+    go(1, 2, 3)
+    demb = passes(second, zero_pair())
     for m in range(2):
         r.dm[chan, m : m + 1, :] = col(demb[m]).astype(BF).astype(F32)
     moves_dm = links.group([(r.dm.at[chan], r.dm.at[chan], d) for d in quads])
@@ -815,17 +822,17 @@
             at.results.copy(src, dst)
 
     moves_e, moves_out = links.group(), links.group()
-    go(0, 4, 5, 6)
+    go(0)
     data_one()
-    go(2, 1)
+    go(6, 4, 5, 3, 1)
     norm_one()
-    go(3, 0, 6, 4, 2, 3, 0, 5)
+    go(2, 0, 4, 6)
     send_maps()
-    go(1)
+    go(1, 5, 0, 2, 3)
     send_gains()
-    go(6, 2, 4, 3, 5, 0, 1, 6)
+    go(4, 6, 1, 5, 2, 0, 3)
     embedding()
-    go(2, 4, 3, 5, 0, 1, 2, 6, 3, 1, 4, 5)
+    go(4, 6, 1, 5, 2, 0, 3, 1, 4, 2, 3, 6, 5)
     for item in items:
         item.finish()
     at.results.wait()

time: 69.4 us -> 65.8 us (0.948)
  Pallas kernels: 67.9 us -> 64.3 us
    pallas_call x1, Pallas kernels: 64 us -> 60.4 us  [per_device(): pl.pallas_call(functools.partial(mega, n_dp, list(inputs) + list(middle)...]
where the time goes in v5:
time: 65.8 us; the launch traced here: 65.6 us
  Pallas kernels  64.3 us (98%)
  between operations  1.3 us (2%)
    pallas_call x1, Pallas kernels, per_device(): pl.pallas_call(functools.partial(mega, n_dp, list(inputs) + list(middle)...  60.4 us
    pallas_call x1, Pallas kernels, per_device(): pl.pallas_call(functools.partial(finish, n_dp, list(middle) + list(result...  3.85 us

profile of v5, /device:TPU:0, one launch (start us, length us, event | category | flops | bytes accessed | tf_op | source)
XLA Modules:
  0.0 65.6 jit_solution(6091572047279867931)
XLA Ops:
  1.3 60.4 %blocks.1 = (bf16[4,256,128]{2,1,0:T(8,128)(2,1)}, bf16[4,256,128]{2,1,0:T(8,128)(2,1)}, f32[8,8,128]{2,1,0:T(8,128)}, f32[8,8,128]{2,1,0:T(8,128)}, bf16[128,51...) custom-call(bf16[8,256,64]{2,1,0:T(8,128)(2,1)} %bitcast.40, ...), custom_call_target="tpu_custom_call" | custom-call | tf_op jit(solution)/shard_map/blocks/pallas_call | solution.py:962
  61.7 3.8 %finish.1 = (bf16[8,256,64]{2,1,0:T(8,128)(2,1)}, bf16[8,256,64]{2,1,0:T(8,128)(2,1)}, f32[1000,512]{1,0:T(8,128)}, f32[9,64,256]{2,1,0:T(8,128)}, f32[9,64,256]...) custom-call(bf16[4,256,128]{2,1,0:T(8,128)(2,1)} %get-tuple-element., ...), custom_call_target="tpu_custom_call" | custom-call | tf_op jit(solution)/shard_map/finish/pallas_call | solution.py:978

commit v6 on v5

--- a/solution.py
+++ b/solution.py
@@ -87,22 +87,25 @@
 
 
 def norm_forward(load, n_ref, gain, shift, bd, emit, first=None, early=None, midway=None):
-    def sums(m, at, held):
-        return held + fold((first or load)(m, at))
-
-    total = passes(sums, zero_pair())
+    sums = []
+    for at in range(0, ROWS, CH):
+        for m in range(2):
+            value = (first or load)(m, at)
+            if at == 0:
+                near = col(value[0:32]) * (1.0 / 32)
+                sums.append([near, zero_pair()[0], zero_pair()[0]])
+            d = value - sums[m][0]
+            sums[m][1] = sums[m][1] + fold(d)
+            sums[m][2] = sums[m][2] + fold(d * d)
     if early is not None:
         early()
-    mean = group_total([col(t) for t in total], bd)
-    mean = [v * (1.0 / COUNT) for v in mean]
-
-    def squares(m, at, held):
-        d = load(m, at) - mean[m]
-        return held + fold(d * d)
-
-    total = passes(squares, zero_pair())
-    var = group_total([col(t) for t in total], bd)
-    rstd = [lax.rsqrt(v * (1.0 / COUNT) + EPS) for v in var]
+    ones = [col(t[1]) for t in sums]
+    middle = [t[0] + one * (1.0 / ROWS) for t, one in zip(sums, ones)]
+    mean = [v * (GROUPS / C) for v in group_total(middle, bd)]
+    spread = [
+        col(t[2]) - one * one * (1.0 / ROWS) + ROWS * (mid - mu) * (mid - mu)
+        for t, one, mid, mu in zip(sums, ones, middle, mean)]
+    rstd = [lax.rsqrt(v * (1.0 / COUNT) + EPS) for v in group_total(spread, bd)]
     if midway is not None:
         midway()
 
@@ -156,7 +159,7 @@
 BLOCKS = ((0, STEP), (STEP, ROWS))
 
 
-def conv_forward(a_ref, w_ref, h_ref, rows, add):
+def conv_forward(a_ref, w_ref, h_ref, rows):
     for start, size in BLOCKS:
         total = None
         for row in rows:
@@ -164,7 +167,7 @@
                 at = 16 * row + start
                 part = dot_nt(a_ref[at : at + size, C * c : C * c + C], w_ref[3 * row + c])
                 total = part if total is None else total + part
-        h_ref[start : start + size, :] = total + h_ref[start : start + size, :] if add else total
+        h_ref[start : start + size, :] = total
 
 
 def conv_back(d_ref, w_ref, h_ref):
@@ -193,14 +196,18 @@
         links.used += 1
 
     def remote(self, src, dst, device):
+        self.plan(src, dst, device)()
+
+    def plan(self, src, dst, device):
         links, rows = self.links, rows_in(src)
         if links.sending + rows > links.idle.shape[0]:
             links.ended.append((links.senders, links.sending))
             links.senders, links.sending = links.senders + 1, 0
         links.sending += rows
         self.rows += rows
-        pltpu.make_async_remote_copy(
-            src_ref=src, dst_ref=dst, send_sem=links.send.at[links.senders], recv_sem=links.recv.at[self.at],
+        sender = links.send.at[links.senders]
+        return lambda: pltpu.make_async_remote_copy(
+            src_ref=src, dst_ref=dst, send_sem=sender, recv_sem=links.recv.at[self.at],
             device_id=device, device_id_type=MESH).start()
 
     def wait(self):
@@ -497,33 +504,52 @@
         r.par[i : i + 1, 0:SL] = r.pin[i].astype(F32)
     pl.semaphore_wait(barrier, CHAN + n_dp - 1)
 
-    part = 32 * bit
     far = SL * (2 * (1 - y) + core)
+    low = (dp // 2) % 2
+    above = (dp + 2 - 4 * low, chan) if n_dp > 2 else None
 
     class Share:
-        def __init__(self, w, g, half):
-            self.w, self.g, self.half = w, g, half
+        def __init__(self, w, g, parts, later=None):
+            self.w, self.g, self.parts = w, g, parts if n_dp > 2 else min(parts, 2)
             self.from_sibling = links.group()
-            rows = (part, 32) if half else (0, SL)
-            self.over = links.group([
-                (w.at[:, aligned(*rows), :], g.at[:, aligned(SL * chan + rows[0], rows[1]), :], across)])
+            self.size = SL // self.parts
+            self.part = {1: 0, 2: 32 * bit, 4: 32 * low + 16 * bit}[self.parts]
+            self.over = links.group()
+            start = self.over.plan(
+                w.at[:, aligned(self.part, self.size), :], g.at[:, aligned(SL * chan + self.part, self.size), :], across)
+            if later is None:
+                start()
+            else:
+                later.append(start)
 
         def own(self):
             self.from_sibling.remote(self.w, self.g.at[:, mine, :], sibling)
 
+        def piece(self, start, size):
+            return self.g.at[:, aligned(far + start, size), :]
+
+        def to_sibling(self, start, size):
+            piece = self.piece(start, size)
+            self.from_sibling.remote(piece, piece, sibling)
+
         def relay(self):
             self.over.wait()
-            if self.half:
-                piece = self.g.at[:, aligned(far + part, 32), :]
+            piece = self.piece(self.part, self.size)
+            if self.parts > 1:
                 self.around = links.group([(piece, piece, beside)])
-            else:
-                piece = self.g.at[:, aligned(far, SL), :]
-            self.from_sibling.remote(piece, piece, sibling)
+            if self.parts < 4:
+                self.to_sibling(self.part, self.size)
+
+        def relay_up(self):
+            if self.parts == 4:
+                self.around.wait()
+                piece = self.piece(32 * low, 32)
+                self.around = links.group([(piece, piece, above)])
+                self.to_sibling(32 * low, 32)
 
         def relay_again(self):
             self.around.wait()
-            piece = self.g.at[:, aligned(far + 32 - part, 32), :]
-            self.from_sibling.remote(piece, piece, sibling)
+            self.to_sibling(32 - 32 * (low if self.parts == 4 else bit), 32)
 
         def landed(self):
             self.from_sibling.wait()
@@ -531,8 +557,12 @@
     def rows3(ref, row):
         return ref.at[3 * row : 3 * row + 3]
 
-    one = [Share(rows3(r.w1, row), rows3(r.w1g, row), True) for row in range(3)]
+    one = [Share(rows3(r.w1, row), rows3(r.w1g, row), 2 if row == 2 else 4) for row in range(3)]
     for share in one:
+        share.own()
+    later = []
+    two = [Share(rows3(r.w2, row), rows3(r.w2g, row), 4, later) for row in range(2)]
+    for share in two:
         share.own()
 
     load_ts.wait()
@@ -558,9 +588,16 @@
     r.el[...] = jnp.zeros((8, 128), F32)
     r.el[:, 0:SL] = dot_nt(tsil, r.wel[0])[0:8]
     r.eg[chan] = r.el[...]
-    moves_x = links.group(
-        [(r.xp.at[d[1]], r.xg.at[chan], d) for d in quads] + [(r.par, r.pg.at[chan], d) for d in quads])
-    moves_emb = links.group([(r.el, r.eg.at[chan], d) for d in quads])
+    moves_x, moves_emb = links.group(), links.group()
+    later += [moves_x.plan(r.xp.at[d[1]], r.xg.at[chan], d) for d in quads]
+    later += [moves_x.plan(r.par, r.pg.at[chan], d) for d in quads]
+    later += [moves_emb.plan(r.el, r.eg.at[chan], d) for d in quads]
+
+    def start_later():
+        for start in later:
+            start()
+
+    pl.when(core == 0)(start_later)
     r.xg[chan] = r.xp[chan]
     r.pg[chan] = r.par[...]
     at_row = lax.broadcasted_iota(jnp.int32, (C, C), 0) // (C // GROUPS)
@@ -572,24 +609,30 @@
     load_dy.wait()
     pack(r.dyl, r.dyp)
     r.dyg[chan] = r.dyp[chan]
-    two = []
-    for row in range(3):
-        one[row].relay()
-        two.append(Share(rows3(r.w2, row), rows3(r.w2g, row), row < 2))
-        two[row].own()
-    one[0].relay_again()
-    out = [Share(r.wq, r.wqg.at[0:3], False), Share(r.wo, r.wqg.at[3:4], False)]
+    for share in one:
+        share.relay()
+    pl.when(core == 1)(start_later)
+    two.append(Share(rows3(r.w2, 2), rows3(r.w2g, 2), 1))
+    two[2].own()
+    one[0].relay_up()
+    two[0].relay()
+    one[1].relay_up()
+    out = [Share(r.wq, r.wqg.at[0:3], 1), Share(r.wo, r.wqg.at[3:4], 1)]
     for share in out:
         share.own()
-    one[1].relay_again()
+    two[1].relay()
+    one[2].relay_again()
+    two[0].relay_up()
     moves_dy = links.group([(r.dyp.at[d[1]], r.dyg.at[chan], d) for d in quads])
-    one[2].relay_again()
-    mix = Share(r.we, r.weg, False)
+    mix = Share(r.we, r.weg, 1)
     mix.own()
     moves_late = links.group([(r.tl, r.ta.at[dp], d) for d in others()])
+    one[0].relay_again()
+    two[1].relay_up()
 
     bd = r.bd[...]
     moves_x.wait()
+    one[1].relay_again()
     for b in range(2):
         first, _ = unpack(r.pg[2 * b], r.pg[2 * b + 1])
         r.pa[:, 128 * b : 128 * b + 128] = first
@@ -603,12 +646,6 @@
                 value = pair[m] if scale is None else pair[m] * scale[m]
                 dst[pl.ds(pl.multiple_of(at + m * ROWS, CH), CH), 128 * b : 128 * b + 128] = value.astype(dst.dtype)
 
-    def open_x(i, held):
-        spread_out(r.xg, chunk_at(i), r.xf)
-        return held
-
-    lax.fori_loop(0, ROWS // CH, open_x, 0)
-
     def rows_of(m, at):
         return pl.ds(pl.multiple_of(at + m * ROWS, CH), CH)
 
@@ -620,29 +657,30 @@
             write_shift(dst, m, at, u * sigmoid(u), True)
         return emit
 
-    rstd1 = norm_forward(lambda m, at: r.xf[rows_of(m, at), :], r.n1, gain1, shift1, bd, to_shift(r.a1),
-                         early=two[0].relay, midway=two[1].relay)
+    def open_x(m, at):
+        if m == 0:
+            spread_out(r.xg, at, r.xf)
+        return r.xf[rows_of(m, at), :]
+
+    rstd1 = norm_forward(lambda m, at: r.xf[rows_of(m, at), :], r.n1, gain1, shift1, bd, to_shift(r.a1), first=open_x)
     fill.wait()
 
     for share in one:
         share.landed()
-    conv_forward(r.a1, r.w1g, r.h, (0, 1, 2), False)
+    conv_forward(r.a1, r.w1g, r.h, (0, 1, 2))
+    two[0].relay_again()
     moves_emb.wait()
     for b in range(2):
         first, _ = unpack(r.eg[2 * b], r.eg[2 * b + 1])
         r.emb[:, 128 * b : 128 * b + 128] = first
     emb = [r.emb[pl.ds(2 * chan + m, 1), :] for m in range(2)]
     rstd2 = norm_forward(lambda m, at: r.h[rows_gap(m, at), :] + emb[m], r.n2, gain2, shift2, bd, to_shift(r.a2),
-                         midway=two[2].relay)
-    two[0].relay_again()
-    two[1].relay_again()
-    two[0].landed()
-    two[2].landed()
-    conv_forward(r.a2, r.w2g, r.h, (0, 2), False)
-    for share in out:
-        share.relay()
-    two[1].landed()
-    conv_forward(r.a2, r.w2g, r.h, (1,), True)
+                         early=two[2].relay, midway=two[1].relay_again)
+    out[0].relay()
+    for share in two:
+        share.landed()
+    conv_forward(r.a2, r.w2g, r.h, (0, 1, 2))
+    out[1].relay()
 
     def load_resid(m, at):
         return r.xf[rows_of(m, at), :]

time: 65.8 us -> 64 us (0.973)
  Pallas kernels: 64.3 us -> 62.5 us
    pallas_call x1, Pallas kernels: 60.4 us -> 58.7 us  [per_device(): pl.pallas_call(functools.partial(mega, n_dp, list(inputs) + list(middle)...]
where the time goes in v6:
time: 64 us; the launch traced here: 63.8 us
  Pallas kernels  62.5 us (98%)
  between operations  1.3 us (2%)
    pallas_call x1, Pallas kernels, per_device(): pl.pallas_call(functools.partial(mega, n_dp, list(inputs) + list(middle)...  58.7 us
    pallas_call x1, Pallas kernels, per_device(): pl.pallas_call(functools.partial(finish, n_dp, list(middle) + list(result...  3.85 us

profile of v6, /device:TPU:0, one launch (start us, length us, event | category | flops | bytes accessed | tf_op | source)
XLA Modules:
  0.0 63.8 jit_solution(12504022201956371008)
XLA Ops:
  1.3 58.7 %blocks.1 = (bf16[4,256,128]{2,1,0:T(8,128)(2,1)}, bf16[4,256,128]{2,1,0:T(8,128)(2,1)}, f32[8,8,128]{2,1,0:T(8,128)}, f32[8,8,128]{2,1,0:T(8,128)}, bf16[128,51...) custom-call(bf16[8,256,64]{2,1,0:T(8,128)(2,1)} %bitcast.40, ...), custom_call_target="tpu_custom_call" | custom-call | tf_op jit(solution)/shard_map/blocks/pallas_call | solution.py:1000
  60.0 3.8 %finish.1 = (bf16[8,256,64]{2,1,0:T(8,128)(2,1)}, bf16[8,256,64]{2,1,0:T(8,128)(2,1)}, f32[1000,512]{1,0:T(8,128)}, f32[9,64,256]{2,1,0:T(8,128)}, f32[9,64,256]...) custom-call(bf16[4,256,128]{2,1,0:T(8,128)(2,1)} %get-tuple-element., ...), custom_call_target="tpu_custom_call" | custom-call | tf_op jit(solution)/shard_map/finish/pallas_call | solution.py:1016

commit v7 on v6

--- a/solution.py
+++ b/solution.py
@@ -878,19 +878,28 @@
     links.close()
 
 
+STORES = ["y", "dm", "de_out", "dq", "do", "d2", "d1", "dt"]
+
+
 def finish(n_dp, names, *refs):
     r = SimpleNamespace(**dict(zip(names, refs)))
     maps = 8 * n_dp
     steps = r.dt.shape[0]
     links = Links(None, None, r.own, None)
-    items = list(ITEMS)
     load = {name: links.here(getattr(r, name), getattr(r, name + "_v"))
-            for name in ["tall", "both", "yo", "mo", "de"] + items + ["ext"]}
-    stores = []
-
-    def out(src, dst):
-        stores.append(links.here(src, dst))
-
+            for name in ["yo", "mo", "tall", "both"] + list(ITEMS) + ["de", "ext"]}
+
+    def out(name, src, index=slice(None)):
+        dst = getattr(r, name)
+        pltpu.make_async_copy(src.at[index], dst.at[index], r.stores.at[STORES.index(name)]).start()
+
+    for name, dst, src, dst_v in (("yo", "y", r.yo_v, r.y_v), ("mo", "dm", r.mo_v, r.dm_v)):
+        load[name].wait()
+        for j in range(CHAN):
+            block = src[j].astype(F32)
+            dst_v[2 * j] = block[:, 0:SL].astype(BF)
+            dst_v[2 * j + 1] = pltpu.roll(block, SL, 1)[:, 0:SL].astype(BF)
+        out(dst, dst_v)
     load["tall"].wait()
     load["both"].wait()
     lanes = r.tall_v[...].reshape(maps, 128).T[0:1, :]
@@ -900,16 +909,7 @@
         ids = lax.broadcasted_iota(jnp.int32, (size, 2 * maps), 0).astype(F32) + float(start)
         hot = jnp.where(ids == lanes, 1.0, 0.0).astype(BF)
         r.dt_v[start : start + size, :] = dot(hot, r.both_v[...])
-        out(r.dt_v.at[start : start + size], r.dt.at[start : start + size])
-
-    def unpack_maps(name, dst, dst_v):
-        load[name].wait()
-        src = getattr(r, name + "_v")
-        for j in range(CHAN):
-            block = src[j].astype(F32)
-            dst_v[2 * j] = block[:, 0:SL].astype(BF)
-            dst_v[2 * j + 1] = pltpu.roll(block, SL, 1)[:, 0:SL].astype(BF)
-        out(dst_v, dst)
+        out("dt", r.dt_v, slice(start, start + size))
 
     def whole(name, dst_v, base, taps):
         src = getattr(r, name + "_v")
@@ -917,32 +917,33 @@
             for half in range(2):
                 dst_v[base + i, :, 128 * half : 128 * half + 128] = src[0, half, SL * t : SL * t + SL, :].astype(F32)
 
-    unpack_maps("yo", r.y, r.y_v)
-    unpack_maps("mo", r.dm, r.dm_v)
+    done = dict(b=0, c=0)
+    for name, (taps, _, _) in ITEMS.items():
+        load[name].wait()
+        if name[1] == "a":
+            whole(name, r.dq_v, 0, range(3))
+            out("dq", r.dq_v)
+            whole(name, r.do_v, 0, [3])
+            out("do", r.do_v)
+        else:
+            key, start = dict(b="d2", c="d1")[name[1]], done[name[1]]
+            dst_v = getattr(r, key + "_v")
+            whole(name, dst_v, start, range(taps))
+            out(key, dst_v, slice(start, start + taps))
+            done[name[1]] += taps
     load["de"].wait()
-    out(r.de_v, r.de_out)
-    load["ga0"].wait()
-    whole("ga0", r.dq_v, 0, range(3))
-    out(r.dq_v, r.dq)
-    whole("ga0", r.do_v, 0, [3])
-    out(r.do_v, r.do)
-    for letter, dst_v, dst in (("b", r.d2_v, r.d2), ("c", r.d1_v, r.d1)):
-        start = 0
-        for name, (taps, _, _) in ITEMS.items():
-            if name[1] == letter:
-                load[name].wait()
-                whole(name, dst_v, start, range(taps))
-                out(dst_v.at[start : start + taps], dst.at[start : start + taps])
-                start += taps
+    out("de_out", r.de_v)
     load["ext"].wait()
     total = r.ext_v[0]
     for i in range(1, n_dp):
         total = total + r.ext_v[i]
     for i in range(6):
         r.gains_v[i] = total[i : i + 1, 0:SL]
-        out(r.gains_v.at[i], getattr(r, f"e{i}"))
-    for copy in stores:
-        copy.wait()
+        pltpu.make_async_copy(r.gains_v.at[i], getattr(r, f"e{i}"), r.stores.at[len(STORES)]).start()
+    for at, name in enumerate(STORES):
+        src = r.de_v if name == "de_out" else getattr(r, name + "_v")
+        pltpu.make_async_copy(src, getattr(r, name), r.stores.at[at]).wait()
+    pltpu.make_async_copy(r.gains_v, r.gains_v, r.stores.at[len(STORES)]).wait()
 
 
 def per_device(x_maps, timesteps, counts, emb_table, w_first, w_second, w_embed, w_qkv, w_out, gain_one, shift_one,
@@ -1012,7 +1013,9 @@
     results.update({f"e{i}": of((1, SL), F32) for i in range(6)})
     scratch = {name + "_v": v(o.shape, o.dtype) for name, o in middle.items()}
     scratch.update({name + "_v": v(o.shape, o.dtype) for name, o in results.items() if name[0] != "e"})
-    scratch.update(gains_v=v((6, 1, SL), F32), own=pltpu.SemaphoreType.DMA((48,)))
+    scratch.update(
+        gains_v=v((6, 1, SL), F32), own=pltpu.SemaphoreType.DMA((len(middle),)),
+        stores=pltpu.SemaphoreType.DMA((len(STORES) + 1,)))
     got = pl.pallas_call(
         functools.partial(finish, n_dp, list(middle) + list(results) + list(scratch)),
         out_shape=tuple(results.values()),

time: 64 us -> 63.7 us (level)
  no operation moved by 1% of the time
where the time goes in v7:
time: 63.7 us; the launch traced here: 63.6 us
  Pallas kernels  62.2 us (98%)
  between operations  1.3 us (2%)
    pallas_call x1, Pallas kernels, per_device(): pl.pallas_call(functools.partial(mega, n_dp, list(inputs) + list(middle)...  58.7 us
    pallas_call x1, Pallas kernels, per_device(): pl.pallas_call(functools.partial(finish, n_dp, list(middle) + list(result...  3.57 us

profile of v7, /device:TPU:0, one launch (start us, length us, event | category | flops | bytes accessed | tf_op | source)
XLA Modules:
  0.0 63.6 jit_solution(11329774987340014247)
XLA Ops:
  1.3 58.7 %blocks.1 = (bf16[4,256,128]{2,1,0:T(8,128)(2,1)}, bf16[4,256,128]{2,1,0:T(8,128)(2,1)}, f32[8,8,128]{2,1,0:T(8,128)}, f32[8,8,128]{2,1,0:T(8,128)}, bf16[128,51...) custom-call(bf16[8,256,64]{2,1,0:T(8,128)(2,1)} %bitcast.40, ...), custom_call_target="tpu_custom_call" | custom-call | tf_op jit(solution)/shard_map/blocks/pallas_call | solution.py:1001
  60.0 3.6 %finish.1 = (bf16[8,256,64]{2,1,0:T(8,128)(2,1)}, bf16[8,256,64]{2,1,0:T(8,128)(2,1)}, f32[1000,512]{1,0:T(8,128)}, f32[9,64,256]{2,1,0:T(8,128)}, f32[9,64,256]...) custom-call(bf16[4,256,128]{2,1,0:T(8,128)(2,1)} %get-tuple-element., ...), custom_call_target="tpu_custom_call" | custom-call | tf_op jit(solution)/shard_map/finish/pallas_call | solution.py:1019

commit v8 on v7

--- a/solution.py
+++ b/solution.py
@@ -279,7 +279,7 @@
 def reduction_scratch(taps, order, kind, teams):
     rows = SL * taps
     part = (1, 1, rows, 128)
-    shapes = dict(rc=(2, taps, SL, C), s0=(2, 2, rows, 128), pc=part, rt=(teams,) + part)
+    shapes = dict(rc=(2, taps, SL, C), s0=(2, 2, rows, 128), pc=part, sum=part, rt=(teams,) + part)
     shapes.update({name: part for name in ("c0", "c1", "c2", "p0", "p1", "t0", "t1")})
     size = dict(y=2, x=2)
     for k, axis in enumerate(order):
@@ -337,8 +337,8 @@
         total = w.rt[0].astype(F32)
         for s in range(1, at.teams):
             total = total + w.rt[s].astype(F32)
-        w.pc[...] = total.astype(BF)
-        return w.pc
+        w.sum[...] = total.astype(BF)
+        return w.sum
 
     def share(self, source):
         source = self.across_teams(source) if self.at.teams > 1 else source

time: 63.7 us -> 63.7 us (level)
  no operation moved by 1% of the time
where the time goes in v8:
time: 63.7 us; the launch traced here: 63.6 us
  Pallas kernels  62.2 us (98%)
  between operations  1.3 us (2%)
    pallas_call x1, Pallas kernels, per_device(): pl.pallas_call(functools.partial(mega, n_dp, list(inputs) + list(middle)...  58.7 us
    pallas_call x1, Pallas kernels, per_device(): pl.pallas_call(functools.partial(finish, n_dp, list(middle) + list(result...  3.57 us

profile of v8, /device:TPU:0, one launch (start us, length us, event | category | flops | bytes accessed | tf_op | source)
XLA Modules:
  0.0 63.6 jit_solution(11329774987340014247)
XLA Ops:
  1.3 58.7 %blocks.1 = (bf16[4,256,128]{2,1,0:T(8,128)(2,1)}, bf16[4,256,128]{2,1,0:T(8,128)(2,1)}, f32[8,8,128]{2,1,0:T(8,128)}, f32[8,8,128]{2,1,0:T(8,128)}, bf16[128,51...) custom-call(bf16[8,256,64]{2,1,0:T(8,128)(2,1)} %bitcast.40, ...), custom_call_target="tpu_custom_call" | custom-call | tf_op jit(solution)/shard_map/blocks/pallas_call | solution.py:1001
  60.0 3.6 %finish.1 = (bf16[8,256,64]{2,1,0:T(8,128)(2,1)}, bf16[8,256,64]{2,1,0:T(8,128)(2,1)}, f32[1000,512]{1,0:T(8,128)}, f32[9,64,256]{2,1,0:T(8,128)}, f32[9,64,256]...) custom-call(bf16[4,256,128]{2,1,0:T(8,128)(2,1)} %get-tuple-element., ...), custom_call_target="tpu_custom_call" | custom-call | tf_op jit(solution)/shard_map/finish/pallas_call | solution.py:1019

commit v9 on v8

--- a/solution.py
+++ b/solution.py
@@ -20,7 +20,7 @@
 GAP = 16
 STEP = ROWS + GAP
 TALL = 2 * ROWS + GAP
-CH = 128
+CH = 256
 COUNT = ROWS * (C // GROUPS)
 
 
@@ -762,13 +762,13 @@
         return held
 
     passes(norm_back(r.h, r.n3, gain3, shift3, rstd3, bd, False, r.e, 4, to_dres))
-    go(0)
 
     def turn():
         for m in range(2):
             r.turn[m] = r.dd[GAP + STEP * m : GAP + STEP * m + ROWS, C : 2 * C].T
 
     turn()
+    go(0)
     for row in range(3):
         conv_weight(r.a2, r.turn, r.dw2, row)
     reduce("b", r.dw2)

time: 63.7 us -> 63.7 us (level)
  no operation moved by 1% of the time
where the time goes in v9:
time: 63.7 us; the launch traced here: 63.6 us
  Pallas kernels  62.3 us (98%)
  between operations  1.3 us (2%)
    pallas_call x1, Pallas kernels, per_device(): pl.pallas_call(functools.partial(mega, n_dp, list(inputs) + list(middle)...  58.7 us
    pallas_call x1, Pallas kernels, per_device(): pl.pallas_call(functools.partial(finish, n_dp, list(middle) + list(result...  3.58 us

profile of v9, /device:TPU:0, one launch (start us, length us, event | category | flops | bytes accessed | tf_op | source)
XLA Modules:
  0.0 63.6 jit_solution(14355502438758629648)
XLA Ops:
  1.3 58.7 %blocks.1 = (bf16[4,256,128]{2,1,0:T(8,128)(2,1)}, bf16[4,256,128]{2,1,0:T(8,128)(2,1)}, f32[8,8,128]{2,1,0:T(8,128)}, f32[8,8,128]{2,1,0:T(8,128)}, bf16[128,51...) custom-call(bf16[8,256,64]{2,1,0:T(8,128)(2,1)} %bitcast.40, ...), custom_call_target="tpu_custom_call" | custom-call | tf_op jit(solution)/shard_map/blocks/pallas_call | solution.py:1001
  60.0 3.6 %finish.1 = (bf16[8,256,64]{2,1,0:T(8,128)(2,1)}, bf16[8,256,64]{2,1,0:T(8,128)(2,1)}, f32[1000,512]{1,0:T(8,128)}, f32[9,64,256]{2,1,0:T(8,128)}, f32[9,64,256]...) custom-call(bf16[4,256,128]{2,1,0:T(8,128)(2,1)} %get-tuple-element., ...), custom_call_target="tpu_custom_call" | custom-call | tf_op jit(solution)/shard_map/finish/pallas_call | solution.py:1019
